TPU v7x, 128 devices: a whole 4x4x4 slice. The times are simulated.
128 devices in a mesh: row: 8 (over y, core), col: 16 (over z, x).
Axes of the slice: x: 4, y: 4, z: 4, core: 2. Of those that a mesh axis runs over, the one named last changes fastest.
Arguments:
- precip: float32 [2048, 8192], P('row', 'col'), may hold values from 0.002 to 0.02
- head: float32 [2048, 8192], P('row', 'col'), may hold values from -4 to 4
- trans_coef: float32 [2048, 8192], P('row', 'col'), may hold values from 0.05 to 0.5
- land: int32 [2048, 8192], P('row', 'col'), may hold values 0 or 1
- dest: int32 [2048, 64], P('row', 'col'), may hold values from 0 to 131071, as said below
- moisture: float32 [131072, 16, 128], P(('row', 'col')), may hold values from 0.08 to 0.42
- ksat: float32 [131072, 128], P(('row', 'col')), may hold values from 0.002 to 0.01
Outputs:
- saturation: float32 [131072, 16, 128], P(('row', 'col'))
- head_new: float32 [2048, 8192], P('row', 'col')
Inputs may be any that keep to these rules, and one draw needn't show every extreme that they name: dest is a permutation of 0 .. 131071; its value is an owner's index along row+col times 1024 plus a slot. At most 16 blocks of one device's tile go to one owner, and every device sends exactly 16 to some owner; every owner receives 1024 blocks.
All inputs are finite; a program needn't handle non-finite values. No bound on the sum of `land` on one device may be relied on, other than what follows from the above.
Results may differ from a plain program's by a relative error of at most 0.00002.
Values sent between devices are 32-bit elements; how exact they have to be, the bound alone decides.
No kernel may reach another device: no remote copies, remote signals or barrier semaphores. Data moves between devices by JAX's collectives and lax.ppermute only.
A program may use at most 192 MiB of HBM per device.

v0:
```python
import math

import jax
import jax.numpy as jnp
from jax import lax
from jax.experimental import pallas as pl
from jax.experimental.pallas import tpu as pltpu
from jax.sharding import PartitionSpec as P

SWEEPS = 4
LANES = 128
EDGE = 8

layer_depth = 0.1
step_ratio = 0.1
residual_water = 0.05
pore_range = 0.4
couple_rate = 0.05
recharge_gain = 20.0
store_rate = 0.2

F32 = jnp.float32
BF16 = jnp.bfloat16
MIB = 1 << 20


def iota(shape, dim):
    return lax.broadcasted_iota(jnp.int32, shape, dim)


def params(mib):
    return pltpu.CompilerParams(vmem_limit_bytes=mib * MIB)


def cost(us):
    return pl.CostEstimate(flops=0, bytes_accessed=int(us * 3.0e6), transcendentals=0)


def halves(x):
    high = x.astype(BF16)
    low = (x - high.astype(F32)).astype(BF16)
    return high, low


def whole(count):
    return [pl.BlockSpec(memory_space=pltpu.VMEM)] * count


def pack_kernel(peers, cap, owned, dest_ref, precip_ref, head_ref, land_ref, out_ref, place_ref, hot_ref, data_ref):
    rows, cols = precip_ref.shape
    parts = cols // LANES
    blocks = rows * parts
    stride = 2 * cap + 1
    dest = dest_ref[...]
    shift = owned.bit_length() - 1
    owner = dest >> shift
    label = (dest & (owned - 1)) + 1
    owner_hot = owner == iota((peers, blocks), 0)
    before = (iota((LANES, LANES), 0) < iota((LANES, LANES), 1)).astype(F32).astype(BF16)
    carry = jnp.zeros((peers, 1), F32)
    ranks = []
    for chunk in range(blocks // LANES):
        hot = owner_hot[:, chunk * LANES : (chunk + 1) * LANES]
        hot_f = hot.astype(F32)
        count = jnp.dot(hot_f.astype(BF16), before, preferred_element_type=F32) + carry
        ranks.append(jnp.sum(count * hot_f, axis=0, keepdims=True))
        carry = carry + jnp.sum(hot_f, axis=1, keepdims=True)
    rank = jnp.concatenate(ranks, axis=1).astype(jnp.int32)
    place = owner + peers * rank
    place_f = place.astype(F32)
    eye = iota((LANES, LANES), 0) == iota((LANES, LANES), 1)
    for chunk in range(blocks // LANES):
        line = place_f[:, chunk * LANES : (chunk + 1) * LANES]
        place_ref[chunk * LANES : (chunk + 1) * LANES, :] = jnp.sum(
            jnp.where(eye, line, 0.0), axis=1, keepdims=True
        ).astype(jnp.int32)
    for part in range(parts):
        lane = slice(part * LANES, (part + 1) * LANES)
        line = slice(part * rows, (part + 1) * rows)
        infil = precip_ref[:, lane] * land_ref[:, lane].astype(F32)
        for at, piece in enumerate(halves(infil) + halves(head_ref[:, lane])):
            data_ref[line, at * LANES : (at + 1) * LANES] = piece
    for rank_k in range(cap):
        hot_ref[rank_k * peers : (rank_k + 1) * peers, :] = (
            (place == iota((peers, blocks), 0) + rank_k * peers).astype(F32).astype(BF16)
        )
    group = 8
    for first in range(0, cap, group):
        moved = jnp.dot(
            hot_ref[first * peers : (first + group) * peers, :], data_ref[...], preferred_element_type=F32
        )
        for k in range(group):
            part = moved[k * peers : (k + 1) * peers]
            out_ref[pl.ds(first + k, peers, stride=stride), :] = part[:, :LANES] + part[:, LANES : 2 * LANES]
            out_ref[pl.ds(cap + first + k, peers, stride=stride), :] = (
                part[:, 2 * LANES : 3 * LANES] + part[:, 3 * LANES :]
            )
    owner_f = owner_hot.astype(F32)
    rank_hot = (rank == iota((LANES, blocks), 0)).astype(F32).astype(BF16)
    contract = (((1,), (1,)), ((), ()))
    tops = (owner_f * (label >> 5).astype(F32)).astype(BF16)
    lows = (owner_f * (label & 31).astype(F32)).astype(BF16)
    labels = 32.0 * lax.dot_general(tops, rank_hot, contract, preferred_element_type=F32)
    labels = labels + lax.dot_general(lows, rank_hot, contract, preferred_element_type=F32)
    out_ref[pl.ds(2 * cap, peers, stride=stride), :] = labels


def pack(dest_row, precip, head, land, peers, cap, owned):
    blocks = dest_row.shape[1]

    def kernel(*refs):
        pack_kernel(peers, cap, owned, *refs)

    return pl.pallas_call(
        kernel,
        out_shape=(
            jax.ShapeDtypeStruct((peers * (2 * cap + 1), LANES), F32),
            jax.ShapeDtypeStruct((blocks, 1), jnp.int32),
        ),
        in_specs=whole(4),
        out_specs=tuple(whole(2)),
        scratch_shapes=[pltpu.VMEM((peers * cap, blocks), BF16), pltpu.VMEM((blocks, 4 * LANES), BF16)],
        compiler_params=params(40),
        cost_estimate=cost(5),
        name="pack_forcing",
    )(dest_row, precip, head, land)


def layer_terms(moist, half_k, depth_factor):
    wet = moist * (1.0 / pore_range) - residual_water / pore_range
    wet2 = wet * wet
    a = half_k * depth_factor
    t = a * wet2
    return wet, 7.5 * t, t * wet, a + 5.0 * t


def inverse(x):
    y = pl.reciprocal(x, approx=True)
    return y * (2.0 - x * y)


def eliminate(layers, load, ksat, infil, response, keep):
    half_k = 0.5 * ksat
    moist = load(0)
    wet, hs, hc, d5 = layer_terms(moist, half_k, math.exp(-0.5 * layer_depth))
    flux_above = infil
    ratio = reduced = resp = hs_prev = g_prev = None
    for k in range(layers):
        last = k == layers - 1
        if not last:
            moist_n = load(k + 1)
            wet_n, hs_n, hc_n, d5_n = layer_terms(
                moist_n, half_k, math.exp(-(k + 1.5) * layer_depth)
            )
            g = d5 + d5_n
            flux = (hc + hc_n) - g * (moist_n - moist)
        if k == 0:
            diagonal = (g + step_ratio) + hs
        elif last:
            diagonal = (g_prev + (step_ratio + couple_rate)) + hs
        else:
            diagonal = (g_prev + step_ratio) + g
        if last:
            bottom = 2.0 * hc + couple_rate * (moist - residual_water)
            right = flux_above - bottom
        else:
            right = (0.0 - flux) if flux_above is None else (flux_above - flux)
        if k == 0:
            inv = inverse(diagonal)
            reduced = right * inv
            resp = inv
        else:
            neg_sub = hs_prev + g_prev
            inv = inverse(diagonal + neg_sub * ratio)
            reduced = (right + neg_sub * reduced) * inv
            if response:
                resp = neg_sub * resp * inv
        if last:
            return bottom, 2.0 * hs + couple_rate, reduced, resp, inv, wet
        ratio = (hs_n - g) * inv
        if keep is not None:
            keep(k, wet, ratio, reduced)
        hs_prev, g_prev = hs, g
        flux_above = flux
        moist, wet, hs, hc, d5 = moist_n, wet_n, hs_n, hc_n, d5_n


def response_kernel(layers, chunk, moist_ref, ksat_ref, alpha_ref, beta_ref, gamma_ref):
    def step(j, carry):
        base = j * (chunk * layers)
        line = pl.ds(j * chunk, chunk)
        load = lambda k: moist_ref[pl.ds(base + k, chunk, stride=layers), :]
        bottom, gain, reduced, resp, inv, _ = eliminate(layers, load, ksat_ref[line, :], None, True, None)
        alpha_ref[line, :] = bottom + gain * reduced
        beta_ref[line, :] = gain * resp
        gamma_ref[line, :] = (couple_rate * pore_range) * (gain * inv - 1.0)
        return carry

    lax.fori_loop(0, ksat_ref.shape[0] // chunk, step, 0)


def response(moist2, ksat, layers):
    owned = ksat.shape[0]
    size = 128

    def kernel(*refs):
        response_kernel(layers, 32, *refs)

    small = pl.BlockSpec((size, LANES), lambda i: (i, 0))
    return pl.pallas_call(
        kernel,
        grid=(owned // size,),
        out_shape=(jax.ShapeDtypeStruct((owned, LANES), F32),) * 3,
        in_specs=[pl.BlockSpec((size * layers, LANES), lambda i: (i, 0)), small],
        out_specs=(small,) * 3,
        compiler_params=params(24),
        cost_estimate=cost(11),
        name="column_response",
    )(moist2, ksat)


def saturation_kernel(layers, chunk, moist_ref, ksat_ref, infil_ref, share_ref, out_ref, wet_s, ratio_s, reduced_s):
    def step(j, carry):
        base = j * (chunk * layers)
        line = pl.ds(j * chunk, chunk)
        load = lambda k: moist_ref[pl.ds(base + k, chunk, stride=layers), :]

        def keep(k, wet, ratio, reduced):
            wet_s[k] = wet
            ratio_s[k] = ratio
            reduced_s[k] = reduced

        _, _, reduced, _, inv, wet = eliminate(layers, load, ksat_ref[line, :], infil_ref[line, :], False, keep)
        change = reduced + (couple_rate * pore_range) * share_ref[line, :] * inv
        out_ref[pl.ds(base + layers - 1, chunk, stride=layers), :] = wet + (1.0 / pore_range) * change
        for k in range(layers - 2, -1, -1):
            change = reduced_s[k] - ratio_s[k] * change
            out_ref[pl.ds(base + k, chunk, stride=layers), :] = wet_s[k] + (1.0 / pore_range) * change
        return carry

    lax.fori_loop(0, ksat_ref.shape[0] // chunk, step, 0)


def saturate(moist2, ksat, infil, share, layers):
    owned = ksat.shape[0]
    size, chunk = 128, 32

    def kernel(*refs):
        saturation_kernel(layers, chunk, *refs)

    small = pl.BlockSpec((size, LANES), lambda i: (i, 0))
    large = pl.BlockSpec((size * layers, LANES), lambda i: (i, 0))
    return pl.pallas_call(
        kernel,
        grid=(owned // size,),
        out_shape=jax.ShapeDtypeStruct((owned * layers, LANES), F32),
        in_specs=[large, small, small, small],
        out_specs=large,
        scratch_shapes=[pltpu.VMEM((layers - 1, chunk, LANES), F32)] * 3,
        compiler_params=params(24),
        cost_estimate=cost(13),
        name="column_saturation",
    )(moist2, ksat, infil, share)


def owner_kernel(peers, cap, got_ref, alpha_ref, beta_ref, gamma_ref, infil_ref, share_ref, ans_ref, data_ref, hot_ref, back_ref, rech_ref):
    owned = alpha_ref.shape[0]
    stride = 2 * cap + 1
    labels = got_ref[pl.ds(2 * cap, peers, stride=stride), :]
    turned = jnp.transpose(labels).astype(jnp.int32) - 1
    labels = labels.astype(jnp.int32) - 1
    for k in range(cap):
        line = slice(k * peers, (k + 1) * peers)
        pieces = halves(got_ref[pl.ds(k, peers, stride=stride), :])
        pieces = pieces + halves(got_ref[pl.ds(cap + k, peers, stride=stride), :])
        for at, piece in enumerate(pieces):
            data_ref[line, at * LANES : (at + 1) * LANES] = piece
        hot_ref[:, line] = (turned[k : k + 1, :] == iota((owned, peers), 0)).astype(F32).astype(BF16)
        back_ref[line, :] = (labels[:, k : k + 1] == iota((peers, owned), 1)).astype(F32).astype(BF16)
    group = 512
    for first in range(0, owned, group):
        line = slice(first, first + group)
        moved = jnp.dot(hot_ref[line, :], data_ref[...], preferred_element_type=F32)
        infil = moved[:, :LANES] + moved[:, LANES : 2 * LANES]
        head = moved[:, 2 * LANES : 3 * LANES] + moved[:, 3 * LANES :]
        share = jax.nn.sigmoid(head)
        infil_ref[line, :] = infil
        share_ref[line, :] = share
        rech = alpha_ref[line, :] + beta_ref[line, :] * infil + gamma_ref[line, :] * share
        high, low = halves(rech)
        rech_ref[line, :LANES] = high
        rech_ref[line, LANES:] = low
    many = 8
    for first in range(0, cap, many):
        moved = jnp.dot(
            back_ref[first * peers : (first + many) * peers, :], rech_ref[...], preferred_element_type=F32
        )
        for k in range(many):
            part = moved[k * peers : (k + 1) * peers]
            ans_ref[pl.ds(first + k, peers, stride=cap), :] = part[:, :LANES] + part[:, LANES:]


def owner_side(got, alpha, beta, gamma, peers, cap):
    owned = alpha.shape[0]

    def kernel(*refs):
        owner_kernel(peers, cap, *refs)

    return pl.pallas_call(
        kernel,
        out_shape=(
            jax.ShapeDtypeStruct((owned, LANES), F32),
            jax.ShapeDtypeStruct((owned, LANES), F32),
            jax.ShapeDtypeStruct((peers * cap, LANES), F32),
        ),
        in_specs=whole(4),
        out_specs=tuple(whole(3)),
        scratch_shapes=[
            pltpu.VMEM((peers * cap, 4 * LANES), BF16),
            pltpu.VMEM((owned, peers * cap), BF16),
            pltpu.VMEM((peers * cap, owned), BF16),
            pltpu.VMEM((owned, 2 * LANES), BF16),
        ],
        compiler_params=params(48),
        cost_estimate=cost(8),
        name="owner_side",
    )(got, alpha, beta, gamma)


def put_sides(x, left_ref, right_ref, at):
    cols = x.shape[1]
    left_ref[at : at + EDGE, :] = jnp.transpose(x[:, :LANES])[:EDGE, :]
    right_ref[at : at + EDGE, :] = jnp.transpose(x[:, cols - LANES :])[LANES - EDGE :, :]


def source_kernel(peers, cap, back_ref, place_ref, initial_ref, source_ref, left_ref, right_ref, data_ref, hot_ref):
    rows, cols = initial_ref.shape
    blocks = place_ref.shape[0]
    place = place_ref[...]
    for k in range(cap):
        line = slice(k * peers, (k + 1) * peers)
        high, low = halves(back_ref[pl.ds(k, peers, stride=cap), :])
        data_ref[line, :LANES] = high
        data_ref[line, LANES:] = low
        hot_ref[:, line] = (place == iota((blocks, peers), 1) + k * peers).astype(F32).astype(BF16)
    for part in range(cols // LANES):
        lane = slice(part * LANES, (part + 1) * LANES)
        moved = jnp.dot(hot_ref[part * rows : (part + 1) * rows, :], data_ref[...], preferred_element_type=F32)
        source_ref[:, lane] = store_rate * initial_ref[:, lane] + recharge_gain * (
            moved[:, :LANES] + moved[:, LANES:]
        )
    put_sides(source_ref[...], left_ref, right_ref, 0)


def source_of(back, place, initial, peers, cap):
    rows, cols = initial.shape
    blocks = place.shape[0]

    def kernel(*refs):
        source_kernel(peers, cap, *refs)

    side = jax.ShapeDtypeStruct((EDGE, rows), F32)
    return pl.pallas_call(
        kernel,
        out_shape=(jax.ShapeDtypeStruct((rows, cols), F32), side, side),
        in_specs=whole(3),
        out_specs=tuple(whole(3)),
        scratch_shapes=[pltpu.VMEM((peers * cap, 2 * LANES), BF16), pltpu.VMEM((blocks, peers * cap), BF16)],
        compiler_params=params(32),
        cost_estimate=cost(4),
        name="tile_source",
    )(back, place, initial)


def derive_kernel(head_ref, trans_ref, land_ref, initial_ref, left_ref, right_ref, up_ref, down_ref, transmit_ref):
    rows = head_ref.shape[0]
    head = head_ref[...]
    share = land_ref[...].astype(F32)
    initial = head * share
    transmit = trans_ref[...] * (1.0 + 0.5 * jnp.tanh(head))
    initial_ref[...] = initial
    transmit_ref[...] = transmit
    for at, x in enumerate((initial, transmit, share)):
        put_sides(x, left_ref, right_ref, at * EDGE)
        up_ref[at * EDGE : (at + 1) * EDGE, :] = x[:EDGE, :]
        down_ref[at * EDGE : (at + 1) * EDGE, :] = x[rows - EDGE :, :]


def derive(head, trans_coef, land):
    rows, cols = head.shape
    tile = jax.ShapeDtypeStruct((rows, cols), F32)
    side = jax.ShapeDtypeStruct((3 * EDGE, rows), F32)
    line = jax.ShapeDtypeStruct((3 * EDGE, cols), F32)
    return pl.pallas_call(
        derive_kernel,
        out_shape=(tile, side, side, line, line, tile),
        in_specs=whole(3),
        out_specs=tuple(whole(6)),
        compiler_params=params(24),
        cost_estimate=cost(3),
        name="derive_tile",
    )(head, trans_coef, land)


def exchange(up_line, down_line, left_side, right_side):
    rows = left_side.shape[1]

    def ring(axis, by):
        count = lax.axis_size(axis)
        return [(i, (i + by) % count) for i in range(count)]

    from_left = lax.ppermute(right_side, "col", ring("col", 1))
    from_right = lax.ppermute(left_side, "col", ring("col", -1))
    down_send = jnp.concatenate([down_line, from_left[:, rows - LANES :], from_right[:, rows - LANES :]], axis=1)
    up_send = jnp.concatenate([up_line, from_left[:, :LANES], from_right[:, :LANES]], axis=1)
    from_above = lax.ppermute(down_send, "row", ring("row", 1))
    from_below = lax.ppermute(up_send, "row", ring("row", -1))
    return from_left, from_right, from_above, from_below


def left_block(side):
    return jnp.transpose(jnp.concatenate([jnp.zeros((LANES - EDGE, LANES), F32), side], axis=0))


def right_block(side):
    return jnp.transpose(jnp.concatenate([side, jnp.zeros((LANES - EDGE, LANES), F32)], axis=0))


def assemble(out_ref, tile, sides, at):
    from_left, from_right, from_above, from_below = sides
    rows, cols = tile.shape
    part = slice(at * EDGE, (at + 1) * EDGE)
    bottom = slice(EDGE + rows, 2 * EDGE + rows)
    right = slice(LANES + cols, 2 * LANES + cols)
    mid = slice(LANES, LANES + cols)
    out_ref[EDGE : EDGE + rows, mid] = tile
    out_ref[:EDGE, mid] = from_above[part, :cols]
    out_ref[bottom, mid] = from_below[part, :cols]
    for first in range(0, rows, LANES):
        line = slice(EDGE + first, EDGE + first + LANES)
        out_ref[line, :LANES] = left_block(from_left[part, first : first + LANES])
        out_ref[line, right] = right_block(from_right[part, first : first + LANES])
    out_ref[:EDGE, :LANES] = left_block(from_above[part, cols : cols + LANES])[LANES - EDGE :, :]
    out_ref[:EDGE, right] = right_block(from_above[part, cols + LANES :])[LANES - EDGE :, :]
    out_ref[bottom, :LANES] = left_block(from_below[part, cols : cols + LANES])[:EDGE, :]
    out_ref[bottom, right] = right_block(from_below[part, cols + LANES :])[:EDGE, :]


def shifted(x, by, axis):
    return pltpu.roll(x, by % x.shape[axis], axis)


def weights_kernel(where_ref, initial_ref, transmit_ref, land_ref, left_ref, right_ref, above_ref, below_ref, *rest):
    center_ref, up_ref, down_ref, wleft_ref, wright_ref, first_ref, ext_ref = rest
    rows, cols = initial_ref.shape
    height, width = ext_ref.shape
    sides = (left_ref, right_ref, above_ref, below_ref)
    i = iota((height, width), 0)
    j = iota((height, width), 1)
    inside = (i >= where_ref[0]) & (i < where_ref[1]) & (j >= where_ref[2]) & (j < where_ref[3])

    def extended(tile, at):
        assemble(ext_ref, tile, sides, at)
        return jnp.where(inside, ext_ref[...], 0.0)

    transmit = extended(transmit_ref[...], 1)
    share = extended(land_ref[...].astype(F32), 2)
    up = 0.5 * (transmit + shifted(transmit, 1, 0))
    down = 0.5 * (transmit + shifted(transmit, -1, 0))
    left = 0.5 * (transmit + shifted(transmit, 1, 1))
    right = 0.5 * (transmit + shifted(transmit, -1, 1))
    scale = share / (store_rate + (up + down + left + right))
    center_ref[...] = scale
    up, down, left, right = up * scale, down * scale, left * scale, right * scale
    up_ref[...] = up
    down_ref[...] = down
    wleft_ref[...] = left
    wright_ref[...] = right
    initial = extended(initial_ref[...], 0)
    inflow = up * shifted(initial, 1, 0) + down * shifted(initial, -1, 0)
    first_ref[...] = inflow + left * shifted(initial, 1, 1) + right * shifted(initial, -1, 1)


def weights(where, initial, transmit, land, sides):
    rows, cols = initial.shape
    ext = (rows + 2 * EDGE, cols + 2 * LANES)
    return pl.pallas_call(
        weights_kernel,
        out_shape=(jax.ShapeDtypeStruct(ext, F32),) * 6,
        in_specs=[pl.BlockSpec(memory_space=pltpu.SMEM)] + whole(7),
        out_specs=tuple(whole(6)),
        scratch_shapes=[pltpu.VMEM(ext, F32)],
        compiler_params=params(32),
        cost_estimate=cost(6),
        name="flow_weights",
    )(where, initial, transmit, land, *sides)


def relax_kernel(source_ref, left_ref, right_ref, above_ref, below_ref, *rest):
    center_ref, up_ref, down_ref, wleft_ref, wright_ref, first_ref, out_ref, ext_ref = rest
    rows, cols = source_ref.shape
    assemble(ext_ref, source_ref[...], (left_ref, right_ref, above_ref, below_ref), 0)
    forced = center_ref[...] * ext_ref[...]
    surface = forced + first_ref[...]
    for _ in range(SWEEPS - 1):
        inflow = up_ref[...] * shifted(surface, 1, 0) + down_ref[...] * shifted(surface, -1, 0)
        inflow = inflow + wleft_ref[...] * shifted(surface, 1, 1) + wright_ref[...] * shifted(surface, -1, 1)
        surface = forced + inflow
    out_ref[...] = surface[EDGE : EDGE + rows, LANES : LANES + cols]


def relax(source, sides, weight):
    rows, cols = source.shape
    ext = weight[0].shape
    return pl.pallas_call(
        relax_kernel,
        out_shape=jax.ShapeDtypeStruct((rows, cols), F32),
        in_specs=whole(11),
        out_specs=pl.BlockSpec(memory_space=pltpu.VMEM),
        scratch_shapes=[pltpu.VMEM(ext, F32)],
        compiler_params=params(32),
        cost_estimate=cost(5),
        name="lateral_relax",
    )(source, *sides, *weight)


def on_device(precip, head, trans_coef, land, dest, moisture, ksat):
    rows, cols = precip.shape
    row_count = lax.axis_size("row")
    col_count = lax.axis_size("col")
    peers = row_count * col_count
    owned, layers, _ = moisture.shape
    blocks = rows * cols // LANES
    cap = 2 * blocks // peers
    axes = ("row", "col")
    moist2 = moisture.reshape(owned * layers, LANES)
    dest_row = jnp.transpose(dest).reshape(1, blocks)

    sent, place = pack(dest_row, precip, head, land, peers, cap, owned)
    wide = (2 * cap + 1) * LANES
    got = lax.all_to_all(sent.reshape(peers, 1, wide), axes, split_axis=0, concat_axis=0, tiled=True)
    got = got.reshape(peers * (2 * cap + 1), LANES)

    alpha, beta, gamma = response(moist2, ksat, layers)
    initial, left, right, up, down, transmit = derive(head, trans_coef, land)
    sides = exchange(up, down, left, right)
    row_at, col_at = lax.axis_index("row"), lax.axis_index("col")
    where = jnp.stack(
        [
            jnp.where(row_at == 0, EDGE, 0),
            jnp.where(row_at == row_count - 1, EDGE + rows, 2 * EDGE + rows),
            jnp.where(col_at == 0, LANES, 0),
            jnp.where(col_at == col_count - 1, LANES + cols, 2 * LANES + cols),
        ]
    ).astype(jnp.int32)
    weight = weights(where, initial, transmit, land, sides)

    infil, share, answer = owner_side(got, alpha, beta, gamma, peers, cap)
    back = lax.all_to_all(answer.reshape(peers, cap, LANES), axes, split_axis=0, concat_axis=0, tiled=True)
    back = back.reshape(peers * cap, LANES)
    saturation = saturate(moist2, ksat, infil, share, layers).reshape(owned, layers, LANES)

    source, left, right = source_of(back, place, initial, peers, cap)
    sides = exchange(source[:EDGE, :], source[rows - EDGE :, :], left, right)
    surface = relax(source, sides, weight)
    return (saturation, surface)


def solution(mesh):
    tile = P("row", "col")
    return jax.shard_map(
        on_device,
        mesh=mesh,
        in_specs=(tile,) * 5 + (P(("row", "col"), None, None), P(("row", "col"), None)),
        out_specs=(P(("row", "col"), None, None), tile),
        check_vma=False,
    )
```

profile of v0, /device:TPU:0, one launch (start us, length us, event | category | flops | bytes accessed | tf_op | source)
XLA Modules:
  0.0 124.5 jit_solution(2126868564127279015)
XLA Ops:
  1.3 1.0 copy-done.2
  2.4 1.0 copy-done.5
  3.4 1.0 copy-done.10
  4.4 2.8 %pack_forcing.1 = (f32[4224,128]{1,0:T(8,128)S(1)}, s32[1024,1]{1,0:T(8,128)S(1)}) custom-call(s32[1,1024]{1,0:T(1,128)S(1)} %bitcast.20, f32[256,512]{1,0:T(8,128)S(1)} %copy-done.10, f32[256,512]{1,0:T(8,128)S(1)} %copy-done.5, s32[256,512]{1,0:T(8,128)S(1)} %copy-done.2), custom_call_target="tpu_custom_call" | custom-call | bytes 15000000 | tf_op jit(solution)/shard_map/pack_forcing/pallas_call | solution.py:114
  7.3 1.3 %copy-done.4 = f32[4224,128]{1,0:T(8,128)} copy-done((f32[4224,128]{1,0:T(8,128)}, f32[4224,128]{1,0:T(8,128)S(1)}, u32[]{:S(2)}) %copy-start.4) | copy-done | bytes 2162712
  9.4 11.1 %all-to-all-start = ((f32[128,1,4224]{2,1,0:T(1,128)}), f32[128,1,4224]{2,1,0:T(1,128)S(1)}, u32[]{:S(2)}, u32[]{:S(2)}) async-start(f32[128,1,4224]{2,1,0:T(1,128)} %bitcast.18), calls=%async_computation | async-start | bytes 4325376 | tf_op jit(solution)/shard_map/all_to_all | solution.py:541
  20.6 3.4 %copy-done = f32[1024,16,128]{2,1,0:T(8,128)S(1)} copy-done((f32[1024,16,128]{2,1,0:T(8,128)S(1)}, f32[1024,16,128]{2,1,0:T(8,128)}, u32[]{:S(2)}) %copy-start) | copy-done | bytes 8388632
  24.0 1.0 copy-done.7
  25.0 13.2 %column_response.1 = (f32[1024,128]{1,0:T(8,128)S(1)}, f32[1024,128]{1,0:T(8,128)S(1)}, f32[1024,128]{1,0:T(8,128)S(1)}) custom-call(f32[16384,128]{1,0:T(8,128)S(1)} %bitcast.14, f32[1024,128]{1,0:T(8,128)S(1)} %copy-done.7), custom_call_target="tpu_custom_call" | custom-call | bytes 33000000 | tf_op jit(solution)/shard_map/column_response/pallas_call | solution.py:210
  40.6 10.3 %all-to-all-done = f32[128,1,4224]{2,1,0:T(1,128)S(1)} async-done(((f32[128,1,4224]{2,1,0:T(1,128)}), f32[128,1,4224]{2,1,0:T(1,128)S(1)}, u32[]{:S(2)}, u32[]{:S(2)}) %all-to-all-start) | async-done | bytes 2162720 | tf_op jit(solution)/shard_map/all_to_all | solution.py:541
  51.0 1.0 copy-done.17
  52.0 1.0 copy-done.19
  53.0 1.0 copy-done.21
  54.1 3.9 %owner_side.1 = (f32[1024,128]{1,0:T(8,128)S(1)}, f32[1024,128]{1,0:T(8,128)S(1)}, f32[2048,128]{1,0:T(8,128)S(1)}) custom-call(f32[4224,128]{1,0:T(8,128)S(1)} %bitcast.16, f32[1024,128]{1,0:T(8,128)S(1)} %copy-done.17, f32[1024,128]{1,0:T(8,128)S(1)} %copy-done.19, f32[1024,128]{1,0:T(8,128)S(1)} %copy-done.21), custom_call_target="tpu_custom_call" | custom-call | bytes 24000000 | tf_op jit(solution)/shard_map/owner_side/pallas_call | solution.py:309
  59.6 1.0 copy-done.9
  60.5 4.6 %all-to-all-start.1 = ((f32[128,16,128]{2,1,0:T(8,128)}), f32[128,16,128]{2,1,0:T(8,128)S(1)}, u32[]{:S(2)}, u32[]{:S(2)}) async-start(f32[128,16,128]{2,1,0:T(8,128)} %bitcast.19), calls=%async_computation.1 | async-start | bytes 2097152 | tf_op jit(solution)/shard_map/all_to_all | solution.py:559
  65.2 1.0 copy-done.11
  68.2 4.5 %collective-permute-start.5 = (f32[24,256]{1,0:T(8,128)S(1)}, f32[24,256]{1,0:T(8,128)S(1)}, u32[]{:S(2)}, u32[]{:S(2)}) collective-permute-start(f32[24,256]{1,0:T(8,128)S(1)} %get-tuple-element.39), channel_id=1, source_target_pairs={{0,15},{1,0},{2,1},{3,2},{4,3},{5,4},{6,5},{7,6},{8,7},{9,8},{10,9... | collective-permute-start | bytes 73736 | tf_op jit(solution)/shard_map/ppermute | solution.py:413
  72.7 9.3 %collective-permute-done.4.left_ref = f32[24,256]{1,0:T(8,128)S(1)} collective-permute-done((f32[24,256]{1,0:T(8,128)S(1)}, f32[24,256]{1,0:T(8,128)S(1)}, u32[]{:S(2)}, u32[]{:S(2)}) %collective-permute-start.4) | collective-permute-done | bytes 24608 | tf_op jit(solution)/shard_map/ppermute | solution.py:412
  82.1 2.9 %collective-permute-start.7 = (f32[24,768]{1,0:T(8,128)S(1)}, f32[24,768]{1,0:T(8,128)S(1)}, u32[]{:S(2)}, u32[]{:S(2)}) collective-permute-start(f32[24,768]{1,0:T(8,128)S(1)} %pad_maximum_fusion.1), channel_id=1, source_target_pairs={{0,112},{16,0},{32,16},{48,32},{64,48},{80,64},{96,80},{112,96},{1... | collective-permute-start | bytes 221192 | tf_op jit(solution)/shard_map/ppermute | solution.py:417
  85.1 1.0 copy-done.25
  86.1 2.1 %tile_source.1 = (f32[256,512]{1,0:T(8,128)S(1)}, f32[8,256]{1,0:T(8,128)S(1)}, f32[8,256]{1,0:T(8,128)S(1)}) custom-call(f32[2048,128]{1,0:T(8,128)S(1)} %bitcast.17, s32[1024,1]{1,0:T(8,128)S(1)} %copy-done.25, f32[256,512]{1,0:T(8,128)S(1)} %get-tuple-element.33.refs_2_.initial_ref), custom_call_target="tpu_custom_call" | custom-call | bytes 12000000 | tf_op jit(solution)/shard_map/tile_source/pallas_call | solution.py:363
  88.3 5.3 %collective-permute-start.1 = (f32[8,256]{1,0:T(8,128)S(1)}, f32[8,256]{1,0:T(8,128)S(1)}, u32[]{:S(2)}, u32[]{:S(2)}) collective-permute-start(f32[8,256]{1,0:T(8,128)S(1)} %get-tuple-element.36), channel_id=1, source_target_pairs={{0,15},{1,0},{2,1},{3,2},{4,3},{5,4},{6,5},{7,6},{8,7},{9,8},{10,9... | collective-permute-start | bytes 24584 | tf_op jit(solution)/shard_map/ppermute | solution.py:413
  93.7 1.6 %collective-permute-done.left_ref = f32[8,256]{1,0:T(8,128)S(1)} collective-permute-done((f32[8,256]{1,0:T(8,128)S(1)}, f32[8,256]{1,0:T(8,128)S(1)}, u32[]{:S(2)}, u32[]{:S(2)}) %collective-permute-start) | collective-permute-done | bytes 8224 | tf_op jit(solution)/shard_map/ppermute | solution.py:412
  95.4 2.9 %collective-permute-start.3 = (f32[8,768]{1,0:T(8,128)S(1)}, f32[8,768]{1,0:T(8,128)S(1)}, u32[]{:S(2)}, u32[]{:S(2)}) collective-permute-start(f32[8,768]{1,0:T(8,128)S(1)} %pad_maximum_fusion.3), channel_id=1, source_target_pairs={{0,112},{16,0},{32,16},{48,32},{64,48},{80,64},{96,80},{112,96},{1... | collective-permute-start | bytes 73736 | tf_op jit(solution)/shard_map/ppermute | solution.py:417
  98.4 1.0 copy-done.23
  99.4 2.6 %flow_weights.1 = (f32[272,768]{1,0:T(8,128)S(1)}, f32[272,768]{1,0:T(8,128)S(1)}, f32[272,768]{1,0:T(8,128)S(1)}, f32[272,768]{1,0:T(8,128)S(1)}, f32[272,768]{1,0:T(8,128)S(1)}, /*index=5*/f32[272,768]{1,0:T(8,128)S(1)}) custom-call(s32[4]{0:T(128)S(1)} %pad_add_fusion.where_ref, f32[256,512]{1,0:T(8,128)S(1)} %get-tuple-element.33.refs_2_.initial_ref, ...), custom_call_target="tpu_custom_call" | custom-call | bytes 18000000 | tf_op jit(solution)/shard_map/flow_weights/pallas_call | solution.py:487
  102.0 3.4 %copy-done.1 = f32[1024,16,128]{2,1,0:T(8,128)S(1)} copy-done((f32[1024,16,128]{2,1,0:T(8,128)S(1)}, f32[1024,16,128]{2,1,0:T(8,128)}, u32[]{:S(2)}) %copy-start.1) | copy-done | bytes 8388632
  105.4 1.0 copy-done.13
  106.4 1.0 copy-done.15
  107.5 14.3 %column_saturation.1 = f32[16384,128]{1,0:T(8,128)} custom-call(f32[16384,128]{1,0:T(8,128)S(1)} %bitcast.15, f32[1024,128]{1,0:T(8,128)S(1)} %copy-done.8, f32[1024,128]{1,0:T(8,128)S(1)} %copy-done.13, f32[1024,128]{1,0:T(8,128)S(1)} %copy-done.15), custom_call_target="tpu_custom_call" | custom-call | bytes 39000000 | tf_op jit(solution)/shard_map/column_saturation/pallas_call | solution.py:253
  121.8 2.7 %lateral_relax.1 = f32[256,512]{1,0:T(8,128)} custom-call(f32[256,512]{1,0:T(8,128)S(1)} %get-tuple-element.34.source_ref, f32[8,256]{1,0:T(8,128)S(1)} %collective-permute-done.left_ref, f32[8,256]{1,0:T(8,128)S(1)} %collective-permute-done.1.right_ref, f32[8,768]{1,0:T(8,128)S(1)} %collective-permute-done.2.above_ref, ...), custom_call_target="tpu_custom_call" | custom-call | bytes 15000000 | tf_op jit(solution)/shard_map/lateral_relax/pallas_call | solution.py:515
  (59 shorter events, 7.8 us)
Async XLA Ops:
  1.3 1.0 copy-start.2
  2.4 1.0 copy-start.5
  3.4 1.0 copy-start.10
  7.3 1.3 %copy-start.4 = (f32[4224,128]{1,0:T(8,128)}, f32[4224,128]{1,0:T(8,128)S(1)}, u32[]{:S(2)}) copy-start(f32[4224,128]{1,0:T(8,128)S(1)} %get-tuple-element.25) | copy-start | bytes 6488068
  8.6 0.8 copy-start.24
  9.4 41.5 %all-to-all-start = ((f32[128,1,4224]{2,1,0:T(1,128)}), f32[128,1,4224]{2,1,0:T(1,128)S(1)}, u32[]{:S(2)}, u32[]{:S(2)}) async-start(f32[128,1,4224]{2,1,0:T(1,128)} %bitcast.18), calls=%async_computation | async-start | bytes 4325376 | tf_op jit(solution)/shard_map/all_to_all | solution.py:541
  20.6 3.4 %copy-start = (f32[1024,16,128]{2,1,0:T(8,128)S(1)}, f32[1024,16,128]{2,1,0:T(8,128)}, u32[]{:S(2)}) copy-start(f32[1024,16,128]{2,1,0:T(8,128)} %param.12) | copy-start | bytes 25165828
  24.0 1.0 copy-start.7
  25.0 40.1 %copy-start.3 = (s32[256,512]{1,0:T(8,128)S(1)}, s32[256,512]{1,0:T(8,128)}, u32[]{:S(2)}) copy-start(s32[256,512]{1,0:T(8,128)} %land_ref.3) | copy-start | bytes 1572868
  25.0 40.1 %copy-start.6 = (f32[256,512]{1,0:T(8,128)S(1)}, f32[256,512]{1,0:T(8,128)}, u32[]{:S(2)}) copy-start(f32[256,512]{1,0:T(8,128)} %head_ref.1) | copy-start | bytes 1572868
  39.8 0.8 copy-start.20
  51.0 1.0 copy-start.17
  52.0 1.0 copy-start.19
  53.0 1.0 copy-start.21
  59.6 1.0 copy-start.9
  59.6 42.5 %copy-start.8 = (f32[1024,128]{1,0:T(8,128)S(1)}, f32[1024,128]{1,0:T(8,128)}, u32[]{:S(2)}) copy-start(f32[1024,128]{1,0:T(8,128)} %refs_1_.5) | copy-start | bytes 1572868
  60.5 24.6 %all-to-all-start.1 = ((f32[128,16,128]{2,1,0:T(8,128)}), f32[128,16,128]{2,1,0:T(8,128)S(1)}, u32[]{:S(2)}, u32[]{:S(2)}) async-start(f32[128,16,128]{2,1,0:T(8,128)} %bitcast.19), calls=%async_computation.1 | async-start | bytes 2097152 | tf_op jit(solution)/shard_map/all_to_all | solution.py:559
  65.2 1.0 copy-start.11
  66.5 0.8 copy-start.22
  67.4 14.7 %collective-permute-start.4 = (f32[24,256]{1,0:T(8,128)S(1)}, f32[24,256]{1,0:T(8,128)S(1)}, u32[]{:S(2)}, u32[]{:S(2)}) collective-permute-start(f32[24,256]{1,0:T(8,128)S(1)} %get-tuple-element.38), channel_id=1, source_target_pairs={{0,1},{1,2},{2,3},{3,4},{4,5},{5,6},{6,7},{7,8},{8,9},{9,10},{10,1... | collective-permute-start | bytes 73736 | tf_op jit(solution)/shard_map/ppermute | solution.py:412
  68.2 13.8 %collective-permute-start.5 = (f32[24,256]{1,0:T(8,128)S(1)}, f32[24,256]{1,0:T(8,128)S(1)}, u32[]{:S(2)}, u32[]{:S(2)}) collective-permute-start(f32[24,256]{1,0:T(8,128)S(1)} %get-tuple-element.39), channel_id=1, source_target_pairs={{0,15},{1,0},{2,1},{3,2},{4,3},{5,4},{6,5},{7,6},{8,7},{9,8},{10,9... | collective-permute-start | bytes 73736 | tf_op jit(solution)/shard_map/ppermute | solution.py:413
  82.1 16.3 %collective-permute-start.6 = (f32[24,768]{1,0:T(8,128)S(1)}, f32[24,768]{1,0:T(8,128)S(1)}, u32[]{:S(2)}, u32[]{:S(2)}) collective-permute-start(f32[24,768]{1,0:T(8,128)S(1)} %pad_maximum_fusion), channel_id=1, source_target_pairs={{0,16},{16,32},{32,48},{48,64},{64,80},{80,96},{96,112},{112,0},{1... | collective-permute-start | bytes 221192 | tf_op jit(solution)/shard_map/ppermute | solution.py:416
  82.1 16.2 %collective-permute-start.7 = (f32[24,768]{1,0:T(8,128)S(1)}, f32[24,768]{1,0:T(8,128)S(1)}, u32[]{:S(2)}, u32[]{:S(2)}) collective-permute-start(f32[24,768]{1,0:T(8,128)S(1)} %pad_maximum_fusion.1), channel_id=1, source_target_pairs={{0,112},{16,0},{32,16},{48,32},{64,48},{80,64},{96,80},{112,96},{1... | collective-permute-start | bytes 221192 | tf_op jit(solution)/shard_map/ppermute | solution.py:417
  85.1 1.0 copy-start.25
  88.3 7.0 %collective-permute-start = (f32[8,256]{1,0:T(8,128)S(1)}, f32[8,256]{1,0:T(8,128)S(1)}, u32[]{:S(2)}, u32[]{:S(2)}) collective-permute-start(f32[8,256]{1,0:T(8,128)S(1)} %get-tuple-element.35), channel_id=1, source_target_pairs={{0,1},{1,2},{2,3},{3,4},{4,5},{5,6},{6,7},{7,8},{8,9},{9,10},{10,1... | collective-permute-start | bytes 24584 | tf_op jit(solution)/shard_map/ppermute | solution.py:412
  88.3 7.0 %collective-permute-start.1 = (f32[8,256]{1,0:T(8,128)S(1)}, f32[8,256]{1,0:T(8,128)S(1)}, u32[]{:S(2)}, u32[]{:S(2)}) collective-permute-start(f32[8,256]{1,0:T(8,128)S(1)} %get-tuple-element.36), channel_id=1, source_target_pairs={{0,15},{1,0},{2,1},{3,2},{4,3},{5,4},{6,5},{7,6},{8,7},{9,8},{10,9... | collective-permute-start | bytes 24584 | tf_op jit(solution)/shard_map/ppermute | solution.py:413
  95.3 26.5 %collective-permute-start.2 = (f32[8,768]{1,0:T(8,128)S(1)}, f32[8,768]{1,0:T(8,128)S(1)}, u32[]{:S(2)}, u32[]{:S(2)}) collective-permute-start(f32[8,768]{1,0:T(8,128)S(1)} %pad_maximum_fusion.2), channel_id=1, source_target_pairs={{0,16},{16,32},{32,48},{48,64},{64,80},{80,96},{96,112},{112,0},{1... | collective-permute-start | bytes 73736 | tf_op jit(solution)/shard_map/ppermute | solution.py:416
  95.4 26.4 %collective-permute-start.3 = (f32[8,768]{1,0:T(8,128)S(1)}, f32[8,768]{1,0:T(8,128)S(1)}, u32[]{:S(2)}, u32[]{:S(2)}) collective-permute-start(f32[8,768]{1,0:T(8,128)S(1)} %pad_maximum_fusion.3), channel_id=1, source_target_pairs={{0,112},{16,0},{32,16},{48,32},{64,48},{80,64},{96,80},{112,96},{1... | collective-permute-start | bytes 73736 | tf_op jit(solution)/shard_map/ppermute | solution.py:417
  98.4 1.0 copy-start.23
  102.0 3.4 %copy-start.1 = (f32[1024,16,128]{2,1,0:T(8,128)S(1)}, f32[1024,16,128]{2,1,0:T(8,128)}, u32[]{:S(2)}) copy-start(f32[1024,16,128]{2,1,0:T(8,128)} %param.12) | copy-start | bytes 25165828
  105.4 1.0 copy-start.13
  106.4 1.0 copy-start.15
  (4 other events, 3.2 us)
where the time goes:
time: 125 us
  Pallas kernels  41.9 us (34%)
  starting transfers between devices  32.4 us (26%)
  local copies, waits for them, and re-layouts  27.9 us (22%)
  waiting for transfers between devices  21.3 us (17%)
    unnamed x53, local copies, waits for them, and re-layouts  27.9 us
    pallas_call x1, Pallas kernels, saturate(): pl.pallas_call(kernel, grid=(owned // size,), out_shape=jax.ShapeDtypeStr...  14.3 us
    pallas_call x1, Pallas kernels, response(): pl.pallas_call(kernel, grid=(owned // size,), out_shape=(jax.ShapeDtypeSt...  13.2 us
    all_to_all x1, starting transfers between devices, on_device(): lax.all_to_all(sent.reshape(peers, 1, wide), axes, split_axis=0, concat_a...  11.1 us
    ppermute x2, waiting for transfers between devices, exchange(): from_left = lax.ppermute(right_side, 'col', ring('col', 1))  11 us
    all_to_all x1, waiting for transfers between devices, on_device(): lax.all_to_all(sent.reshape(peers, 1, wide), axes, split_axis=0, concat_a...  10.3 us
    ppermute x2, starting transfers between devices, exchange(): from_right = lax.ppermute(left_side, 'col', ring('col', -1))  9.81 us
    ppermute x2, starting transfers between devices, exchange(): from_below = lax.ppermute(up_send, 'row', ring('row', -1))  5.87 us
  transfers between devices with their start and end apart: 10, of which 3 were waited for; matrix products, arithmetic and copies ran while one was open for 0% of the time, Pallas kernels for 26%

commit v1 on v0

v1 whole, which is shorter than its diff:
```python
import math

import jax
import jax.numpy as jnp
from jax import lax
from jax.experimental import pallas as pl
from jax.experimental.pallas import tpu as pltpu
from jax.sharding import PartitionSpec as P

SWEEPS = 4
LANES = 128
EDGE = 8
GROUPS = 4

layer_depth = 0.1
step_ratio = 0.1
residual_water = 0.05
pore_range = 0.4
couple_rate = 0.05
recharge_gain = 20.0
store_rate = 0.2

F32 = jnp.float32
BF16 = jnp.bfloat16
MIB = 1 << 20


def iota(shape, dim):
    return lax.broadcasted_iota(jnp.int32, shape, dim)


def params():
    return pltpu.CompilerParams(vmem_limit_bytes=56 * MIB)


def cost(us):
    return pl.CostEstimate(flops=0, bytes_accessed=int(us * 3.0e6), transcendentals=0)


def halves(x):
    high = x.astype(BF16)
    low = (x - high.astype(F32)).astype(BF16)
    return high, low


def hbm(x):
    return pltpu.with_memory_space_constraint(x, pltpu.HBM)


def vmem(x):
    return pltpu.with_memory_space_constraint(x, pltpu.VMEM)


def staged(body, name, ins, outs, scratch, us, after=(), held=(), left=(), pieces=None, in_smem=()):
    n, m, k = len(ins), len(outs), len(after)
    pieces = pieces or (1,) * m
    moved = [i for i in range(n) if i not in held and i not in in_smem]
    sent = [i for i in range(m) if i not in left]

    def kernel(*refs):
        in_at, out_at = refs[:n], refs[n + k : n + k + m]
        rest = refs[n + k + m :]
        in_ref = dict(zip(moved, rest))
        rest = rest[len(moved) :]
        out_ref = dict(enumerate(out_at)) | dict(zip(sent, rest))
        rest = rest[len(sent) :]
        in_sem, out_sem = rest[:2]
        reads = {i: pltpu.make_async_copy(in_at[i], in_ref[i], in_sem.at[i]) for i in moved}
        writes = {}
        for i in sent:
            size = outs[i].shape[0] // pieces[i]
            for p in range(pieces[i]):
                part = pl.ds(p * size, size)
                sem = out_sem.at[sum(pieces[:i]) + p]
                writes[i, p] = pltpu.make_async_copy(out_ref[i].at[part], out_at[i].at[part], sem)
        for read in reads.values():
            read.start()

        def take(i):
            if i not in moved:
                return in_at[i]
            reads[i].wait()
            return in_ref[i]

        body(take, [out_ref[i] for i in range(m)], lambda i, p=0: writes[i, p].start(), *rest[2:])
        for write in writes.values():
            write.wait()

    spaces = {**{i: pltpu.VMEM for i in held}, **{i: pltpu.SMEM for i in in_smem}}
    in_specs = [pl.BlockSpec(memory_space=spaces.get(i, pltpu.HBM)) for i in range(n)]
    placed = [x if i in in_smem else vmem(x) if i in held else hbm(x) for i, x in enumerate(ins)]
    return pl.pallas_call(
        kernel,
        out_shape=tuple(
            pltpu.VMEM(x.shape, x.dtype) if i in left else pltpu.HBM(x.shape, x.dtype) for i, x in enumerate(outs)
        ),
        in_specs=in_specs + [pl.BlockSpec(memory_space=pltpu.HBM)] * k,
        out_specs=tuple(pl.BlockSpec(memory_space=pltpu.VMEM if i in left else pltpu.HBM) for i in range(m)),
        scratch_shapes=[pltpu.VMEM(ins[i].shape, ins[i].dtype) for i in moved]
        + [pltpu.VMEM(outs[i].shape, outs[i].dtype) for i in sent]
        + [pltpu.SemaphoreType.DMA((n,)), pltpu.SemaphoreType.DMA((sum(pieces),))]
        + list(scratch),
        compiler_params=pltpu.CompilerParams(vmem_limit_bytes=40 * MIB),
        cost_estimate=cost(us),
        name=name,
    )(*placed, *[hbm(x) for x in after])


def floats(*shape):
    return jax.ShapeDtypeStruct(shape, F32)


def pack_kernel(peers, cap, owned, rows, cols, take, outs, give, hot_ref, data_ref):
    out_ref, place_ref = outs
    parts = cols // LANES
    blocks = rows * parts
    stride = 2 * cap + 1
    dest_ref = take(0)
    dest = jnp.concatenate([dest_ref[k : k + 1, :] for k in range(parts)], axis=1)
    shift = owned.bit_length() - 1
    owner = dest >> shift
    label = (dest & (owned - 1)) + 1
    owner_hot = owner == iota((peers, blocks), 0)
    before = (iota((LANES, LANES), 0) < iota((LANES, LANES), 1)).astype(F32).astype(BF16)
    carry = jnp.zeros((peers, 1), F32)
    ranks = []
    for chunk in range(blocks // LANES):
        hot = owner_hot[:, chunk * LANES : (chunk + 1) * LANES]
        hot_f = hot.astype(F32)
        count = jnp.dot(hot_f.astype(BF16), before, preferred_element_type=F32) + carry
        ranks.append(jnp.sum(count * hot_f, axis=0, keepdims=True))
        carry = carry + jnp.sum(hot_f, axis=1, keepdims=True)
    rank = jnp.concatenate(ranks, axis=1).astype(jnp.int32)
    place = owner + peers * rank
    place_f = place.astype(F32)
    eye = iota((LANES, LANES), 0) == iota((LANES, LANES), 1)
    for chunk in range(blocks // LANES):
        line = place_f[:, chunk * LANES : (chunk + 1) * LANES]
        place_ref[chunk * LANES : (chunk + 1) * LANES, :] = jnp.sum(
            jnp.where(eye, line, 0.0), axis=1, keepdims=True
        ).astype(jnp.int32)
    give(1)
    precip_ref, head_ref, land_ref = take(1), take(2), take(3)
    for part in range(parts):
        lane = slice(part * LANES, (part + 1) * LANES)
        line = slice(part * rows, (part + 1) * rows)
        infil = precip_ref[:, lane] * land_ref[:, lane].astype(F32)
        for at, piece in enumerate(halves(infil) + halves(head_ref[:, lane])):
            data_ref[line, at * LANES : (at + 1) * LANES] = piece
    owner_f = owner_hot.astype(F32)
    rank_hot = (rank == iota((LANES, blocks), 0)).astype(F32).astype(BF16)
    contract = (((1,), (1,)), ((), ()))
    tops = (owner_f * (label >> 5).astype(F32)).astype(BF16)
    lows = (owner_f * (label & 31).astype(F32)).astype(BF16)
    labels = 32.0 * lax.dot_general(tops, rank_hot, contract, preferred_element_type=F32)
    labels = labels + lax.dot_general(lows, rank_hot, contract, preferred_element_type=F32)
    out_ref[pl.ds(2 * cap, peers, stride=stride), :] = labels
    size = peers // GROUPS
    for group in range(GROUPS):
        for k in range(cap):
            at = (group * cap + k) * size
            hot_ref[at : at + size, :] = (
                (place == iota((size, blocks), 0) + (k * peers + group * size)).astype(F32).astype(BF16)
            )
        line = slice(group * cap * size, (group + 1) * cap * size)
        moved = jnp.dot(hot_ref[line, :], data_ref[...], preferred_element_type=F32)
        for k in range(cap):
            part = moved[k * size : (k + 1) * size]
            row = group * size * stride + k
            out_ref[pl.ds(row, size, stride=stride), :] = part[:, :LANES] + part[:, LANES : 2 * LANES]
            out_ref[pl.ds(row + cap, size, stride=stride), :] = part[:, 2 * LANES : 3 * LANES] + part[:, 3 * LANES :]
        give(0, group)


def pack(dest, precip, head, land, peers, cap, owned):
    rows, cols = precip.shape
    blocks = rows * cols // LANES

    def body(*refs):
        pack_kernel(peers, cap, owned, rows, cols, *refs)

    return staged(
        body,
        "pack_forcing",
        (jnp.transpose(dest), precip, head, land),
        (floats(peers * (2 * cap + 1), LANES), jax.ShapeDtypeStruct((blocks, 1), jnp.int32)),
        [pltpu.VMEM((peers * cap, blocks), BF16), pltpu.VMEM((blocks, 4 * LANES), BF16)],
        5,
        pieces=(GROUPS, 1),
    )


def layer_terms(moist, half_k, depth_factor):
    wet = moist * (1.0 / pore_range) - residual_water / pore_range
    wet2 = wet * wet
    a = half_k * depth_factor
    t = a * wet2
    return wet, 7.5 * t, t * wet, a + 5.0 * t


def inverse(x):
    y = pl.reciprocal(x, approx=True)
    return y * (2.0 - x * y)


def eliminate(layers, load, ksat, infil, response, keep):
    half_k = 0.5 * ksat
    moist = load(0)
    wet, hs, hc, d5 = layer_terms(moist, half_k, math.exp(-0.5 * layer_depth))
    flux_above = infil
    ratio = reduced = resp = hs_prev = g_prev = None
    for k in range(layers):
        last = k == layers - 1
        if not last:
            moist_n = load(k + 1)
            wet_n, hs_n, hc_n, d5_n = layer_terms(
                moist_n, half_k, math.exp(-(k + 1.5) * layer_depth)
            )
            g = d5 + d5_n
            flux = (hc + hc_n) - g * (moist_n - moist)
        if k == 0:
            diagonal = (g + step_ratio) + hs
        elif last:
            diagonal = (g_prev + (step_ratio + couple_rate)) + hs
        else:
            diagonal = (g_prev + step_ratio) + g
        if last:
            bottom = 2.0 * hc + couple_rate * (moist - residual_water)
            right = flux_above - bottom
        else:
            right = (0.0 - flux) if flux_above is None else (flux_above - flux)
        if k == 0:
            inv = inverse(diagonal)
            reduced = right * inv
            resp = inv
        else:
            neg_sub = hs_prev + g_prev
            inv = inverse(diagonal + neg_sub * ratio)
            reduced = (right + neg_sub * reduced) * inv
            if response:
                resp = neg_sub * resp * inv
        if last:
            return bottom, 2.0 * hs + couple_rate, reduced, resp, inv, wet
        ratio = (hs_n - g) * inv
        if keep is not None:
            keep(k, wet, ratio, reduced)
        hs_prev, g_prev = hs, g
        flux_above = flux
        moist, wet, hs, hc, d5 = moist_n, wet_n, hs_n, hc_n, d5_n


def response_kernel(layers, chunk, moist_ref, ksat_ref, alpha_ref, beta_ref, gamma_ref):
    def step(j, carry):
        base = j * (chunk * layers)
        line = pl.ds(j * chunk, chunk)
        load = lambda k: moist_ref[pl.ds(base + k, chunk, stride=layers), :]
        bottom, gain, reduced, resp, inv, _ = eliminate(layers, load, ksat_ref[line, :], None, True, None)
        alpha_ref[line, :] = bottom + gain * reduced
        beta_ref[line, :] = gain * resp
        gamma_ref[line, :] = (couple_rate * pore_range) * (gain * inv - 1.0)
        return carry

    lax.fori_loop(0, ksat_ref.shape[0] // chunk, step, 0)


def response(moist2, ksat, layers, half, count, after=()):
    owned = ksat.shape[0] // count
    size = 128
    first = half * (owned // size)

    def kernel(moist_ref, ksat_ref, *refs):
        response_kernel(layers, 32, moist_ref, ksat_ref, *refs[len(after) :])

    small = pl.BlockSpec((size, LANES), lambda i: (i, 0))
    return pl.pallas_call(
        kernel,
        grid=(owned // size,),
        out_shape=(pltpu.HBM((owned, LANES), F32),) * 3,
        in_specs=[
            pl.BlockSpec((size * layers, LANES), lambda i: (i + first, 0)),
            pl.BlockSpec((size, LANES), lambda i: (i + first, 0)),
        ]
        + [pl.BlockSpec(memory_space=pltpu.HBM)] * len(after),
        out_specs=(small,) * 3,
        compiler_params=params(),
        cost_estimate=cost(13 / count),
        name="column_response",
    )(*[hbm(x) for x in (moist2, ksat, *after)])


def saturation_kernel(layers, chunk, moist_ref, ksat_ref, infil_ref, share_ref, out_ref, wet_s, ratio_s, reduced_s):
    def step(j, carry):
        base = j * (chunk * layers)
        line = pl.ds(j * chunk, chunk)
        load = lambda k: moist_ref[pl.ds(base + k, chunk, stride=layers), :]

        def keep(k, wet, ratio, reduced):
            wet_s[k] = wet
            ratio_s[k] = ratio
            reduced_s[k] = reduced

        _, _, reduced, _, inv, wet = eliminate(layers, load, ksat_ref[line, :], infil_ref[line, :], False, keep)
        change = reduced + (couple_rate * pore_range) * share_ref[line, :] * inv
        out_ref[pl.ds(base + layers - 1, chunk, stride=layers), :] = wet + (1.0 / pore_range) * change
        for k in range(layers - 2, -1, -1):
            change = reduced_s[k] - ratio_s[k] * change
            out_ref[pl.ds(base + k, chunk, stride=layers), :] = wet_s[k] + (1.0 / pore_range) * change
        return carry

    lax.fori_loop(0, ksat_ref.shape[0] // chunk, step, 0)


def saturate(moist2, ksat, infil, share, layers):
    owned = ksat.shape[0]
    size, chunk = 128, 32

    def kernel(*refs):
        saturation_kernel(layers, chunk, *refs)

    small = pl.BlockSpec((size, LANES), lambda i: (i, 0))
    large = pl.BlockSpec((size * layers, LANES), lambda i: (i, 0))
    return pl.pallas_call(
        kernel,
        grid=(owned // size,),
        out_shape=pltpu.HBM((owned * layers, LANES), F32),
        in_specs=[large, small, small, small],
        out_specs=large,
        scratch_shapes=[pltpu.VMEM((layers - 1, chunk, LANES), F32)] * 3,
        compiler_params=params(),
        cost_estimate=cost(14),
        name="column_saturation",
    )(*[hbm(x) for x in (moist2, ksat, infil, share)])


def owner_kernel(peers, cap, owned, take, outs, give, data_ref, hot_ref, back_ref, rech_ref):
    infil_ref, share_ref, ans_ref = outs
    got_ref = take(0)
    stride = 2 * cap + 1
    labels = got_ref[pl.ds(2 * cap, peers, stride=stride), :]
    turned = jnp.transpose(labels).astype(jnp.int32) - 1
    labels = labels.astype(jnp.int32) - 1
    for k in range(cap):
        line = slice(k * peers, (k + 1) * peers)
        pieces = halves(got_ref[pl.ds(k, peers, stride=stride), :])
        pieces = pieces + halves(got_ref[pl.ds(cap + k, peers, stride=stride), :])
        for at, piece in enumerate(pieces):
            data_ref[line, at * LANES : (at + 1) * LANES] = piece
        hot_ref[:, line] = (turned[k : k + 1, :] == iota((owned, peers), 0)).astype(F32).astype(BF16)
    responses = [take(1 + k) for k in range(3)]
    group = 512
    alpha_ref, beta_ref, gamma_ref = responses
    for first in range(0, owned, group):
        line = slice(first, first + group)
        moved = jnp.dot(hot_ref[line, :], data_ref[...], preferred_element_type=F32)
        infil = moved[:, :LANES] + moved[:, LANES : 2 * LANES]
        head = moved[:, 2 * LANES : 3 * LANES] + moved[:, 3 * LANES :]
        share = jax.nn.sigmoid(head)
        infil_ref[line, :] = infil
        share_ref[line, :] = share
        rech = alpha_ref[line, :] + beta_ref[line, :] * infil + gamma_ref[line, :] * share
        high, low = halves(rech)
        rech_ref[line, :LANES] = high
        rech_ref[line, LANES:] = low
    give(0)
    give(1)
    size = peers // GROUPS
    for first in range(0, peers, size):
        for k in range(cap):
            at = first * cap + k * size
            back_ref[at : at + size, :] = (
                (labels[first : first + size, k : k + 1] == iota((size, owned), 1)).astype(F32).astype(BF16)
            )
        line = slice(first * cap, (first + size) * cap)
        moved = jnp.dot(back_ref[line, :], rech_ref[...], preferred_element_type=F32)
        for k in range(cap):
            part = moved[k * size : (k + 1) * size]
            ans_ref[pl.ds(first * cap + k, size, stride=cap), :] = part[:, :LANES] + part[:, LANES:]
        give(2, first // size)


def owner_side(got, responses, peers, cap, after):
    owned = responses[0].shape[0]

    def body(*refs):
        owner_kernel(peers, cap, owned, *refs)

    return staged(
        body,
        "owner_side",
        (got,) + tuple(responses),
        (floats(owned, LANES), floats(owned, LANES), floats(peers * cap, LANES)),
        [
            pltpu.VMEM((peers * cap, 4 * LANES), BF16),
            pltpu.VMEM((owned, peers * cap), BF16),
            pltpu.VMEM((peers * cap, owned), BF16),
            pltpu.VMEM((owned, 2 * LANES), BF16),
        ],
        8,
        after,
        held=(0,),
        pieces=(1, 1, GROUPS),
    )


def put_sides(x, left_ref, right_ref, at):
    cols = x.shape[1]
    left_ref[at : at + EDGE, :] = jnp.transpose(x[:, :LANES])[:EDGE, :]
    right_ref[at : at + EDGE, :] = jnp.transpose(x[:, cols - LANES :])[LANES - EDGE :, :]


def source_kernel(peers, cap, take, outs, give, data_ref, hot_ref):
    source_ref, left_ref, right_ref, up_ref, down_ref = outs
    rows, cols = source_ref.shape
    blocks = rows * cols // LANES
    place = take(1)[...]
    for k in range(cap):
        line = slice(k * peers, (k + 1) * peers)
        hot_ref[:, line] = (place == iota((blocks, peers), 1) + k * peers).astype(F32).astype(BF16)
    back_ref = take(0)
    for k in range(cap):
        line = slice(k * peers, (k + 1) * peers)
        high, low = halves(back_ref[pl.ds(k, peers, stride=cap), :])
        data_ref[line, :LANES] = high
        data_ref[line, LANES:] = low
    initial_ref = take(2)
    for part in range(cols // LANES):
        lane = slice(part * LANES, (part + 1) * LANES)
        moved = jnp.dot(hot_ref[part * rows : (part + 1) * rows, :], data_ref[...], preferred_element_type=F32)
        source_ref[:, lane] = store_rate * initial_ref[:, lane] + recharge_gain * (
            moved[:, :LANES] + moved[:, LANES:]
        )
    put_sides(source_ref[...], left_ref, right_ref, 0)
    up_ref[:EDGE, :] = source_ref[:EDGE, :]
    down_ref[:EDGE, :] = source_ref[rows - EDGE :, :]
    for i, ref in enumerate((left_ref, right_ref, up_ref, down_ref)):
        ref[EDGE:, :] = take(3 + i)[...]


def source_of(back, place, initial, edges, peers, cap, after):
    rows, cols = initial.shape
    blocks = place.shape[0]
    side, line = floats(4 * EDGE, rows), floats(4 * EDGE, cols)

    def body(*refs):
        source_kernel(peers, cap, *refs)

    return staged(
        body,
        "tile_source",
        (back, place, initial) + tuple(edges),
        (floats(rows, cols), side, side, line, line),
        [pltpu.VMEM((peers * cap, 2 * LANES), BF16), pltpu.VMEM((blocks, peers * cap), BF16)],
        4,
        after,
        held=(0,),
        left=range(5),
    )


def derive_kernel(take, outs, give):
    initial_ref, left_ref, right_ref, up_ref, down_ref, transmit_ref = outs
    rows = initial_ref.shape[0]
    head = take(0)[...]
    share = take(2)[...].astype(F32)
    initial = head * share
    initial_ref[...] = initial
    transmit = take(1)[...] * (1.0 + 0.5 * jnp.tanh(head))
    transmit_ref[...] = transmit
    for at, x in enumerate((initial, transmit, share)):
        put_sides(x, left_ref, right_ref, at * EDGE)
        up_ref[at * EDGE : (at + 1) * EDGE, :] = x[:EDGE, :]
        down_ref[at * EDGE : (at + 1) * EDGE, :] = x[rows - EDGE :, :]
    for i in range(6):
        give(i)


def derive(head, trans_coef, land):
    rows, cols = head.shape
    tile, side, line = floats(rows, cols), floats(3 * EDGE, rows), floats(3 * EDGE, cols)
    return staged(
        derive_kernel, "derive_tile", (head, trans_coef, land), (tile, side, side, line, line, tile), [], 3
    )


def exchange(up_line, down_line, left_side, right_side):
    rows = left_side.shape[1]

    def ring(axis, by):
        count = lax.axis_size(axis)
        return [(i, (i + by) % count) for i in range(count)]

    from_left = lax.ppermute(right_side, "col", ring("col", 1))
    from_right = lax.ppermute(left_side, "col", ring("col", -1))
    down_send = jnp.concatenate([down_line, from_left[:, rows - LANES :], from_right[:, rows - LANES :]], axis=1)
    up_send = jnp.concatenate([up_line, from_left[:, :LANES], from_right[:, :LANES]], axis=1)
    from_above = lax.ppermute(down_send, "row", ring("row", 1))
    from_below = lax.ppermute(up_send, "row", ring("row", -1))
    return from_left, from_right, from_above, from_below


def left_block(side):
    return jnp.transpose(jnp.concatenate([jnp.zeros((LANES - EDGE, LANES), F32), side], axis=0))


def right_block(side):
    return jnp.transpose(jnp.concatenate([side, jnp.zeros((LANES - EDGE, LANES), F32)], axis=0))


def put_edges(out_ref, rows, cols, sides, at):
    from_left, from_right, from_above, from_below = sides
    part = slice(at * EDGE, (at + 1) * EDGE)
    bottom = slice(EDGE + rows, 2 * EDGE + rows)
    right = slice(LANES + cols, 2 * LANES + cols)
    mid = slice(LANES, LANES + cols)
    out_ref[:EDGE, mid] = from_above[part, :cols]
    out_ref[bottom, mid] = from_below[part, :cols]
    for first in range(0, rows, LANES):
        line = slice(EDGE + first, EDGE + first + LANES)
        out_ref[line, :LANES] = left_block(from_left[part, first : first + LANES])
        out_ref[line, right] = right_block(from_right[part, first : first + LANES])
    out_ref[:EDGE, :LANES] = left_block(from_above[part, cols : cols + LANES])[LANES - EDGE :, :]
    out_ref[:EDGE, right] = right_block(from_above[part, cols + LANES :])[LANES - EDGE :, :]
    out_ref[bottom, :LANES] = left_block(from_below[part, cols : cols + LANES])[:EDGE, :]
    out_ref[bottom, right] = right_block(from_below[part, cols + LANES :])[:EDGE, :]


def shifted(x, by, axis):
    return pltpu.roll(x, by % x.shape[axis], axis)


def relax_kernel(take, outs, give, *ext_refs):
    (out_ref,) = outs
    rows, cols = out_ref.shape
    height, width = ext_refs[0].shape
    where = take(0)
    sides = [take(5 + i) for i in range(4)]
    for at in range(4):
        put_edges(ext_refs[at], rows, cols, sides, at)
    i = iota((height, width), 0)
    j = iota((height, width), 1)
    inside = (i >= where[0]) & (i < where[1]) & (j >= where[2]) & (j < where[3])

    def extended(tile, at):
        ext_refs[at][EDGE : EDGE + rows, LANES : LANES + cols] = tile
        return jnp.where(inside, ext_refs[at][...], 0.0)

    transmit = extended(take(1)[...], 2)
    share = extended(take(2)[...].astype(F32), 3)
    up = 0.5 * (transmit + shifted(transmit, 1, 0))
    down = 0.5 * (transmit + shifted(transmit, -1, 0))
    left = 0.5 * (transmit + shifted(transmit, 1, 1))
    right = 0.5 * (transmit + shifted(transmit, -1, 1))
    scale = share / (store_rate + (up + down + left + right))
    up_ref, down_ref, left_ref, right_ref = ext_refs[4:]
    up_ref[...] = up * scale
    down_ref[...] = down * scale
    left_ref[...] = left * scale
    right_ref[...] = right * scale
    surface = extended(take(3)[...], 1)
    forced = scale * extended(take(4)[...], 0)
    for _ in range(SWEEPS):
        inflow = up_ref[...] * shifted(surface, 1, 0) + down_ref[...] * shifted(surface, -1, 0)
        inflow = inflow + left_ref[...] * shifted(surface, 1, 1) + right_ref[...] * shifted(surface, -1, 1)
        surface = forced + inflow
    out_ref[...] = surface[EDGE : EDGE + rows, LANES : LANES + cols]
    give(0)


def relax(where, transmit, land, initial, source, sides):
    rows, cols = source.shape
    ext = (rows + 2 * EDGE, cols + 2 * LANES)
    return staged(
        relax_kernel,
        "lateral_relax",
        (where, transmit, land, initial, source) + tuple(sides),
        (floats(rows, cols),),
        [pltpu.VMEM(ext, F32)] * 8,
        6,
        held=range(4, 9),
        in_smem=(0,),
    )[0]


def on_device(precip, head, trans_coef, land, dest, moisture, ksat):
    rows, cols = precip.shape
    row_count = lax.axis_size("row")
    col_count = lax.axis_size("col")
    peers = row_count * col_count
    owned, layers, _ = moisture.shape
    cap = 2 * (rows * cols // LANES) // peers
    axes = ("row", "col")
    moist2 = moisture.reshape(owned * layers, LANES)

    sent, place = pack(dest, precip, head, land, peers, cap, owned)
    wide = (2 * cap + 1) * LANES
    got = lax.all_to_all(sent.reshape(peers, 1, wide), axes, split_axis=0, concat_axis=0, tiled=True)
    got = got.reshape(peers * (2 * cap + 1), LANES)

    initial, left, right, up, down, transmit = derive(head, trans_coef, land)
    responses = response(moist2, ksat, layers, 0, 1, (left,))
    row_at, col_at = lax.axis_index("row"), lax.axis_index("col")
    where = jnp.stack(
        [
            jnp.where(row_at == 0, EDGE, 0),
            jnp.where(row_at == row_count - 1, EDGE + rows, 2 * EDGE + rows),
            jnp.where(col_at == 0, LANES, 0),
            jnp.where(col_at == col_count - 1, LANES + cols, 2 * LANES + cols),
        ]
    ).astype(jnp.int32)

    infil, share, answer = owner_side(got, responses, peers, cap, ())
    back = lax.all_to_all(answer.reshape(peers, cap, LANES), axes, split_axis=0, concat_axis=0, tiled=True)
    back = back.reshape(peers * cap, LANES)
    saturation = saturate(moist2, ksat, infil, share, layers)

    source, *edges = source_of(back, place, initial, (left, right, up, down), peers, cap, (saturation,))
    left, right, up, down = edges
    surface = relax(where, transmit, land, initial, source, exchange(up, down, left, right))
    return (saturation.reshape(owned, layers, LANES), surface)


def solution(mesh):
    tile = P("row", "col")
    return jax.shard_map(
        on_device,
        mesh=mesh,
        in_specs=(tile,) * 5 + (P(("row", "col"), None, None), P(("row", "col"), None)),
        out_specs=(P(("row", "col"), None, None), tile),
        check_vma=False,
    )
```

time: 125 us -> 102 us (0.82)
  local copies, waits for them, and re-layouts: 27.9 us -> 0.01 us
  Pallas kernels: 41.9 us -> 55.6 us
  starting transfers between devices: 32.4 us -> 24.4 us
  waiting for transfers between devices: 21.3 us -> 19.8 us
    unnamed x53 -> x0, local copies, waits for them, and re-layouts: 27.9 us -> none
    pallas_call x8 -> x7, Pallas kernels: 41.9 us -> 55.6 us  [the longest x5 24.6 us: staged(): pl.pallas_call(kernel, out_shape=tuple((pltpu.VMEM(x.shape, x.dtype) if i...]
    ppermute x2 -> x1, waiting for transfers between devices: 11 us -> 1.89 us  [exchange(): from_left = lax.ppermute(right_side, 'col', ring('col', 1))]
    ppermute x2 -> x1, starting transfers between devices: 9.81 us -> 4.63 us  [exchange(): from_right = lax.ppermute(left_side, 'col', ring('col', -1))]
    all_to_all x1, waiting for transfers between devices: 0.01 us -> 3.18 us  [on_device(): lax.all_to_all(answer.reshape(peers, cap, LANES), axes, split_axis=0, con...]
    ppermute x2 -> x1, starting transfers between devices: 5.87 us -> 2.95 us  [exchange(): from_below = lax.ppermute(up_send, 'row', ring('row', -1))]
    all_to_all x1, waiting for transfers between devices: 10.3 us -> 12.5 us  [on_device(): lax.all_to_all(sent.reshape(peers, 1, wide), axes, split_axis=0, concat_a...]
    ppermute x2 -> x1, waiting for transfers between devices: 0.01 us -> 2.2 us  [exchange(): from_above = lax.ppermute(down_send, 'row', ring('row', 1))]
  transfers between devices with their start and end apart: 10 -> 6, of which waited for: 3 -> 4; matrix products, arithmetic and copies ran while one was open for 0% -> 0% of each run, Pallas kernels for 26% -> 33%
where the time goes in v1:
time: 102 us; the launch traced here: 101 us
  Pallas kernels  55.6 us (55%)
  starting transfers between devices  24.4 us (24%)
  waiting for transfers between devices  19.8 us (19%)
    pallas_call x5, Pallas kernels, staged(): pl.pallas_call(kernel, out_shape=tuple((pltpu.VMEM(x.shape, x.dtype) if i...  24.6 us
    pallas_call x1, Pallas kernels, saturate(): pl.pallas_call(kernel, grid=(owned // size,), out_shape=pltpu.HBM((owned...  15.7 us
    pallas_call x1, Pallas kernels, response(): pl.pallas_call(kernel, grid=(owned // size,), out_shape=(pltpu.HBM((owned...  15.2 us
    all_to_all x1, waiting for transfers between devices, on_device(): lax.all_to_all(sent.reshape(peers, 1, wide), axes, split_axis=0, concat_a...  12.5 us
    all_to_all x1, starting transfers between devices, on_device(): lax.all_to_all(sent.reshape(peers, 1, wide), axes, split_axis=0, concat_a...  11.2 us
    all_to_all x1, starting transfers between devices, on_device(): lax.all_to_all(answer.reshape(peers, cap, LANES), axes, split_axis=0, con...  4.83 us
    ppermute x1, starting transfers between devices, exchange(): from_right = lax.ppermute(left_side, 'col', ring('col', -1))  4.63 us
    all_to_all x1, waiting for transfers between devices, on_device(): lax.all_to_all(answer.reshape(peers, cap, LANES), axes, split_axis=0, con...  3.18 us
  transfers between devices with their start and end apart: 6, of which 4 were waited for; matrix products, arithmetic and copies ran while one was open for 0% of the time, Pallas kernels for 33%

profile of v1, /device:TPU:0, one launch (start us, length us, event | category | flops | bytes accessed | tf_op | source)
XLA Modules:
  0.0 100.7 jit_solution(318862118659656555)
XLA Ops:
  0.6 4.8 %pack_forcing.1 = (f32[4224,128]{1,0:T(8,128)}, s32[1024,1]{1,0:T(8,128)}) custom-call(s32[4,256]{1,0:T(4,128)} %bitcast.18, f32[256,512]{1,0:T(8,128)} %refs_1_.3, f32[256,512]{1,0:T(8,128)} %refs_0_.1, s32[256,512]{1,0:T(8,128)} %refs_2_.5), custom_call_target="tpu_custom_call" | custom-call | bytes 15000000 | tf_op jit(solution)/shard_map/pack_forcing/pallas_call | solution.py:92
  5.4 11.2 %all-to-all-start = ((f32[128,1,4224]{2,1,0:T(1,128)}), f32[128,1,4224]{2,1,0:T(1,128)S(1)}, u32[]{:S(2)}, u32[]{:S(2)}) async-start(f32[128,1,4224]{2,1,0:T(1,128)} %bitcast.16), calls=%async_computation | async-start | bytes 4325376 | tf_op jit(solution)/shard_map/all_to_all | solution.py:596
  16.6 2.6 %derive_tile.1 = (f32[256,512]{1,0:T(8,128)}, f32[24,256]{1,0:T(8,128)}, f32[24,256]{1,0:T(8,128)}, f32[24,512]{1,0:T(8,128)}, f32[24,512]{1,0:T(8,128)}, /*index=5*/f32[256,512]{1,0:T(8,128)}) custom-call(f32[256,512]{1,0:T(8,128)} %refs_0_.1, f32[256,512]{1,0:T(8,128)} %refs_1_.4, s32[256,512]{1,0:T(8,128)} %refs_2_.5), custom_call_target="tpu_custom_call" | custom-call | bytes 9000000 | tf_op jit(solution)/shard_map/derive_tile/pallas_call | solution.py:92
  19.2 15.2 %column_response.1 = (f32[1024,128]{1,0:T(8,128)}, f32[1024,128]{1,0:T(8,128)}, f32[1024,128]{1,0:T(8,128)}) custom-call(f32[16384,128]{1,0:T(8,128)} %bitcast.13, f32[1024,128]{1,0:T(8,128)} %refs_1_.5, f32[24,256]{1,0:T(8,128)} %get-tuple-element.22.refs_0_.refs_3_), custom_call_target="tpu_custom_call" | custom-call | bytes 39000000 | tf_op jit(solution)/shard_map/column_response/pallas_call | solution.py:275
  34.4 12.5 %all-to-all-done = f32[128,1,4224]{2,1,0:T(1,128)S(1)} async-done(((f32[128,1,4224]{2,1,0:T(1,128)}), f32[128,1,4224]{2,1,0:T(1,128)S(1)}, u32[]{:S(2)}, u32[]{:S(2)}) %all-to-all-start) | async-done | bytes 2162720 | tf_op jit(solution)/shard_map/all_to_all | solution.py:596
  47.0 7.5 %owner_side.1 = (f32[1024,128]{1,0:T(8,128)}, f32[1024,128]{1,0:T(8,128)}, f32[2048,128]{1,0:T(8,128)}) custom-call(f32[4224,128]{1,0:T(8,128)S(1)} %bitcast.11, f32[1024,128]{1,0:T(8,128)} %get-tuple-element.23.refs_1_, f32[1024,128]{1,0:T(8,128)} %get-tuple-element.24.refs_2_, f32[1024,128]{1,0:T(8,128)} %get-tuple-element.25.refs_3_), custom_call_target="tpu_custom_call" | custom-call | bytes 24000000 | tf_op jit(solution)/shard_map/owner_side/pallas_call | solution.py:92
  54.4 4.8 %all-to-all-start.1 = ((f32[128,16,128]{2,1,0:T(8,128)}), f32[128,16,128]{2,1,0:T(8,128)S(1)}, u32[]{:S(2)}, u32[]{:S(2)}) async-start(f32[128,16,128]{2,1,0:T(8,128)} %bitcast.17), calls=%async_computation.1 | async-start | bytes 2097152 | tf_op jit(solution)/shard_map/all_to_all | solution.py:612
  59.3 15.7 %column_saturation.1.refs_7_ = f32[16384,128]{1,0:T(8,128)} custom-call(f32[16384,128]{1,0:T(8,128)} %bitcast.14, f32[1024,128]{1,0:T(8,128)} %refs_1_.5, f32[1024,128]{1,0:T(8,128)} %get-tuple-element.26.refs_2_, f32[1024,128]{1,0:T(8,128)} %get-tuple-element.27.refs_3_), custom_call_target="tpu_custom_call" | custom-call | bytes 42000000 | tf_op jit(solution)/shard_map/column_saturation/pallas_call | solution.py:322
  74.9 3.2 %all-to-all-done.1 = f32[128,16,128]{2,1,0:T(8,128)S(1)} async-done(((f32[128,16,128]{2,1,0:T(8,128)}), f32[128,16,128]{2,1,0:T(8,128)S(1)}, u32[]{:S(2)}, u32[]{:S(2)}) %all-to-all-start.1) | async-done | bytes 1048608 | tf_op jit(solution)/shard_map/all_to_all | solution.py:612
  78.1 3.8 %tile_source.1 = (f32[256,512]{1,0:T(8,128)S(1)}, f32[32,256]{1,0:T(8,128)S(1)}, f32[32,256]{1,0:T(8,128)S(1)}, f32[32,512]{1,0:T(8,128)S(1)}, f32[32,512]{1,0:T(8,128)S(1)}) custom-call(f32[2048,128]{1,0:T(8,128)S(1)} %bitcast.12, s32[1024,1]{1,0:T(8,128)} %get-tuple-element.31.refs_1_, f32[256,512]{1,0:T(8,128)} %get-tuple-element.29.refs_2_.refs_3_, ...), custom_call_target="tpu_custom_call" | custom-call | bytes 12000000 | tf_op jit(solution)/shard_map/tile_source/pallas_call | solution.py:92
  81.9 0.8 collective-permute-start
  82.7 4.6 %collective-permute-start.1 = (f32[32,256]{1,0:T(8,128)S(1)}, f32[32,256]{1,0:T(8,128)S(1)}, u32[]{:S(2)}, u32[]{:S(2)}) collective-permute-start(f32[32,256]{1,0:T(8,128)S(1)} %get-tuple-element.37), channel_id=1, source_target_pairs={{0,15},{1,0},{2,1},{3,2},{4,3},{5,4},{6,5},{7,6},{8,7},{9,8},{10,9... | collective-permute-start | bytes 98312 | tf_op jit(solution)/shard_map/ppermute | solution.py:493
  87.3 1.9 %collective-permute-done.refs_5_ = f32[32,256]{1,0:T(8,128)S(1)} collective-permute-done((f32[32,256]{1,0:T(8,128)S(1)}, f32[32,256]{1,0:T(8,128)S(1)}, u32[]{:S(2)}, u32[]{:S(2)}) %collective-permute-start) | collective-permute-done | bytes 32800 | tf_op jit(solution)/shard_map/ppermute | solution.py:492
  89.2 0.0 collective-permute-done.1.refs_6_
  89.3 0.0 collective-permute-start.2
  89.3 2.9 %collective-permute-start.3 = (f32[32,768]{1,0:T(8,128)S(1)}, f32[32,768]{1,0:T(8,128)S(1)}, u32[]{:S(2)}, u32[]{:S(2)}) collective-permute-start(f32[32,768]{1,0:T(8,128)S(1)} %pad_maximum_fusion.1), channel_id=1, source_target_pairs={{0,112},{16,0},{32,16},{48,32},{64,48},{80,64},{96,80},{112,96},{1... | collective-permute-start | bytes 294920 | tf_op jit(solution)/shard_map/ppermute | solution.py:497
  92.3 0.1 pad_add_fusion.refs_0_
  92.3 2.2 %collective-permute-done.2.refs_7_ = f32[32,768]{1,0:T(8,128)S(1)} collective-permute-done((f32[32,768]{1,0:T(8,128)S(1)}, f32[32,768]{1,0:T(8,128)S(1)}, u32[]{:S(2)}, u32[]{:S(2)}) %collective-permute-start.2) | collective-permute-done | bytes 98336 | tf_op jit(solution)/shard_map/ppermute | solution.py:496
  94.5 0.0 collective-permute-done.3.refs_8_
  94.5 6.0 %lateral_relax.1 = f32[256,512]{1,0:T(8,128)} custom-call(s32[4]{0:T(128)S(1)} %pad_add_fusion.refs_0_, f32[256,512]{1,0:T(8,128)} %get-tuple-element.28.refs_1_, s32[256,512]{1,0:T(8,128)} %refs_2_.5, f32[256,512]{1,0:T(8,128)} %get-tuple-element.29.refs_2_.refs_3_, f32[256,512]{1,0:T(8,128)S(1)} %get-tuple-element.35.refs_4_, ...), custom_call_target="tpu_custom_call" | custom-call | bytes 18000000 | tf_op jit(solution)/shard_map/lateral_relax/pallas_call | solution.py:92
  (4 shorter events, 0.0 us)
Async XLA Ops:
  5.4 41.5 %all-to-all-start = ((f32[128,1,4224]{2,1,0:T(1,128)}), f32[128,1,4224]{2,1,0:T(1,128)S(1)}, u32[]{:S(2)}, u32[]{:S(2)}) async-start(f32[128,1,4224]{2,1,0:T(1,128)} %bitcast.16), calls=%async_computation | async-start | bytes 4325376 | tf_op jit(solution)/shard_map/all_to_all | solution.py:596
  54.4 23.7 %all-to-all-start.1 = ((f32[128,16,128]{2,1,0:T(8,128)}), f32[128,16,128]{2,1,0:T(8,128)S(1)}, u32[]{:S(2)}, u32[]{:S(2)}) async-start(f32[128,16,128]{2,1,0:T(8,128)} %bitcast.17), calls=%async_computation.1 | async-start | bytes 2097152 | tf_op jit(solution)/shard_map/all_to_all | solution.py:612
  81.9 7.3 %collective-permute-start = (f32[32,256]{1,0:T(8,128)S(1)}, f32[32,256]{1,0:T(8,128)S(1)}, u32[]{:S(2)}, u32[]{:S(2)}) collective-permute-start(f32[32,256]{1,0:T(8,128)S(1)} %get-tuple-element.36), channel_id=1, source_target_pairs={{0,1},{1,2},{2,3},{3,4},{4,5},{5,6},{6,7},{7,8},{8,9},{9,10},{10,1... | collective-permute-start | bytes 98312 | tf_op jit(solution)/shard_map/ppermute | solution.py:492
  82.7 6.5 %collective-permute-start.1 = (f32[32,256]{1,0:T(8,128)S(1)}, f32[32,256]{1,0:T(8,128)S(1)}, u32[]{:S(2)}, u32[]{:S(2)}) collective-permute-start(f32[32,256]{1,0:T(8,128)S(1)} %get-tuple-element.37), channel_id=1, source_target_pairs={{0,15},{1,0},{2,1},{3,2},{4,3},{5,4},{6,5},{7,6},{8,7},{9,8},{10,9... | collective-permute-start | bytes 98312 | tf_op jit(solution)/shard_map/ppermute | solution.py:493
  89.3 5.3 %collective-permute-start.2 = (f32[32,768]{1,0:T(8,128)S(1)}, f32[32,768]{1,0:T(8,128)S(1)}, u32[]{:S(2)}, u32[]{:S(2)}) collective-permute-start(f32[32,768]{1,0:T(8,128)S(1)} %pad_maximum_fusion), channel_id=1, source_target_pairs={{0,16},{16,32},{32,48},{48,64},{64,80},{80,96},{96,112},{112,0},{1... | collective-permute-start | bytes 294920 | tf_op jit(solution)/shard_map/ppermute | solution.py:496
  89.3 5.2 %collective-permute-start.3 = (f32[32,768]{1,0:T(8,128)S(1)}, f32[32,768]{1,0:T(8,128)S(1)}, u32[]{:S(2)}, u32[]{:S(2)}) collective-permute-start(f32[32,768]{1,0:T(8,128)S(1)} %pad_maximum_fusion.1), channel_id=1, source_target_pairs={{0,112},{16,0},{32,16},{48,32},{64,48},{80,64},{96,80},{112,96},{1... | collective-permute-start | bytes 294920 | tf_op jit(solution)/shard_map/ppermute | solution.py:497

commit v2 on v1

--- a/solution.py
+++ b/solution.py
@@ -10,6 +10,7 @@
 SWEEPS = 4
 LANES = 128
 EDGE = 8
+PAD = 8
 GROUPS = 4
 
 layer_depth = 0.1
@@ -30,7 +31,7 @@
 
 
 def params():
-    return pltpu.CompilerParams(vmem_limit_bytes=56 * MIB)
+    return pltpu.CompilerParams(vmem_limit_bytes=24 * MIB)
 
 
 def cost(us):
@@ -51,7 +52,7 @@
     return pltpu.with_memory_space_constraint(x, pltpu.VMEM)
 
 
-def staged(body, name, ins, outs, scratch, us, after=(), held=(), left=(), pieces=None, in_smem=()):
+def staged(body, name, ins, outs, scratch, us, after=(), held=(), left=(), pieces=None, by_lanes=False, in_smem=(), small=False):
     n, m, k = len(ins), len(outs), len(after)
     pieces = pieces or (1,) * m
     moved = [i for i in range(n) if i not in held and i not in in_smem]
@@ -68,9 +69,10 @@
         reads = {i: pltpu.make_async_copy(in_at[i], in_ref[i], in_sem.at[i]) for i in moved}
         writes = {}
         for i in sent:
-            size = outs[i].shape[0] // pieces[i]
+            size = outs[i].shape[by_lanes] // pieces[i]
             for p in range(pieces[i]):
                 part = pl.ds(p * size, size)
+                part = (slice(None), part) if by_lanes else part
                 sem = out_sem.at[sum(pieces[:i]) + p]
                 writes[i, p] = pltpu.make_async_copy(out_ref[i].at[part], out_at[i].at[part], sem)
         for read in reads.values():
@@ -94,7 +96,7 @@
         out_shape=tuple(
             pltpu.VMEM(x.shape, x.dtype) if i in left else pltpu.HBM(x.shape, x.dtype) for i, x in enumerate(outs)
         ),
-        in_specs=in_specs + [pl.BlockSpec(memory_space=pltpu.HBM)] * k,
+        in_specs=in_specs + [pl.BlockSpec(memory_space=pltpu.VMEM if small else pltpu.HBM)] * k,
         out_specs=tuple(pl.BlockSpec(memory_space=pltpu.VMEM if i in left else pltpu.HBM) for i in range(m)),
         scratch_shapes=[pltpu.VMEM(ins[i].shape, ins[i].dtype) for i in moved]
         + [pltpu.VMEM(outs[i].shape, outs[i].dtype) for i in sent]
@@ -103,7 +105,7 @@
         compiler_params=pltpu.CompilerParams(vmem_limit_bytes=40 * MIB),
         cost_estimate=cost(us),
         name=name,
-    )(*placed, *[hbm(x) for x in after])
+    )(*placed, *[vmem(x) if small else hbm(x) for x in after])
 
 
 def floats(*shape):
@@ -132,21 +134,8 @@
         carry = carry + jnp.sum(hot_f, axis=1, keepdims=True)
     rank = jnp.concatenate(ranks, axis=1).astype(jnp.int32)
     place = owner + peers * rank
-    place_f = place.astype(F32)
-    eye = iota((LANES, LANES), 0) == iota((LANES, LANES), 1)
-    for chunk in range(blocks // LANES):
-        line = place_f[:, chunk * LANES : (chunk + 1) * LANES]
-        place_ref[chunk * LANES : (chunk + 1) * LANES, :] = jnp.sum(
-            jnp.where(eye, line, 0.0), axis=1, keepdims=True
-        ).astype(jnp.int32)
+    place_ref[...] = place
     give(1)
-    precip_ref, head_ref, land_ref = take(1), take(2), take(3)
-    for part in range(parts):
-        lane = slice(part * LANES, (part + 1) * LANES)
-        line = slice(part * rows, (part + 1) * rows)
-        infil = precip_ref[:, lane] * land_ref[:, lane].astype(F32)
-        for at, piece in enumerate(halves(infil) + halves(head_ref[:, lane])):
-            data_ref[line, at * LANES : (at + 1) * LANES] = piece
     owner_f = owner_hot.astype(F32)
     rank_hot = (rank == iota((LANES, blocks), 0)).astype(F32).astype(BF16)
     contract = (((1,), (1,)), ((), ()))
@@ -156,12 +145,25 @@
     labels = labels + lax.dot_general(lows, rank_hot, contract, preferred_element_type=F32)
     out_ref[pl.ds(2 * cap, peers, stride=stride), :] = labels
     size = peers // GROUPS
-    for group in range(GROUPS):
+
+    def mark(group):
         for k in range(cap):
             at = (group * cap + k) * size
             hot_ref[at : at + size, :] = (
                 (place == iota((size, blocks), 0) + (k * peers + group * size)).astype(F32).astype(BF16)
             )
+
+    mark(0)
+    precip_ref, head_ref, land_ref = take(1), take(2), take(3)
+    for part in range(parts):
+        lane = slice(part * LANES, (part + 1) * LANES)
+        line = slice(part * rows, (part + 1) * rows)
+        infil = precip_ref[:, lane] * land_ref[:, lane].astype(F32)
+        for at, piece in enumerate(halves(infil) + halves(head_ref[:, lane])):
+            data_ref[line, at * LANES : (at + 1) * LANES] = piece
+    for group in range(GROUPS):
+        if group + 1 < GROUPS:
+            mark(group + 1)
         line = slice(group * cap * size, (group + 1) * cap * size)
         moved = jnp.dot(hot_ref[line, :], data_ref[...], preferred_element_type=F32)
         for k in range(cap):
@@ -183,7 +185,7 @@
         body,
         "pack_forcing",
         (jnp.transpose(dest), precip, head, land),
-        (floats(peers * (2 * cap + 1), LANES), jax.ShapeDtypeStruct((blocks, 1), jnp.int32)),
+        (floats(peers * (2 * cap + 1), LANES), jax.ShapeDtypeStruct((1, blocks), jnp.int32)),
         [pltpu.VMEM((peers * cap, blocks), BF16), pltpu.VMEM((blocks, 4 * LANES), BF16)],
         5,
         pieces=(GROUPS, 1),
@@ -199,8 +201,7 @@
 
 
 def inverse(x):
-    y = pl.reciprocal(x, approx=True)
-    return y * (2.0 - x * y)
+    return 1.0 / x
 
 
 def eliminate(layers, load, ksat, infil, response, keep):
@@ -263,29 +264,24 @@
     lax.fori_loop(0, ksat_ref.shape[0] // chunk, step, 0)
 
 
-def response(moist2, ksat, layers, half, count, after=()):
-    owned = ksat.shape[0] // count
+def response(moist2, ksat, layers):
+    owned = ksat.shape[0]
     size = 128
-    first = half * (owned // size)
-
-    def kernel(moist_ref, ksat_ref, *refs):
-        response_kernel(layers, 32, moist_ref, ksat_ref, *refs[len(after) :])
+
+    def kernel(*refs):
+        response_kernel(layers, 128, *refs)
 
     small = pl.BlockSpec((size, LANES), lambda i: (i, 0))
     return pl.pallas_call(
         kernel,
         grid=(owned // size,),
         out_shape=(pltpu.HBM((owned, LANES), F32),) * 3,
-        in_specs=[
-            pl.BlockSpec((size * layers, LANES), lambda i: (i + first, 0)),
-            pl.BlockSpec((size, LANES), lambda i: (i + first, 0)),
-        ]
-        + [pl.BlockSpec(memory_space=pltpu.HBM)] * len(after),
+        in_specs=[pl.BlockSpec((size * layers, LANES), lambda i: (i, 0)), small],
         out_specs=(small,) * 3,
         compiler_params=params(),
-        cost_estimate=cost(13 / count),
+        cost_estimate=cost(13),
         name="column_response",
-    )(*[hbm(x) for x in (moist2, ksat, *after)])
+    )(hbm(moist2), hbm(ksat))
 
 
 def saturation_kernel(layers, chunk, moist_ref, ksat_ref, infil_ref, share_ref, out_ref, wet_s, ratio_s, reduced_s):
@@ -339,16 +335,23 @@
     labels = got_ref[pl.ds(2 * cap, peers, stride=stride), :]
     turned = jnp.transpose(labels).astype(jnp.int32) - 1
     labels = labels.astype(jnp.int32) - 1
+    group = owned // 2
+
+    def mark(first):
+        for k in range(cap):
+            hot_ref[first : first + group, k * peers : (k + 1) * peers] = (
+                (turned[k : k + 1, :] == iota((group, peers), 0) + first).astype(F32).astype(BF16)
+            )
+
     for k in range(cap):
         line = slice(k * peers, (k + 1) * peers)
         pieces = halves(got_ref[pl.ds(k, peers, stride=stride), :])
         pieces = pieces + halves(got_ref[pl.ds(cap + k, peers, stride=stride), :])
         for at, piece in enumerate(pieces):
             data_ref[line, at * LANES : (at + 1) * LANES] = piece
-        hot_ref[:, line] = (turned[k : k + 1, :] == iota((owned, peers), 0)).astype(F32).astype(BF16)
-    responses = [take(1 + k) for k in range(3)]
-    group = 512
-    alpha_ref, beta_ref, gamma_ref = responses
+    mark(0)
+    alpha_ref, beta_ref, gamma_ref = [take(1 + k) for k in range(3)]
+    mark(group)
     for first in range(0, owned, group):
         line = slice(first, first + group)
         moved = jnp.dot(hot_ref[line, :], data_ref[...], preferred_element_type=F32)
@@ -361,21 +364,27 @@
         high, low = halves(rech)
         rech_ref[line, :LANES] = high
         rech_ref[line, LANES:] = low
-    give(0)
-    give(1)
     size = peers // GROUPS
-    for first in range(0, peers, size):
+    for turn in range(GROUPS):
+        first = turn * size
         for k in range(cap):
             at = first * cap + k * size
             back_ref[at : at + size, :] = (
                 (labels[first : first + size, k : k + 1] == iota((size, owned), 1)).astype(F32).astype(BF16)
             )
+    for turn in range(GROUPS):
+        first = turn * size
         line = slice(first * cap, (first + size) * cap)
         moved = jnp.dot(back_ref[line, :], rech_ref[...], preferred_element_type=F32)
         for k in range(cap):
             part = moved[k * size : (k + 1) * size]
             ans_ref[pl.ds(first * cap + k, size, stride=cap), :] = part[:, :LANES] + part[:, LANES:]
-        give(2, first // size)
+        if turn == 1:
+            give(0)
+            give(1)
+            give(2, 0)
+        if turn > 0:
+            give(2, turn)
 
 
 def owner_side(got, responses, peers, cap, after):
@@ -399,6 +408,7 @@
         after,
         held=(0,),
         pieces=(1, 1, GROUPS),
+        small=True,
     )
 
 
@@ -409,36 +419,40 @@
 
 
 def source_kernel(peers, cap, take, outs, give, data_ref, hot_ref):
-    source_ref, left_ref, right_ref, up_ref, down_ref = outs
-    rows, cols = source_ref.shape
+    flow_ref, left_ref, right_ref, up_ref, down_ref = outs
+    rows, cols = flow_ref.shape
     blocks = rows * cols // LANES
-    place = take(1)[...]
-    for k in range(cap):
-        line = slice(k * peers, (k + 1) * peers)
-        hot_ref[:, line] = (place == iota((blocks, peers), 1) + k * peers).astype(F32).astype(BF16)
     back_ref = take(0)
     for k in range(cap):
         line = slice(k * peers, (k + 1) * peers)
         high, low = halves(back_ref[pl.ds(k, peers, stride=cap), :])
         data_ref[line, :LANES] = high
         data_ref[line, LANES:] = low
-    initial_ref = take(2)
+    place_f = take(1)[...].astype(F32)
+    for i, ref in enumerate((left_ref, right_ref, up_ref, down_ref)):
+        ref[EDGE:, :] = take(2 + i)[...]
+    eye = iota((LANES, LANES), 0) == iota((LANES, LANES), 1)
+    for first in range(0, blocks, LANES):
+        column = jnp.sum(jnp.where(eye, place_f[:, first : first + LANES], 0.0), axis=1, keepdims=True)
+        column = column.astype(jnp.int32)
+        for k in range(cap):
+            hot_ref[first : first + LANES, k * peers : (k + 1) * peers] = (
+                (column == iota((LANES, peers), 1) + k * peers).astype(F32).astype(BF16)
+            )
     for part in range(cols // LANES):
-        lane = slice(part * LANES, (part + 1) * LANES)
         moved = jnp.dot(hot_ref[part * rows : (part + 1) * rows, :], data_ref[...], preferred_element_type=F32)
-        source_ref[:, lane] = store_rate * initial_ref[:, lane] + recharge_gain * (
-            moved[:, :LANES] + moved[:, LANES:]
-        )
-    put_sides(source_ref[...], left_ref, right_ref, 0)
-    up_ref[:EDGE, :] = source_ref[:EDGE, :]
-    down_ref[:EDGE, :] = source_ref[rows - EDGE :, :]
-    for i, ref in enumerate((left_ref, right_ref, up_ref, down_ref)):
-        ref[EDGE:, :] = take(3 + i)[...]
-
-
-def source_of(back, place, initial, edges, peers, cap, after):
-    rows, cols = initial.shape
-    blocks = place.shape[0]
+        flow = recharge_gain * (moved[:, :LANES] + moved[:, LANES:])
+        flow_ref[:, part * LANES : (part + 1) * LANES] = flow
+        if part == 0:
+            left_ref[:EDGE, :] = jnp.transpose(flow)[:EDGE, :]
+    right_ref[:EDGE, :] = jnp.transpose(flow)[LANES - EDGE :, :]
+    up_ref[:EDGE, :] = flow_ref[:EDGE, :]
+    down_ref[:EDGE, :] = flow_ref[rows - EDGE :, :]
+
+
+def source_of(back, place, edges, peers, cap, after):
+    rows, cols = edges[0].shape[1], edges[2].shape[1]
+    blocks = place.shape[1]
     side, line = floats(4 * EDGE, rows), floats(4 * EDGE, cols)
 
     def body(*refs):
@@ -447,38 +461,43 @@
     return staged(
         body,
         "tile_source",
-        (back, place, initial) + tuple(edges),
+        (back, place) + tuple(edges),
         (floats(rows, cols), side, side, line, line),
         [pltpu.VMEM((peers * cap, 2 * LANES), BF16), pltpu.VMEM((blocks, peers * cap), BF16)],
         4,
         after,
-        held=(0,),
+        held=(0, 2, 3, 4, 5),
         left=range(5),
     )
 
 
 def derive_kernel(take, outs, give):
-    initial_ref, left_ref, right_ref, up_ref, down_ref, transmit_ref = outs
+    initial_ref, left_ref, right_ref, up_ref, down_ref, transmit_ref, share_ref = outs
     rows = initial_ref.shape[0]
     head = take(0)[...]
     share = take(2)[...].astype(F32)
     initial = head * share
     initial_ref[...] = initial
+    share_ref[...] = share
     transmit = take(1)[...] * (1.0 + 0.5 * jnp.tanh(head))
     transmit_ref[...] = transmit
     for at, x in enumerate((initial, transmit, share)):
         put_sides(x, left_ref, right_ref, at * EDGE)
         up_ref[at * EDGE : (at + 1) * EDGE, :] = x[:EDGE, :]
         down_ref[at * EDGE : (at + 1) * EDGE, :] = x[rows - EDGE :, :]
-    for i in range(6):
-        give(i)
 
 
 def derive(head, trans_coef, land):
     rows, cols = head.shape
     tile, side, line = floats(rows, cols), floats(3 * EDGE, rows), floats(3 * EDGE, cols)
     return staged(
-        derive_kernel, "derive_tile", (head, trans_coef, land), (tile, side, side, line, line, tile), [], 3
+        derive_kernel,
+        "derive_tile",
+        (head, trans_coef, land),
+        (tile, side, side, line, line, tile, tile),
+        [],
+        2,
+        left=range(7),
     )
 
 
@@ -498,86 +517,111 @@
     return from_left, from_right, from_above, from_below
 
 
-def left_block(side):
-    return jnp.transpose(jnp.concatenate([jnp.zeros((LANES - EDGE, LANES), F32), side], axis=0))
-
-
-def right_block(side):
-    return jnp.transpose(jnp.concatenate([side, jnp.zeros((LANES - EDGE, LANES), F32)], axis=0))
-
-
-def put_edges(out_ref, rows, cols, sides, at):
-    from_left, from_right, from_above, from_below = sides
-    part = slice(at * EDGE, (at + 1) * EDGE)
-    bottom = slice(EDGE + rows, 2 * EDGE + rows)
-    right = slice(LANES + cols, 2 * LANES + cols)
-    mid = slice(LANES, LANES + cols)
-    out_ref[:EDGE, mid] = from_above[part, :cols]
-    out_ref[bottom, mid] = from_below[part, :cols]
-    for first in range(0, rows, LANES):
-        line = slice(EDGE + first, EDGE + first + LANES)
-        out_ref[line, :LANES] = left_block(from_left[part, first : first + LANES])
-        out_ref[line, right] = right_block(from_right[part, first : first + LANES])
-    out_ref[:EDGE, :LANES] = left_block(from_above[part, cols : cols + LANES])[LANES - EDGE :, :]
-    out_ref[:EDGE, right] = right_block(from_above[part, cols + LANES :])[LANES - EDGE :, :]
-    out_ref[bottom, :LANES] = left_block(from_below[part, cols : cols + LANES])[:EDGE, :]
-    out_ref[bottom, right] = right_block(from_below[part, cols + LANES :])[:EDGE, :]
-
-
-def shifted(x, by, axis):
-    return pltpu.roll(x, by % x.shape[axis], axis)
-
-
-def relax_kernel(take, outs, give, *ext_refs):
+def relax_kernel(take, outs, give, flow_ref, initial_ref, trans_ref, share_ref, next_ref, *weight_refs):
     (out_ref,) = outs
     rows, cols = out_ref.shape
-    height, width = ext_refs[0].shape
-    where = take(0)
-    sides = [take(5 + i) for i in range(4)]
-    for at in range(4):
-        put_edges(ext_refs[at], rows, cols, sides, at)
-    i = iota((height, width), 0)
-    j = iota((height, width), 1)
-    inside = (i >= where[0]) & (i < where[1]) & (j >= where[2]) & (j < where[3])
-
-    def extended(tile, at):
-        ext_refs[at][EDGE : EDGE + rows, LANES : LANES + cols] = tile
-        return jnp.where(inside, ext_refs[at][...], 0.0)
-
-    transmit = extended(take(1)[...], 2)
-    share = extended(take(2)[...].astype(F32), 3)
-    up = 0.5 * (transmit + shifted(transmit, 1, 0))
-    down = 0.5 * (transmit + shifted(transmit, -1, 0))
-    left = 0.5 * (transmit + shifted(transmit, 1, 1))
-    right = 0.5 * (transmit + shifted(transmit, -1, 1))
-    scale = share / (store_rate + (up + down + left + right))
-    up_ref, down_ref, left_ref, right_ref = ext_refs[4:]
-    up_ref[...] = up * scale
-    down_ref[...] = down * scale
-    left_ref[...] = left * scale
-    right_ref[...] = right * scale
-    surface = extended(take(3)[...], 1)
-    forced = scale * extended(take(4)[...], 0)
-    for _ in range(SWEEPS):
-        inflow = up_ref[...] * shifted(surface, 1, 0) + down_ref[...] * shifted(surface, -1, 0)
-        inflow = inflow + left_ref[...] * shifted(surface, 1, 1) + right_ref[...] * shifted(surface, -1, 1)
-        surface = forced + inflow
-    out_ref[...] = surface[EDGE : EDGE + rows, LANES : LANES + cols]
-    give(0)
-
-
-def relax(where, transmit, land, initial, source, sides):
-    rows, cols = source.shape
-    ext = (rows + 2 * EDGE, cols + 2 * LANES)
+    count = cols // LANES
+    top, height = PAD, rows + 2 * EDGE
+    one, flags = take(0)[0], take(1)
+    ok_above, ok_below, ok_left, ok_right = [flags[i] for i in range(4)]
+    from_left, from_right, from_above, from_below = [take(6 + i) for i in range(4)]
+    fields = (flow_ref, initial_ref, trans_ref, share_ref)
+    lane = iota((LANES, LANES), 1)
+
+    def beside(left, right):
+        many = len(fields) * EDGE
+        fill = jnp.zeros((LANES - 2 * many, LANES), F32)
+        block = jnp.transpose(jnp.concatenate([left, right, fill], axis=0))
+        out = []
+        for at in range(len(fields)):
+            on_left = pltpu.roll(block, (LANES - EDGE - at * EDGE) % LANES, 1) * ok_left
+            on_right = pltpu.roll(block, (-many - at * EDGE) % LANES, 1) * ok_right
+            out.append(jnp.where(lane < EDGE, on_right, jnp.where(lane >= LANES - EDGE, on_left, 0.0)))
+        return out
+
+    first_row, last_row = top + EDGE, top + EDGE + rows
+    for first in range(0, rows, LANES):
+        blocks = beside(from_left[:, first : first + LANES], from_right[:, first : first + LANES])
+        for ref, block in zip(fields, blocks):
+            ref[count, first_row + first : first_row + first + LANES, :] = block
+    above = beside(from_above[:, cols : cols + LANES], from_above[:, cols + LANES :])
+    below = beside(from_below[:, cols : cols + LANES], from_below[:, cols + LANES :])
+    empty = jnp.zeros((PAD, LANES), F32)
+    for at, ref in enumerate(fields):
+        part = slice(at * EDGE, (at + 1) * EDGE)
+        ref[count, top:first_row, :] = above[at][LANES - EDGE :, :] * ok_above
+        ref[count, last_row : last_row + EDGE, :] = below[at][:EDGE, :] * ok_below
+        for b in range(count):
+            ref[b, top:first_row, :] = from_above[part, b * LANES : (b + 1) * LANES] * ok_above
+            ref[b, last_row : last_row + EDGE, :] = from_below[part, b * LANES : (b + 1) * LANES] * ok_below
+        for b in range(count + 1):
+            ref[b, :top, :] = empty
+            ref[b, last_row + EDGE :, :] = empty
+    for b in range(count + 1):
+        next_ref[b, :top, :] = empty
+        next_ref[b, last_row + EDGE :, :] = empty
+    for ref, tile in ((flow_ref, take(5)), (trans_ref, take(2)), (share_ref, take(3)), (initial_ref, take(4))):
+        for b in range(count):
+            ref[b, first_row:last_row, :] = tile[:, b * LANES : (b + 1) * LANES].astype(F32)
+
+    edge = iota((height, LANES), 1)
+
+    def around(ref):
+        mid = [ref[b, top : top + height, :] for b in range(count + 1)]
+        later = [pltpu.roll(x, 1, 1) for x in mid]
+        sooner = [pltpu.roll(x, LANES - 1, 1) for x in mid]
+        for b in range(count + 1):
+            yield (
+                mid[b],
+                ref[b, pl.ds(top - one, height), :],
+                ref[b, pl.ds(top + one, height), :],
+                jnp.where(edge == 0, later[b - 1], later[b]),
+                jnp.where(edge == LANES - 1, sooner[(b + 1) % (count + 1)], sooner[b]),
+            )
+
+    up_ref, down_ref, left_ref, right_ref = weight_refs
+    line = slice(top, top + height)
+    for b, (mid, *others) in enumerate(around(trans_ref)):
+        sums = [mid + x for x in others]
+        total = 0.5 * (sums[0] + sums[1] + sums[2] + sums[3])
+        scale = share_ref[b, line, :] / (store_rate + total)
+        half = 0.5 * scale
+        for ref, x in zip(weight_refs, sums):
+            ref[b] = half * x
+        flow_ref[b, line, :] = scale * (store_rate * initial_ref[b, line, :] + flow_ref[b, line, :])
+    now, later_ref = initial_ref, next_ref
+    for sweep in range(SWEEPS):
+        for b, (_, above, below, on_left, on_right) in enumerate(around(now)):
+            if sweep == SWEEPS - 1 and b == count:
+                continue
+            inflow = up_ref[b] * above + down_ref[b] * below
+            inflow = inflow + left_ref[b] * on_left + right_ref[b] * on_right
+            surface = flow_ref[b, line, :] + inflow
+            if sweep == SWEEPS - 1:
+                out_ref[:, b * LANES : (b + 1) * LANES] = surface[EDGE : EDGE + rows, :]
+                give(0, b)
+            else:
+                later_ref[b, line, :] = surface
+        now, later_ref = later_ref, now
+
+
+def relax(flags, transmit, land_share, initial, flow, sides):
+    rows, cols = flow.shape
+    many = cols // LANES + 1
+    field = pltpu.VMEM((many, rows + 2 * (EDGE + PAD), LANES), F32)
+    weight = pltpu.VMEM((many, rows + 2 * EDGE, LANES), F32)
+    one = jnp.where(flags[:1] < 2.0, 1, 0).astype(jnp.int32)
     return staged(
         relax_kernel,
         "lateral_relax",
-        (where, transmit, land, initial, source) + tuple(sides),
+        (one, flags, transmit, land_share, initial, flow) + tuple(sides),
         (floats(rows, cols),),
-        [pltpu.VMEM(ext, F32)] * 8,
+        [field] * 5 + [weight] * 4,
         6,
-        held=range(4, 9),
-        in_smem=(0,),
+        held=range(2, 10),
+        in_smem=(0, 1),
+        pieces=(cols // LANES,),
+        by_lanes=True,
     )[0]
 
 
@@ -596,26 +640,19 @@
     got = lax.all_to_all(sent.reshape(peers, 1, wide), axes, split_axis=0, concat_axis=0, tiled=True)
     got = got.reshape(peers * (2 * cap + 1), LANES)
 
-    initial, left, right, up, down, transmit = derive(head, trans_coef, land)
-    responses = response(moist2, ksat, layers, 0, 1, (left,))
+    initial, left, right, up, down, transmit, land_share = derive(head, trans_coef, land)
+    responses = response(moist2, ksat, layers)
     row_at, col_at = lax.axis_index("row"), lax.axis_index("col")
-    where = jnp.stack(
-        [
-            jnp.where(row_at == 0, EDGE, 0),
-            jnp.where(row_at == row_count - 1, EDGE + rows, 2 * EDGE + rows),
-            jnp.where(col_at == 0, LANES, 0),
-            jnp.where(col_at == col_count - 1, LANES + cols, 2 * LANES + cols),
-        ]
-    ).astype(jnp.int32)
-
-    infil, share, answer = owner_side(got, responses, peers, cap, ())
+    flags = jnp.stack([row_at > 0, row_at < row_count - 1, col_at > 0, col_at < col_count - 1]).astype(F32)
+
+    infil, share, answer = owner_side(got, responses, peers, cap, (up,))
     back = lax.all_to_all(answer.reshape(peers, cap, LANES), axes, split_axis=0, concat_axis=0, tiled=True)
     back = back.reshape(peers * cap, LANES)
     saturation = saturate(moist2, ksat, infil, share, layers)
 
-    source, *edges = source_of(back, place, initial, (left, right, up, down), peers, cap, (saturation,))
+    flow, *edges = source_of(back, place, (left, right, up, down), peers, cap, (saturation,))
     left, right, up, down = edges
-    surface = relax(where, transmit, land, initial, source, exchange(up, down, left, right))
+    surface = relax(flags, transmit, land_share, initial, flow, exchange(up, down, left, right))
     return (saturation.reshape(owned, layers, LANES), surface)
 
 

time: 102 us -> 98.1 us (0.962)
  Pallas kernels: 55.6 us -> 45.9 us
  waiting for transfers between devices: 19.8 us -> 24.4 us
    pallas_call x5, Pallas kernels: 24.6 us -> 19.7 us  [staged(): pl.pallas_call(kernel, out_shape=tuple((pltpu.VMEM(x.shape, x.dtype) if i...]
    pallas_call x1, Pallas kernels: 15.2 us -> 11.5 us  [response(): pl.pallas_call(kernel, grid=(owned // size,), out_shape=(pltpu.HBM((owned...]
    all_to_all x1, waiting for transfers between devices: 12.5 us -> 16.2 us  [on_device(): lax.all_to_all(sent.reshape(peers, 1, wide), axes, split_axis=0, concat_a...]
  transfers between devices with their start and end apart: 6 -> 6, of which waited for: 4 -> 4; matrix products, arithmetic and copies ran while one was open for 0% -> 0% of each run, Pallas kernels for 33% -> 29%
where the time goes in v2:
time: 98.1 us; the launch traced here: 96.5 us
  Pallas kernels  45.9 us (47%)
  starting transfers between devices  24.4 us (25%)
  waiting for transfers between devices  24.4 us (25%)
    pallas_call x5, Pallas kernels, staged(): pl.pallas_call(kernel, out_shape=tuple((pltpu.VMEM(x.shape, x.dtype) if i...  19.7 us
    all_to_all x1, waiting for transfers between devices, on_device(): lax.all_to_all(sent.reshape(peers, 1, wide), axes, split_axis=0, concat_a...  16.2 us
    pallas_call x1, Pallas kernels, saturate(): pl.pallas_call(kernel, grid=(owned // size,), out_shape=pltpu.HBM((owned...  14.7 us
    pallas_call x1, Pallas kernels, response(): pl.pallas_call(kernel, grid=(owned // size,), out_shape=(pltpu.HBM((owned...  11.5 us
    all_to_all x1, starting transfers between devices, on_device(): lax.all_to_all(sent.reshape(peers, 1, wide), axes, split_axis=0, concat_a...  11.1 us
    all_to_all x1, starting transfers between devices, on_device(): lax.all_to_all(answer.reshape(peers, cap, LANES), axes, split_axis=0, con...  4.83 us
    ppermute x1, starting transfers between devices, exchange(): from_right = lax.ppermute(left_side, 'col', ring('col', -1))  4.63 us
    all_to_all x1, waiting for transfers between devices, on_device(): lax.all_to_all(answer.reshape(peers, cap, LANES), axes, split_axis=0, con...  4.14 us
  transfers between devices with their start and end apart: 6, of which 4 were waited for; matrix products, arithmetic and copies ran while one was open for 0% of the time, Pallas kernels for 29%

profile of v2, /device:TPU:0, one launch (start us, length us, event | category | flops | bytes accessed | tf_op | source)
XLA Modules:
  0.0 96.5 jit_solution(15945661753470381747)
XLA Ops:
  0.6 4.7 %pack_forcing.1 = (f32[4224,128]{1,0:T(8,128)}, s32[1,1024]{1,0:T(1,128)}) custom-call(s32[4,256]{1,0:T(4,128)} %bitcast.20, f32[256,512]{1,0:T(8,128)} %refs_1_.4, f32[256,512]{1,0:T(8,128)} %refs_0_.1, s32[256,512]{1,0:T(8,128)} %refs_2_.3), custom_call_target="tpu_custom_call" | custom-call | bytes 15000000 | tf_op jit(solution)/shard_map/pack_forcing/pallas_call | solution.py:94
  5.3 11.1 %all-to-all-start = ((f32[128,1,4224]{2,1,0:T(1,128)}), f32[128,1,4224]{2,1,0:T(1,128)S(1)}, u32[]{:S(2)}, u32[]{:S(2)}) async-start(f32[128,1,4224]{2,1,0:T(1,128)} %bitcast.18), calls=%async_computation | async-start | bytes 4325376 | tf_op jit(solution)/shard_map/all_to_all | solution.py:640
  16.5 1.8 %derive_tile.1 = (f32[256,512]{1,0:T(8,128)S(1)}, f32[24,256]{1,0:T(8,128)S(1)}, f32[24,256]{1,0:T(8,128)S(1)}, f32[24,512]{1,0:T(8,128)S(1)}, f32[24,512]{1,0:T...) custom-call(f32[256,512]{1,0:T(8,128)} %refs_0_.1, f32[256,512]{1,0:T(8,128)} %refs_1_.6, s32[256,512]{1,0:T(8,128)} %refs_2_.3), custom_call_target="tpu_custom_call" | custom-call | bytes 6000000 | tf_op jit(solution)/shard_map/derive_tile/pallas_call | solution.py:94
  18.3 0.0 copy-start
  18.3 0.8 copy-done
  19.1 11.5 %column_response.1 = (f32[1024,128]{1,0:T(8,128)}, f32[1024,128]{1,0:T(8,128)}, f32[1024,128]{1,0:T(8,128)}) custom-call(f32[16384,128]{1,0:T(8,128)} %bitcast.15, f32[1024,128]{1,0:T(8,128)} %refs_1_.7), custom_call_target="tpu_custom_call" | custom-call | bytes 39000000 | tf_op jit(solution)/shard_map/column_response/pallas_call | solution.py:275
  30.6 16.2 %all-to-all-done = f32[128,1,4224]{2,1,0:T(1,128)S(1)} async-done(((f32[128,1,4224]{2,1,0:T(1,128)}), f32[128,1,4224]{2,1,0:T(1,128)S(1)}, u32[]{:S(2)}, u32[]{:S(2)}) %all-to-all-start) | async-done | bytes 2162720 | tf_op jit(solution)/shard_map/all_to_all | solution.py:640
  46.8 6.1 %owner_side.1 = (f32[1024,128]{1,0:T(8,128)}, f32[1024,128]{1,0:T(8,128)}, f32[2048,128]{1,0:T(8,128)}) custom-call(f32[4224,128]{1,0:T(8,128)S(1)} %bitcast.12, f32[1024,128]{1,0:T(8,128)} %get-tuple-element.23.refs_1_, f32[1024,128]{1,0:T(8,128)} %get-tuple-element.24.refs_2_, f32[1024,128]{1,0:T(8,128)} %get-tuple-element.25.refs_3_, ...), custom_call_target="tpu_custom_call" | custom-call | bytes 24000000 | tf_op jit(solution)/shard_map/owner_side/pallas_call | solution.py:94
  52.9 4.8 %all-to-all-start.1 = ((f32[128,16,128]{2,1,0:T(8,128)}), f32[128,16,128]{2,1,0:T(8,128)S(1)}, u32[]{:S(2)}, u32[]{:S(2)}) async-start(f32[128,16,128]{2,1,0:T(8,128)} %bitcast.19), calls=%async_computation.1 | async-start | bytes 2097152 | tf_op jit(solution)/shard_map/all_to_all | solution.py:649
  57.8 14.7 %column_saturation.1.refs_6_ = f32[16384,128]{1,0:T(8,128)} custom-call(f32[16384,128]{1,0:T(8,128)} %bitcast.16, f32[1024,128]{1,0:T(8,128)} %refs_1_.7, f32[1024,128]{1,0:T(8,128)} %get-tuple-element.27.refs_2_, f32[1024,128]{1,0:T(8,128)} %get-tuple-element.28.refs_3_), custom_call_target="tpu_custom_call" | custom-call | bytes 42000000 | tf_op jit(solution)/shard_map/column_saturation/pallas_call | solution.py:318
  72.5 0.0 copy-start.1
  72.5 4.1 %all-to-all-done.1 = f32[128,16,128]{2,1,0:T(8,128)S(1)} async-done(((f32[128,16,128]{2,1,0:T(8,128)}), f32[128,16,128]{2,1,0:T(8,128)S(1)}, u32[]{:S(2)}, u32[]{:S(2)}) %all-to-all-start.1) | async-done | bytes 1048608 | tf_op jit(solution)/shard_map/all_to_all | solution.py:649
  76.6 2.5 %tile_source.1 = (f32[256,512]{1,0:T(8,128)S(1)}, f32[32,256]{1,0:T(8,128)S(1)}, f32[32,256]{1,0:T(8,128)S(1)}, f32[32,512]{1,0:T(8,128)S(1)}, f32[32,512]{1,0:T(8,128)S(1)}) custom-call(f32[2048,128]{1,0:T(8,128)S(1)} %bitcast.13, s32[1,1024]{1,0:T(1,128)} %get-tuple-element.33.refs_1_, f32[24,256]{1,0:T(8,128)S(1)} %get-tuple-element.34.refs_2_, ...), custom_call_target="tpu_custom_call" | custom-call | bytes 12000000 | tf_op jit(solution)/shard_map/tile_source/pallas_call | solution.py:94
  79.1 0.8 collective-permute-start
  79.9 4.6 %collective-permute-start.1 = (f32[32,256]{1,0:T(8,128)S(1)}, f32[32,256]{1,0:T(8,128)S(1)}, u32[]{:S(2)}, u32[]{:S(2)}) collective-permute-start(f32[32,256]{1,0:T(8,128)S(1)} %get-tuple-element.39), channel_id=1, source_target_pairs={{0,15},{1,0},{2,1},{3,2},{4,3},{5,4},{6,5},{7,6},{8,7},{9,8},{10,9... | collective-permute-start | bytes 98312 | tf_op jit(solution)/shard_map/ppermute | solution.py:512
  84.5 1.9 %collective-permute-done.refs_6_ = f32[32,256]{1,0:T(8,128)S(1)} collective-permute-done((f32[32,256]{1,0:T(8,128)S(1)}, f32[32,256]{1,0:T(8,128)S(1)}, u32[]{:S(2)}, u32[]{:S(2)}) %collective-permute-start) | collective-permute-done | bytes 32800 | tf_op jit(solution)/shard_map/ppermute | solution.py:511
  86.4 0.0 collective-permute-done.1.refs_7_
  86.5 0.0 collective-permute-start.2
  86.5 2.9 %collective-permute-start.3 = (f32[32,768]{1,0:T(8,128)S(1)}, f32[32,768]{1,0:T(8,128)S(1)}, u32[]{:S(2)}, u32[]{:S(2)}) collective-permute-start(f32[32,768]{1,0:T(8,128)S(1)} %pad_maximum_fusion.1), channel_id=1, source_target_pairs={{0,112},{16,0},{32,16},{48,32},{64,48},{80,64},{96,80},{112,96},{1... | collective-permute-start | bytes 294920 | tf_op jit(solution)/shard_map/ppermute | solution.py:516
  89.5 0.1 add_convert_fusion.refs_1_
  89.6 2.1 %collective-permute-done.2.refs_8_ = f32[32,768]{1,0:T(8,128)S(1)} collective-permute-done((f32[32,768]{1,0:T(8,128)S(1)}, f32[32,768]{1,0:T(8,128)S(1)}, u32[]{:S(2)}, u32[]{:S(2)}) %collective-permute-start.2) | collective-permute-done | bytes 98336 | tf_op jit(solution)/shard_map/ppermute | solution.py:515
  91.7 0.0 collective-permute-done.3.refs_9_
  91.7 0.0 copy-done.1
  91.7 4.6 %lateral_relax.1 = f32[256,512]{1,0:T(8,128)} custom-call(s32[1]{0:T(128)S(6)} %select_n.4.refs_0_, f32[4]{0:T(128)S(1)} %add_convert_fusion.refs_1_, f32[256,512]{1,0:T(8,128)S(1)} %get-tuple-element.29.refs_2_, f32[256,512]{1,0:T(8,128)S(1)} %copy-done.1, f32[256,512]{1,0:T(8,128)S(1)} %get-tuple-element.31.refs_4_, ...), custom_call_target="tpu_custom_call" | custom-call | bytes 18000000 | tf_op jit(solution)/shard_map/lateral_relax/pallas_call | solution.py:94
  (4 shorter events, 0.0 us)
Async XLA Ops:
  5.3 41.5 %all-to-all-start = ((f32[128,1,4224]{2,1,0:T(1,128)}), f32[128,1,4224]{2,1,0:T(1,128)S(1)}, u32[]{:S(2)}, u32[]{:S(2)}) async-start(f32[128,1,4224]{2,1,0:T(1,128)} %bitcast.18), calls=%async_computation | async-start | bytes 4325376 | tf_op jit(solution)/shard_map/all_to_all | solution.py:640
  18.3 0.8 copy-start
  52.9 23.7 %all-to-all-start.1 = ((f32[128,16,128]{2,1,0:T(8,128)}), f32[128,16,128]{2,1,0:T(8,128)S(1)}, u32[]{:S(2)}, u32[]{:S(2)}) async-start(f32[128,16,128]{2,1,0:T(8,128)} %bitcast.19), calls=%async_computation.1 | async-start | bytes 2097152 | tf_op jit(solution)/shard_map/all_to_all | solution.py:649
  72.5 19.2 %copy-start.1 = (f32[256,512]{1,0:T(8,128)S(1)}, f32[256,512]{1,0:T(8,128)}, u32[]{:S(2)}) copy-start(f32[256,512]{1,0:T(8,128)} %copy-done) | copy-start | bytes 1572868
  79.1 7.3 %collective-permute-start = (f32[32,256]{1,0:T(8,128)S(1)}, f32[32,256]{1,0:T(8,128)S(1)}, u32[]{:S(2)}, u32[]{:S(2)}) collective-permute-start(f32[32,256]{1,0:T(8,128)S(1)} %get-tuple-element.38), channel_id=1, source_target_pairs={{0,1},{1,2},{2,3},{3,4},{4,5},{5,6},{6,7},{7,8},{8,9},{9,10},{10,1... | collective-permute-start | bytes 98312 | tf_op jit(solution)/shard_map/ppermute | solution.py:511
  79.9 6.5 %collective-permute-start.1 = (f32[32,256]{1,0:T(8,128)S(1)}, f32[32,256]{1,0:T(8,128)S(1)}, u32[]{:S(2)}, u32[]{:S(2)}) collective-permute-start(f32[32,256]{1,0:T(8,128)S(1)} %get-tuple-element.39), channel_id=1, source_target_pairs={{0,15},{1,0},{2,1},{3,2},{4,3},{5,4},{6,5},{7,6},{8,7},{9,8},{10,9... | collective-permute-start | bytes 98312 | tf_op jit(solution)/shard_map/ppermute | solution.py:512
  86.5 5.3 %collective-permute-start.2 = (f32[32,768]{1,0:T(8,128)S(1)}, f32[32,768]{1,0:T(8,128)S(1)}, u32[]{:S(2)}, u32[]{:S(2)}) collective-permute-start(f32[32,768]{1,0:T(8,128)S(1)} %pad_maximum_fusion), channel_id=1, source_target_pairs={{0,16},{16,32},{32,48},{48,64},{64,80},{80,96},{96,112},{112,0},{1... | collective-permute-start | bytes 294920 | tf_op jit(solution)/shard_map/ppermute | solution.py:515
  86.5 5.2 %collective-permute-start.3 = (f32[32,768]{1,0:T(8,128)S(1)}, f32[32,768]{1,0:T(8,128)S(1)}, u32[]{:S(2)}, u32[]{:S(2)}) collective-permute-start(f32[32,768]{1,0:T(8,128)S(1)} %pad_maximum_fusion.1), channel_id=1, source_target_pairs={{0,112},{16,0},{32,16},{48,32},{64,48},{80,64},{96,80},{112,96},{1... | collective-permute-start | bytes 294920 | tf_op jit(solution)/shard_map/ppermute | solution.py:516

commit v3 on v2

--- a/solution.py
+++ b/solution.py
@@ -10,6 +10,7 @@
 SWEEPS = 4
 LANES = 128
 EDGE = 8
+WIDE = 4
 PAD = 8
 GROUPS = 4
 
@@ -135,7 +136,6 @@
     rank = jnp.concatenate(ranks, axis=1).astype(jnp.int32)
     place = owner + peers * rank
     place_ref[...] = place
-    give(1)
     owner_f = owner_hot.astype(F32)
     rank_hot = (rank == iota((LANES, blocks), 0)).astype(F32).astype(BF16)
     contract = (((1,), (1,)), ((), ()))
@@ -189,6 +189,7 @@
         [pltpu.VMEM((peers * cap, blocks), BF16), pltpu.VMEM((blocks, 4 * LANES), BF16)],
         5,
         pieces=(GROUPS, 1),
+        left=(1,),
     )
 
 
@@ -412,25 +413,16 @@
     )
 
 
-def put_sides(x, left_ref, right_ref, at):
-    cols = x.shape[1]
-    left_ref[at : at + EDGE, :] = jnp.transpose(x[:, :LANES])[:EDGE, :]
-    right_ref[at : at + EDGE, :] = jnp.transpose(x[:, cols - LANES :])[LANES - EDGE :, :]
-
-
-def source_kernel(peers, cap, take, outs, give, data_ref, hot_ref):
-    flow_ref, left_ref, right_ref, up_ref, down_ref = outs
-    rows, cols = flow_ref.shape
-    blocks = rows * cols // LANES
-    back_ref = take(0)
-    for k in range(cap):
-        line = slice(k * peers, (k + 1) * peers)
-        high, low = halves(back_ref[pl.ds(k, peers, stride=cap), :])
-        data_ref[line, :LANES] = high
-        data_ref[line, LANES:] = low
-    place_f = take(1)[...].astype(F32)
-    for i, ref in enumerate((left_ref, right_ref, up_ref, down_ref)):
-        ref[EDGE:, :] = take(2 + i)[...]
+def ordered(even, low, high):
+    odd = 1.0 - even
+    return even * high + odd * low, even * low + odd * high
+
+
+def sides_of(first, last, even):
+    return ordered(even, jnp.transpose(first)[:WIDE, :], jnp.transpose(last)[LANES - WIDE :, :])
+
+
+def unpack(place_f, data_ref, hot_ref, blocks, peers, cap):
     eye = iota((LANES, LANES), 0) == iota((LANES, LANES), 1)
     for first in range(0, blocks, LANES):
         column = jnp.sum(jnp.where(eye, place_f[:, first : first + LANES], 0.0), axis=1, keepdims=True)
@@ -439,82 +431,135 @@
             hot_ref[first : first + LANES, k * peers : (k + 1) * peers] = (
                 (column == iota((LANES, peers), 1) + k * peers).astype(F32).astype(BF16)
             )
-    for part in range(cols // LANES):
-        moved = jnp.dot(hot_ref[part * rows : (part + 1) * rows, :], data_ref[...], preferred_element_type=F32)
-        flow = recharge_gain * (moved[:, :LANES] + moved[:, LANES:])
-        flow_ref[:, part * LANES : (part + 1) * LANES] = flow
-        if part == 0:
-            left_ref[:EDGE, :] = jnp.transpose(flow)[:EDGE, :]
-    right_ref[:EDGE, :] = jnp.transpose(flow)[LANES - EDGE :, :]
-    up_ref[:EDGE, :] = flow_ref[:EDGE, :]
-    down_ref[:EDGE, :] = flow_ref[rows - EDGE :, :]
-
-
-def source_of(back, place, edges, peers, cap, after):
-    rows, cols = edges[0].shape[1], edges[2].shape[1]
-    blocks = place.shape[1]
-    side, line = floats(4 * EDGE, rows), floats(4 * EDGE, cols)
+    moved = jnp.dot(hot_ref[:blocks, :], data_ref[...], preferred_element_type=F32)
+    return recharge_gain * (moved[:, :LANES] + moved[:, LANES:])
+
+
+def outer_kernel(peers, cap, rows, cols, take, outs, give, hot_ref):
+    first_ref, last_ref, data_ref, *edge_refs = outs
+    back_ref = take(0)
+    for k in range(cap):
+        line = slice(k * peers, (k + 1) * peers)
+        high, low = halves(back_ref[pl.ds(k, peers, stride=cap), :])
+        data_ref[line, :LANES] = high
+        data_ref[line, LANES:] = low
+    place_f = take(1)[...].astype(F32)
+    flags = take(4)
+    last_at = rows * (cols // LANES - 1)
+    first = unpack(place_f[:, :rows], data_ref, hot_ref.at[:rows], rows, peers, cap)
+    last = unpack(place_f[:, last_at:], data_ref, hot_ref.at[rows:], rows, peers, cap)
+    first_ref[...] = first
+    last_ref[...] = last
+    for ref, raw, x in zip(edge_refs, (take(2), take(3)), sides_of(first, last, flags[4])):
+        ref[...] = jnp.concatenate([x, raw[...]], axis=0)
+
+
+def inner_kernel(peers, cap, take, outs, give, hot_ref):
+    flow_ref, *edge_refs = outs
+    rows, cols = flow_ref.shape
+    first_ref, last_ref, data_ref = take(0), take(1), take(2)
+    flags = take(6)
+    flow_ref[:, :LANES] = first_ref[...]
+    flow_ref[:, cols - LANES :] = last_ref[...]
+    place_f = take(3)[...].astype(F32)
+    for part in range(1, cols // LANES - 1):
+        at = (part - 1) * rows
+        flow_ref[:, part * LANES : (part + 1) * LANES] = unpack(
+            place_f[:, part * rows : (part + 1) * rows], data_ref, hot_ref.at[at : at + rows], rows, peers, cap
+        )
+    lines = ordered(flags[5], flow_ref[:WIDE, :], flow_ref[rows - WIDE :, :])
+    for ref, raw, x in zip(edge_refs, (take(4), take(5)), lines):
+        ref[...] = jnp.concatenate([x, raw[...]], axis=0)
+
+
+def outer_flow(back, place, sides, flags, cols, peers, cap, after):
+    rows = sides[0].shape[1]
+    block, side = floats(rows, LANES), floats(4 * WIDE, rows)
 
     def body(*refs):
-        source_kernel(peers, cap, *refs)
+        outer_kernel(peers, cap, rows, cols, *refs)
 
     return staged(
         body,
-        "tile_source",
-        (back, place) + tuple(edges),
-        (floats(rows, cols), side, side, line, line),
-        [pltpu.VMEM((peers * cap, 2 * LANES), BF16), pltpu.VMEM((blocks, peers * cap), BF16)],
-        4,
+        "outer_flow",
+        (back, place) + tuple(sides) + (flags,),
+        (block, block, jax.ShapeDtypeStruct((peers * cap, 2 * LANES), BF16), side, side),
+        [pltpu.VMEM((2 * rows, peers * cap), BF16)],
+        2,
         after,
-        held=(0, 2, 3, 4, 5),
+        held=(0, 1, 2, 3),
+        in_smem=(4,),
         left=range(5),
     )
 
 
+def inner_flow(first, last, data, place, lines, flags, peers, cap):
+    rows, cols = first.shape[0], lines[0].shape[1]
+    line = floats(4 * WIDE, cols)
+
+    def body(*refs):
+        inner_kernel(peers, cap, *refs)
+
+    return staged(
+        body,
+        "inner_flow",
+        (first, last, data, place) + tuple(lines) + (flags,),
+        (floats(rows, cols), line, line),
+        [pltpu.VMEM((rows * (cols // LANES - 2), peers * cap), BF16)],
+        2,
+        held=range(6),
+        in_smem=(6,),
+        left=range(3),
+    )
+
+
 def derive_kernel(take, outs, give):
-    initial_ref, left_ref, right_ref, up_ref, down_ref, transmit_ref, share_ref = outs
-    rows = initial_ref.shape[0]
+    initial_ref, transmit_ref, share_ref, *edge_refs = outs
+    rows, cols = initial_ref.shape
+    flags = take(3)
     head = take(0)[...]
     share = take(2)[...].astype(F32)
-    initial = head * share
-    initial_ref[...] = initial
+    initial_ref[...] = head * share
     share_ref[...] = share
-    transmit = take(1)[...] * (1.0 + 0.5 * jnp.tanh(head))
-    transmit_ref[...] = transmit
-    for at, x in enumerate((initial, transmit, share)):
-        put_sides(x, left_ref, right_ref, at * EDGE)
-        up_ref[at * EDGE : (at + 1) * EDGE, :] = x[:EDGE, :]
-        down_ref[at * EDGE : (at + 1) * EDGE, :] = x[rows - EDGE :, :]
-
-
-def derive(head, trans_coef, land):
+    transmit_ref[...] = take(1)[...] * (1.0 + 0.5 * jnp.tanh(head))
+    for at, x in enumerate((initial_ref, transmit_ref, share_ref)):
+        sent = sides_of(x[:, :LANES], x[:, cols - LANES :], flags[4])
+        sent = sent + ordered(flags[5], x[:WIDE, :], x[rows - WIDE :, :])
+        for ref, y in zip(edge_refs, sent):
+            ref[at * WIDE : (at + 1) * WIDE, :] = y
+
+
+def derive(head, trans_coef, land, flags):
     rows, cols = head.shape
-    tile, side, line = floats(rows, cols), floats(3 * EDGE, rows), floats(3 * EDGE, cols)
+    tile, side, line = floats(rows, cols), floats(3 * WIDE, rows), floats(3 * WIDE, cols)
     return staged(
         derive_kernel,
         "derive_tile",
-        (head, trans_coef, land),
-        (tile, side, side, line, line, tile, tile),
+        (head, trans_coef, land, flags),
+        (tile, tile, tile, side, side, line, line),
         [],
         2,
+        in_smem=(3,),
         left=range(7),
     )
 
 
-def exchange(up_line, down_line, left_side, right_side):
-    rows = left_side.shape[1]
-
-    def ring(axis, by):
-        count = lax.axis_size(axis)
-        return [(i, (i + by) % count) for i in range(count)]
-
-    from_left = lax.ppermute(right_side, "col", ring("col", 1))
-    from_right = lax.ppermute(left_side, "col", ring("col", -1))
-    down_send = jnp.concatenate([down_line, from_left[:, rows - LANES :], from_right[:, rows - LANES :]], axis=1)
-    up_send = jnp.concatenate([up_line, from_left[:, :LANES], from_right[:, :LANES]], axis=1)
-    from_above = lax.ppermute(down_send, "row", ring("row", 1))
-    from_below = lax.ppermute(up_send, "row", ring("row", -1))
-    return from_left, from_right, from_above, from_below
+def partners(axis):
+    count = lax.axis_size(axis)
+    return [(i, i ^ 1) for i in range(count)], [(i, (i + (1 if i % 2 else -1)) % count) for i in range(count)]
+
+
+def swap(sides, axis):
+    return tuple(lax.ppermute(x, axis, pairs) for x, pairs in zip(sides, partners(axis)))
+
+
+def with_corners(lines, got):
+    rows = got[0].shape[1]
+    even = lax.axis_index("row") % 2 == 0
+    ends = [(x[:, :LANES], x[:, rows - LANES :]) for x in got]
+    to_first = [jnp.where(even, bottom, top) for top, bottom in ends]
+    to_second = [jnp.where(even, top, bottom) for top, bottom in ends]
+    return jnp.concatenate([lines[0], *to_first], axis=1), jnp.concatenate([lines[1], *to_second], axis=1)
 
 
 def relax_kernel(take, outs, give, flow_ref, initial_ref, trans_ref, share_ref, next_ref, *weight_refs):
@@ -524,19 +569,20 @@
     top, height = PAD, rows + 2 * EDGE
     one, flags = take(0)[0], take(1)
     ok_above, ok_below, ok_left, ok_right = [flags[i] for i in range(4)]
-    from_left, from_right, from_above, from_below = [take(6 + i) for i in range(4)]
+    from_right, from_left = ordered(flags[4], take(7)[...], take(6)[...])
+    from_below, from_above = ordered(flags[5], take(9)[...], take(8)[...])
     fields = (flow_ref, initial_ref, trans_ref, share_ref)
     lane = iota((LANES, LANES), 1)
 
     def beside(left, right):
-        many = len(fields) * EDGE
+        many = len(fields) * WIDE
         fill = jnp.zeros((LANES - 2 * many, LANES), F32)
         block = jnp.transpose(jnp.concatenate([left, right, fill], axis=0))
         out = []
         for at in range(len(fields)):
-            on_left = pltpu.roll(block, (LANES - EDGE - at * EDGE) % LANES, 1) * ok_left
-            on_right = pltpu.roll(block, (-many - at * EDGE) % LANES, 1) * ok_right
-            out.append(jnp.where(lane < EDGE, on_right, jnp.where(lane >= LANES - EDGE, on_left, 0.0)))
+            on_left = pltpu.roll(block, (LANES - WIDE - at * WIDE) % LANES, 1) * ok_left
+            on_right = pltpu.roll(block, (-many - at * WIDE) % LANES, 1) * ok_right
+            out.append(jnp.where(lane < WIDE, on_right, jnp.where(lane >= LANES - WIDE, on_left, 0.0)))
         return out
 
     first_row, last_row = top + EDGE, top + EDGE + rows
@@ -544,22 +590,26 @@
         blocks = beside(from_left[:, first : first + LANES], from_right[:, first : first + LANES])
         for ref, block in zip(fields, blocks):
             ref[count, first_row + first : first_row + first + LANES, :] = block
-    above = beside(from_above[:, cols : cols + LANES], from_above[:, cols + LANES :])
-    below = beside(from_below[:, cols : cols + LANES], from_below[:, cols + LANES :])
-    empty = jnp.zeros((PAD, LANES), F32)
+    corners = []
+    for line in (from_above, from_below):
+        on_right, on_left = ordered(flags[4], line[:, cols + LANES :], line[:, cols : cols + LANES])
+        corners.append(beside(on_left, on_right))
+    above, below = corners
+    empty = jnp.zeros((PAD + EDGE, LANES), F32)
     for at, ref in enumerate(fields):
-        part = slice(at * EDGE, (at + 1) * EDGE)
-        ref[count, top:first_row, :] = above[at][LANES - EDGE :, :] * ok_above
-        ref[count, last_row : last_row + EDGE, :] = below[at][:EDGE, :] * ok_below
+        part = slice(at * WIDE, (at + 1) * WIDE)
+        for b in range(count + 1):
+            ref[b, :first_row, :] = empty
+            ref[b, last_row:, :] = empty
+        before, after = slice(first_row - WIDE, first_row), slice(last_row, last_row + WIDE)
+        ref[count, before, :] = above[at][LANES - WIDE :, :] * ok_above
+        ref[count, after, :] = below[at][:WIDE, :] * ok_below
         for b in range(count):
-            ref[b, top:first_row, :] = from_above[part, b * LANES : (b + 1) * LANES] * ok_above
-            ref[b, last_row : last_row + EDGE, :] = from_below[part, b * LANES : (b + 1) * LANES] * ok_below
-        for b in range(count + 1):
-            ref[b, :top, :] = empty
-            ref[b, last_row + EDGE :, :] = empty
+            ref[b, before, :] = from_above[part, b * LANES : (b + 1) * LANES] * ok_above
+            ref[b, after, :] = from_below[part, b * LANES : (b + 1) * LANES] * ok_below
     for b in range(count + 1):
-        next_ref[b, :top, :] = empty
-        next_ref[b, last_row + EDGE :, :] = empty
+        next_ref[b, :first_row, :] = empty
+        next_ref[b, last_row:, :] = empty
     for ref, tile in ((flow_ref, take(5)), (trans_ref, take(2)), (share_ref, take(3)), (initial_ref, take(4))):
         for b in range(count):
             ref[b, first_row:last_row, :] = tile[:, b * LANES : (b + 1) * LANES].astype(F32)
@@ -640,19 +690,22 @@
     got = lax.all_to_all(sent.reshape(peers, 1, wide), axes, split_axis=0, concat_axis=0, tiled=True)
     got = got.reshape(peers * (2 * cap + 1), LANES)
 
-    initial, left, right, up, down, transmit, land_share = derive(head, trans_coef, land)
+    row_at, col_at = lax.axis_index("row"), lax.axis_index("col")
+    flags = [row_at > 0, row_at < row_count - 1, col_at > 0, col_at < col_count - 1, col_at % 2 == 0, row_at % 2 == 0]
+    flags = jnp.stack(flags).astype(F32)
+    initial, transmit, land_share, *edges = derive(head, trans_coef, land, flags)
     responses = response(moist2, ksat, layers)
-    row_at, col_at = lax.axis_index("row"), lax.axis_index("col")
-    flags = jnp.stack([row_at > 0, row_at < row_count - 1, col_at > 0, col_at < col_count - 1]).astype(F32)
-
-    infil, share, answer = owner_side(got, responses, peers, cap, (up,))
+
+    infil, share, answer = owner_side(got, responses, peers, cap, (edges[0],))
     back = lax.all_to_all(answer.reshape(peers, cap, LANES), axes, split_axis=0, concat_axis=0, tiled=True)
     back = back.reshape(peers * cap, LANES)
     saturation = saturate(moist2, ksat, infil, share, layers)
 
-    flow, *edges = source_of(back, place, (left, right, up, down), peers, cap, (saturation,))
-    left, right, up, down = edges
-    surface = relax(flags, transmit, land_share, initial, flow, exchange(up, down, left, right))
+    first, last, data, *sides = outer_flow(back, place, edges[:2], flags, cols, peers, cap, (saturation,))
+    got_sides = swap(sides, "col")
+    flow, *lines = inner_flow(first, last, data, place, edges[2:], flags, peers, cap)
+    got_lines = swap(with_corners(lines, got_sides), "row")
+    surface = relax(flags, transmit, land_share, initial, flow, got_sides + got_lines)
     return (saturation.reshape(owned, layers, LANES), surface)
 
 

time: 98.1 us -> 97 us (0.989)
  starting transfers between devices: 24.4 us -> 18.6 us
  waiting for transfers between devices: 24.4 us -> 28.1 us
  Pallas kernels: 45.9 us -> 47.7 us
    ppermute x4, starting transfers between devices: 8.38 us -> 2.76 us  [swap(): lax.ppermute(x, axis, pairs)]
    ppermute x4, waiting for transfers between devices: 4.04 us -> 8.21 us  [swap(): lax.ppermute(x, axis, pairs)]
    pallas_call x5 -> x6, Pallas kernels: 19.7 us -> 21.5 us  [staged(): pl.pallas_call(kernel, out_shape=tuple((pltpu.VMEM(x.shape, x.dtype) if i...]
  transfers between devices with their start and end apart: 6 -> 6, of which waited for: 4 -> 5; matrix products, arithmetic and copies ran while one was open for 0% -> 0% of each run, Pallas kernels for 29% -> 31%
where the time goes in v3:
time: 97 us; the launch traced here: 96.2 us
  Pallas kernels  47.7 us (49%)
  waiting for transfers between devices  28.1 us (29%)
  starting transfers between devices  18.6 us (19%)
    pallas_call x6, Pallas kernels, staged(): pl.pallas_call(kernel, out_shape=tuple((pltpu.VMEM(x.shape, x.dtype) if i...  21.5 us
    all_to_all x1, waiting for transfers between devices, on_device(): lax.all_to_all(sent.reshape(peers, 1, wide), axes, split_axis=0, concat_a...  15.6 us
    pallas_call x1, Pallas kernels, saturate(): pl.pallas_call(kernel, grid=(owned // size,), out_shape=pltpu.HBM((owned...  14.7 us
    pallas_call x1, Pallas kernels, response(): pl.pallas_call(kernel, grid=(owned // size,), out_shape=(pltpu.HBM((owned...  11.5 us
    all_to_all x1, starting transfers between devices, on_device(): lax.all_to_all(sent.reshape(peers, 1, wide), axes, split_axis=0, concat_a...  11.1 us
    ppermute x4, waiting for transfers between devices, swap(): lax.ppermute(x, axis, pairs)  8.21 us
    all_to_all x1, starting transfers between devices, on_device(): lax.all_to_all(answer.reshape(peers, cap, LANES), axes, split_axis=0, con...  4.65 us
    all_to_all x1, waiting for transfers between devices, on_device(): lax.all_to_all(answer.reshape(peers, cap, LANES), axes, split_axis=0, con...  4.32 us
  transfers between devices with their start and end apart: 6, of which 5 were waited for; matrix products, arithmetic and copies ran while one was open for 0% of the time, Pallas kernels for 31%

profile of v3, /device:TPU:0, one launch (start us, length us, event | category | flops | bytes accessed | tf_op | source)
XLA Modules:
  0.0 96.2 jit_solution(4985018505631093455)
XLA Ops:
  0.6 4.7 %pack_forcing.1 = (f32[4224,128]{1,0:T(8,128)}, s32[1,1024]{1,0:T(1,128)S(1)}) custom-call(s32[4,256]{1,0:T(4,128)} %bitcast.22, f32[256,512]{1,0:T(8,128)} %refs_1_.4, f32[256,512]{1,0:T(8,128)} %refs_0_.1, s32[256,512]{1,0:T(8,128)} %refs_2_.3), custom_call_target="tpu_custom_call" | custom-call | bytes 15000000 | tf_op jit(solution)/shard_map/pack_forcing/pallas_call | solution.py:95
  5.3 11.1 %all-to-all-start = ((f32[128,1,4224]{2,1,0:T(1,128)}), f32[128,1,4224]{2,1,0:T(1,128)S(1)}, u32[]{:S(2)}, u32[]{:S(2)}) async-start(f32[128,1,4224]{2,1,0:T(1,128)} %bitcast.20), calls=%async_computation | async-start | bytes 4325376 | tf_op jit(solution)/shard_map/all_to_all | solution.py:690
  16.5 0.1 stack.27
  16.6 2.4 %derive_tile.1 = (f32[256,512]{1,0:T(8,128)S(1)}, f32[256,512]{1,0:T(8,128)S(1)}, f32[256,512]{1,0:T(8,128)S(1)}, f32[12,256]{1,0:T(8,128)S(1)}, f32[12,256]{1,0...) custom-call(f32[256,512]{1,0:T(8,128)} %refs_0_.1, f32[256,512]{1,0:T(8,128)} %refs_1_.6, ...), custom_call_target="tpu_custom_call" | custom-call | bytes 6000000 | tf_op jit(solution)/shard_map/derive_tile/pallas_call | solution.py:95
  19.0 0.0 copy-start
  19.0 0.8 copy-done
  19.8 11.5 %column_response.1 = (f32[1024,128]{1,0:T(8,128)}, f32[1024,128]{1,0:T(8,128)}, f32[1024,128]{1,0:T(8,128)}) custom-call(f32[16384,128]{1,0:T(8,128)} %bitcast.17, f32[1024,128]{1,0:T(8,128)} %refs_1_.7), custom_call_target="tpu_custom_call" | custom-call | bytes 39000000 | tf_op jit(solution)/shard_map/column_response/pallas_call | solution.py:276
  31.3 15.6 %all-to-all-done = f32[128,1,4224]{2,1,0:T(1,128)S(1)} async-done(((f32[128,1,4224]{2,1,0:T(1,128)}), f32[128,1,4224]{2,1,0:T(1,128)S(1)}, u32[]{:S(2)}, u32[]{:S(2)}) %all-to-all-start) | async-done | bytes 2162720 | tf_op jit(solution)/shard_map/all_to_all | solution.py:690
  46.8 6.1 %owner_side.1 = (f32[1024,128]{1,0:T(8,128)}, f32[1024,128]{1,0:T(8,128)}, f32[2048,128]{1,0:T(8,128)}) custom-call(f32[4224,128]{1,0:T(8,128)S(1)} %bitcast.14, f32[1024,128]{1,0:T(8,128)} %get-tuple-element.26.refs_1_, f32[1024,128]{1,0:T(8,128)} %get-tuple-element.27.refs_2_, f32[1024,128]{1,0:T(8,128)} %get-tuple-element.28.refs_3_, ...), custom_call_target="tpu_custom_call" | custom-call | bytes 24000000 | tf_op jit(solution)/shard_map/owner_side/pallas_call | solution.py:95
  53.0 4.6 %all-to-all-start.1 = ((f32[128,16,128]{2,1,0:T(8,128)}), f32[128,16,128]{2,1,0:T(8,128)S(1)}, u32[]{:S(2)}, u32[]{:S(2)}) async-start(f32[128,16,128]{2,1,0:T(8,128)} %bitcast.21), calls=%async_computation.1 | async-start | bytes 2097152 | tf_op jit(solution)/shard_map/all_to_all | solution.py:700
  57.6 14.7 %column_saturation.1.refs_5_ = f32[16384,128]{1,0:T(8,128)} custom-call(f32[16384,128]{1,0:T(8,128)} %bitcast.18, f32[1024,128]{1,0:T(8,128)} %refs_1_.7, f32[1024,128]{1,0:T(8,128)} %get-tuple-element.30.refs_2_, f32[1024,128]{1,0:T(8,128)} %get-tuple-element.31.refs_3_), custom_call_target="tpu_custom_call" | custom-call | bytes 42000000 | tf_op jit(solution)/shard_map/column_saturation/pallas_call | solution.py:319
  72.3 0.0 copy-start.1
  72.3 4.3 %all-to-all-done.1 = f32[128,16,128]{2,1,0:T(8,128)S(1)} async-done(((f32[128,16,128]{2,1,0:T(8,128)}), f32[128,16,128]{2,1,0:T(8,128)S(1)}, u32[]{:S(2)}, u32[]{:S(2)}) %all-to-all-start.1) | async-done | bytes 1048608 | tf_op jit(solution)/shard_map/all_to_all | solution.py:700
  76.7 2.1 %outer_flow.1 = (f32[256,128]{1,0:T(8,128)S(1)}, f32[256,128]{1,0:T(8,128)S(1)}, bf16[2048,256]{1,0:T(8,128)(2,1)S(1)}, f32[16,256]{1,0:T(8,128)S(1)}, f32[16,256]{1,0:T(8,128)S(1)}) custom-call(f32[2048,128]{1,0:T(8,128)S(1)} %bitcast.15, s32[1,1024]{1,0:T(1,128)S(1)} %get-tuple-element.36.refs_1_.refs_3_, f32[12,256]{1,0:T(8,128)S(1)} %get-tuple-element.29.refs_4_.refs_2_, ...), custom_call_target="tpu_custom_call" | custom-call | bytes 6000000 | tf_op jit(solution)/shard_map/outer_flow/pallas_call | solution.py:95
  78.8 0.8 collective-permute-start
  79.6 1.2 %collective-permute-start.1 = (f32[16,256]{1,0:T(8,128)S(1)}, f32[16,256]{1,0:T(8,128)S(1)}, u32[]{:S(2)}, u32[]{:S(2)}) collective-permute-start(f32[16,256]{1,0:T(8,128)S(1)} %get-tuple-element.45), channel_id=1, source_target_pairs={{0,15},{1,2},{2,1},{3,4},{4,3},{5,6},{6,5},{7,8},{8,7},{9,10},{10,... | collective-permute-start | bytes 49160 | tf_op jit(solution)/shard_map/ppermute | solution.py:553
  80.8 1.6 %inner_flow.1 = (f32[256,512]{1,0:T(8,128)S(1)}, f32[16,512]{1,0:T(8,128)S(1)}, f32[16,512]{1,0:T(8,128)S(1)}) custom-call(f32[256,128]{1,0:T(8,128)S(1)} %get-tuple-element.38.refs_0_, f32[256,128]{1,0:T(8,128)S(1)} %get-tuple-element.39.refs_1_, bf16[2048,256]{1,0:T(8,128)(2,1)S(1)} %get-tuple-element.40.refs_2_, ...), custom_call_target="tpu_custom_call" | custom-call | bytes 6000000 | tf_op jit(solution)/shard_map/inner_flow/pallas_call | solution.py:95
  82.4 0.2 collective-permute-done.refs_6_
  82.6 4.0 %collective-permute-done.1.refs_7_ = f32[16,256]{1,0:T(8,128)S(1)} collective-permute-done((f32[16,256]{1,0:T(8,128)S(1)}, f32[16,256]{1,0:T(8,128)S(1)}, u32[]{:S(2)}, u32[]{:S(2)}) %collective-permute-start.1) | collective-permute-done | bytes 16416 | tf_op jit(solution)/shard_map/ppermute | solution.py:553
  86.6 0.1 collective-permute-start.3
  86.8 0.7 collective-permute-start.2
  87.5 4.0 %collective-permute-done.3.refs_9_ = f32[16,768]{1,0:T(8,128)S(1)} collective-permute-done((f32[16,768]{1,0:T(8,128)S(1)}, f32[16,768]{1,0:T(8,128)S(1)}, u32[]{:S(2)}, u32[]{:S(2)}) %collective-permute-start.3) | collective-permute-done | bytes 49184 | tf_op jit(solution)/shard_map/ppermute | solution.py:553
  91.5 0.0 collective-permute-done.2.refs_8_
  91.5 0.0 copy-done.1
  91.5 4.6 %lateral_relax.1 = f32[256,512]{1,0:T(8,128)} custom-call(s32[1]{0:T(128)S(6)} %select_n.39.refs_0_, f32[6]{0:T(128)S(1)} %convert_element_type.3.refs_3_.refs_4_.refs_6_.refs_1_, f32[256,512]{1,0:T(8,128)S(1)} %get-tuple-element.32.refs_2_, f32[256,512]{1,0:T(8,128)S(1)} %copy-done.1, f32[256,512]{1,0:T(8,128)S(1)} %get-tuple-element.34.refs_4_, ...), custom_call_target="tpu_custom_call" | custom-call | bytes 18000000 | tf_op jit(solution)/shard_map/lateral_relax/pallas_call | solution.py:95
  (5 shorter events, 0.0 us)
Async XLA Ops:
  5.3 41.5 %all-to-all-start = ((f32[128,1,4224]{2,1,0:T(1,128)}), f32[128,1,4224]{2,1,0:T(1,128)S(1)}, u32[]{:S(2)}, u32[]{:S(2)}) async-start(f32[128,1,4224]{2,1,0:T(1,128)} %bitcast.20), calls=%async_computation | async-start | bytes 4325376 | tf_op jit(solution)/shard_map/all_to_all | solution.py:690
  19.0 0.8 copy-start
  53.0 23.7 %all-to-all-start.1 = ((f32[128,16,128]{2,1,0:T(8,128)}), f32[128,16,128]{2,1,0:T(8,128)S(1)}, u32[]{:S(2)}, u32[]{:S(2)}) async-start(f32[128,16,128]{2,1,0:T(8,128)} %bitcast.21), calls=%async_computation.1 | async-start | bytes 2097152 | tf_op jit(solution)/shard_map/all_to_all | solution.py:700
  72.3 19.1 %copy-start.1 = (f32[256,512]{1,0:T(8,128)S(1)}, f32[256,512]{1,0:T(8,128)}, u32[]{:S(2)}) copy-start(f32[256,512]{1,0:T(8,128)} %copy-done) | copy-start | bytes 1572868
  78.8 3.8 %collective-permute-start = (f32[16,256]{1,0:T(8,128)S(1)}, f32[16,256]{1,0:T(8,128)S(1)}, u32[]{:S(2)}, u32[]{:S(2)}) collective-permute-start(f32[16,256]{1,0:T(8,128)S(1)} %get-tuple-element.44), channel_id=1, source_target_pairs={{0,1},{1,0},{2,3},{3,2},{4,5},{5,4},{6,7},{7,6},{8,9},{9,8},{10,11... | collective-permute-start | bytes 49160 | tf_op jit(solution)/shard_map/ppermute | solution.py:553
  79.6 7.1 %collective-permute-start.1 = (f32[16,256]{1,0:T(8,128)S(1)}, f32[16,256]{1,0:T(8,128)S(1)}, u32[]{:S(2)}, u32[]{:S(2)}) collective-permute-start(f32[16,256]{1,0:T(8,128)S(1)} %get-tuple-element.45), channel_id=1, source_target_pairs={{0,15},{1,2},{2,1},{3,4},{4,3},{5,6},{6,5},{7,8},{8,7},{9,10},{10,... | collective-permute-start | bytes 49160 | tf_op jit(solution)/shard_map/ppermute | solution.py:553
  86.6 4.8 %collective-permute-start.3 = (f32[16,768]{1,0:T(8,128)S(1)}, f32[16,768]{1,0:T(8,128)S(1)}, u32[]{:S(2)}, u32[]{:S(2)}) collective-permute-start(f32[16,768]{1,0:T(8,128)S(1)} %pad_maximum_fusion.1), channel_id=1, source_target_pairs={{0,112},{16,32},{32,16},{48,64},{64,48},{80,96},{96,80},{112,0},{1... | collective-permute-start | bytes 147464 | tf_op jit(solution)/shard_map/ppermute | solution.py:553
  86.8 4.7 %collective-permute-start.2 = (f32[16,768]{1,0:T(8,128)S(1)}, f32[16,768]{1,0:T(8,128)S(1)}, u32[]{:S(2)}, u32[]{:S(2)}) collective-permute-start(f32[16,768]{1,0:T(8,128)S(1)} %pad_maximum_fusion), channel_id=1, source_target_pairs={{0,16},{16,0},{32,48},{48,32},{64,80},{80,64},{96,112},{112,96},{1... | collective-permute-start | bytes 147464 | tf_op jit(solution)/shard_map/ppermute | solution.py:553

commit v4 on v3

--- a/solution.py
+++ b/solution.py
@@ -350,41 +350,44 @@
         pieces = pieces + halves(got_ref[pl.ds(cap + k, peers, stride=stride), :])
         for at, piece in enumerate(pieces):
             data_ref[line, at * LANES : (at + 1) * LANES] = piece
-    mark(0)
-    alpha_ref, beta_ref, gamma_ref = [take(1 + k) for k in range(3)]
-    mark(group)
-    for first in range(0, owned, group):
-        line = slice(first, first + group)
-        moved = jnp.dot(hot_ref[line, :], data_ref[...], preferred_element_type=F32)
-        infil = moved[:, :LANES] + moved[:, LANES : 2 * LANES]
-        head = moved[:, 2 * LANES : 3 * LANES] + moved[:, 3 * LANES :]
-        share = jax.nn.sigmoid(head)
-        infil_ref[line, :] = infil
-        share_ref[line, :] = share
-        rech = alpha_ref[line, :] + beta_ref[line, :] * infil + gamma_ref[line, :] * share
-        high, low = halves(rech)
-        rech_ref[line, :LANES] = high
-        rech_ref[line, LANES:] = low
     size = peers // GROUPS
-    for turn in range(GROUPS):
-        first = turn * size
+
+    def mark_back(first):
         for k in range(cap):
             at = first * cap + k * size
             back_ref[at : at + size, :] = (
                 (labels[first : first + size, k : k + 1] == iota((size, owned), 1)).astype(F32).astype(BF16)
             )
+
+    mark(0)
+    for first in range(0, owned, group):
+        line = slice(first, first + group)
+        if first + group < owned:
+            mark(first + group)
+        moved = jnp.dot(hot_ref[line, :], data_ref[...], preferred_element_type=F32)
+        infil_ref[line, :] = moved[:, :LANES] + moved[:, LANES : 2 * LANES]
+        share_ref[line, :] = jax.nn.sigmoid(moved[:, 2 * LANES : 3 * LANES] + moved[:, 3 * LANES :])
+    alpha_ref, beta_ref, gamma_ref = [take(1 + k) for k in range(3)]
+    rech = alpha_ref[...] + beta_ref[...] * infil_ref[...] + gamma_ref[...] * share_ref[...]
+    high, low = halves(rech)
+    rech_ref[:, :LANES] = high
+    rech_ref[:, LANES:] = low
+    mark_back(0)
     for turn in range(GROUPS):
         first = turn * size
+        if turn + 1 < GROUPS:
+            mark_back(first + size)
         line = slice(first * cap, (first + size) * cap)
         moved = jnp.dot(back_ref[line, :], rech_ref[...], preferred_element_type=F32)
         for k in range(cap):
             part = moved[k * size : (k + 1) * size]
             ans_ref[pl.ds(first * cap + k, size, stride=cap), :] = part[:, :LANES] + part[:, LANES:]
         if turn == 1:
+            give(2, 0)
+            give(2, 1)
             give(0)
             give(1)
-            give(2, 0)
-        if turn > 0:
+        if turn > 1:
             give(2, turn)
 
 

time: 97 us -> 96 us (0.990)
  Pallas kernels: 47.7 us -> 46.7 us
    pallas_call x6, Pallas kernels: 21.5 us -> 20.5 us  [staged(): pl.pallas_call(kernel, out_shape=tuple((pltpu.VMEM(x.shape, x.dtype) if i...]
  transfers between devices with their start and end apart: 6 -> 6, of which waited for: 5 -> 5; matrix products, arithmetic and copies ran while one was open for 0% -> 0% of each run, Pallas kernels for 31% -> 32%
where the time goes in v4:
time: 96 us; the launch traced here: 95.2 us
  Pallas kernels  46.7 us (49%)
  waiting for transfers between devices  28.1 us (29%)
  starting transfers between devices  18.6 us (19%)
    pallas_call x6, Pallas kernels, staged(): pl.pallas_call(kernel, out_shape=tuple((pltpu.VMEM(x.shape, x.dtype) if i...  20.5 us
    all_to_all x1, waiting for transfers between devices, on_device(): lax.all_to_all(sent.reshape(peers, 1, wide), axes, split_axis=0, concat_a...  15.6 us
    pallas_call x1, Pallas kernels, saturate(): pl.pallas_call(kernel, grid=(owned // size,), out_shape=pltpu.HBM((owned...  14.7 us
    pallas_call x1, Pallas kernels, response(): pl.pallas_call(kernel, grid=(owned // size,), out_shape=(pltpu.HBM((owned...  11.5 us
    all_to_all x1, starting transfers between devices, on_device(): lax.all_to_all(sent.reshape(peers, 1, wide), axes, split_axis=0, concat_a...  11.1 us
    ppermute x4, waiting for transfers between devices, swap(): lax.ppermute(x, axis, pairs)  8.22 us
    all_to_all x1, starting transfers between devices, on_device(): lax.all_to_all(answer.reshape(peers, cap, LANES), axes, split_axis=0, con...  4.65 us
    all_to_all x1, waiting for transfers between devices, on_device(): lax.all_to_all(answer.reshape(peers, cap, LANES), axes, split_axis=0, con...  4.32 us
  transfers between devices with their start and end apart: 6, of which 5 were waited for; matrix products, arithmetic and copies ran while one was open for 0% of the time, Pallas kernels for 32%

profile of v4, /device:TPU:0, one launch (start us, length us, event | category | flops | bytes accessed | tf_op | source)
XLA Modules:
  0.0 95.2 jit_solution(15160153892800947246)
XLA Ops:
  0.6 4.7 %pack_forcing.1 = (f32[4224,128]{1,0:T(8,128)}, s32[1,1024]{1,0:T(1,128)S(1)}) custom-call(s32[4,256]{1,0:T(4,128)} %bitcast.22, f32[256,512]{1,0:T(8,128)} %refs_1_.4, f32[256,512]{1,0:T(8,128)} %refs_0_.1, s32[256,512]{1,0:T(8,128)} %refs_2_.3), custom_call_target="tpu_custom_call" | custom-call | bytes 15000000 | tf_op jit(solution)/shard_map/pack_forcing/pallas_call | solution.py:95
  5.3 11.1 %all-to-all-start = ((f32[128,1,4224]{2,1,0:T(1,128)}), f32[128,1,4224]{2,1,0:T(1,128)S(1)}, u32[]{:S(2)}, u32[]{:S(2)}) async-start(f32[128,1,4224]{2,1,0:T(1,128)} %bitcast.20), calls=%async_computation | async-start | bytes 4325376 | tf_op jit(solution)/shard_map/all_to_all | solution.py:693
  16.5 0.1 stack.27
  16.6 2.4 %derive_tile.1 = (f32[256,512]{1,0:T(8,128)S(1)}, f32[256,512]{1,0:T(8,128)S(1)}, f32[256,512]{1,0:T(8,128)S(1)}, f32[12,256]{1,0:T(8,128)S(1)}, f32[12,256]{1,0...) custom-call(f32[256,512]{1,0:T(8,128)} %refs_0_.1, f32[256,512]{1,0:T(8,128)} %refs_1_.6, ...), custom_call_target="tpu_custom_call" | custom-call | bytes 6000000 | tf_op jit(solution)/shard_map/derive_tile/pallas_call | solution.py:95
  19.0 0.0 copy-start
  19.0 0.8 copy-done
  19.8 11.5 %column_response.1 = (f32[1024,128]{1,0:T(8,128)}, f32[1024,128]{1,0:T(8,128)}, f32[1024,128]{1,0:T(8,128)}) custom-call(f32[16384,128]{1,0:T(8,128)} %bitcast.17, f32[1024,128]{1,0:T(8,128)} %refs_1_.7), custom_call_target="tpu_custom_call" | custom-call | bytes 39000000 | tf_op jit(solution)/shard_map/column_response/pallas_call | solution.py:276
  31.3 15.6 %all-to-all-done = f32[128,1,4224]{2,1,0:T(1,128)S(1)} async-done(((f32[128,1,4224]{2,1,0:T(1,128)}), f32[128,1,4224]{2,1,0:T(1,128)S(1)}, u32[]{:S(2)}, u32[]{:S(2)}) %all-to-all-start) | async-done | bytes 2162720 | tf_op jit(solution)/shard_map/all_to_all | solution.py:693
  46.8 5.1 %owner_side.1 = (f32[1024,128]{1,0:T(8,128)}, f32[1024,128]{1,0:T(8,128)}, f32[2048,128]{1,0:T(8,128)}) custom-call(f32[4224,128]{1,0:T(8,128)S(1)} %bitcast.14, f32[1024,128]{1,0:T(8,128)} %get-tuple-element.26.refs_1_, f32[1024,128]{1,0:T(8,128)} %get-tuple-element.27.refs_2_, f32[1024,128]{1,0:T(8,128)} %get-tuple-element.28.refs_3_, ...), custom_call_target="tpu_custom_call" | custom-call | bytes 24000000 | tf_op jit(solution)/shard_map/owner_side/pallas_call | solution.py:95
  52.0 4.6 %all-to-all-start.1 = ((f32[128,16,128]{2,1,0:T(8,128)}), f32[128,16,128]{2,1,0:T(8,128)S(1)}, u32[]{:S(2)}, u32[]{:S(2)}) async-start(f32[128,16,128]{2,1,0:T(8,128)} %bitcast.21), calls=%async_computation.1 | async-start | bytes 2097152 | tf_op jit(solution)/shard_map/all_to_all | solution.py:703
  56.6 14.7 %column_saturation.1.refs_5_ = f32[16384,128]{1,0:T(8,128)} custom-call(f32[16384,128]{1,0:T(8,128)} %bitcast.18, f32[1024,128]{1,0:T(8,128)} %refs_1_.7, f32[1024,128]{1,0:T(8,128)} %get-tuple-element.30.refs_2_, f32[1024,128]{1,0:T(8,128)} %get-tuple-element.31.refs_3_), custom_call_target="tpu_custom_call" | custom-call | bytes 42000000 | tf_op jit(solution)/shard_map/column_saturation/pallas_call | solution.py:319
  71.3 0.0 copy-start.1
  71.3 4.3 %all-to-all-done.1 = f32[128,16,128]{2,1,0:T(8,128)S(1)} async-done(((f32[128,16,128]{2,1,0:T(8,128)}), f32[128,16,128]{2,1,0:T(8,128)S(1)}, u32[]{:S(2)}, u32[]{:S(2)}) %all-to-all-start.1) | async-done | bytes 1048608 | tf_op jit(solution)/shard_map/all_to_all | solution.py:703
  75.7 2.1 %outer_flow.1 = (f32[256,128]{1,0:T(8,128)S(1)}, f32[256,128]{1,0:T(8,128)S(1)}, bf16[2048,256]{1,0:T(8,128)(2,1)S(1)}, f32[16,256]{1,0:T(8,128)S(1)}, f32[16,256]{1,0:T(8,128)S(1)}) custom-call(f32[2048,128]{1,0:T(8,128)S(1)} %bitcast.15, s32[1,1024]{1,0:T(1,128)S(1)} %get-tuple-element.36.refs_1_.refs_3_, f32[12,256]{1,0:T(8,128)S(1)} %get-tuple-element.29.refs_4_.refs_2_, ...), custom_call_target="tpu_custom_call" | custom-call | bytes 6000000 | tf_op jit(solution)/shard_map/outer_flow/pallas_call | solution.py:95
  77.8 0.8 collective-permute-start
  78.6 1.2 %collective-permute-start.1 = (f32[16,256]{1,0:T(8,128)S(1)}, f32[16,256]{1,0:T(8,128)S(1)}, u32[]{:S(2)}, u32[]{:S(2)}) collective-permute-start(f32[16,256]{1,0:T(8,128)S(1)} %get-tuple-element.45), channel_id=1, source_target_pairs={{0,15},{1,2},{2,1},{3,4},{4,3},{5,6},{6,5},{7,8},{8,7},{9,10},{10,... | collective-permute-start | bytes 49160 | tf_op jit(solution)/shard_map/ppermute | solution.py:556
  79.8 1.6 %inner_flow.1 = (f32[256,512]{1,0:T(8,128)S(1)}, f32[16,512]{1,0:T(8,128)S(1)}, f32[16,512]{1,0:T(8,128)S(1)}) custom-call(f32[256,128]{1,0:T(8,128)S(1)} %get-tuple-element.38.refs_0_, f32[256,128]{1,0:T(8,128)S(1)} %get-tuple-element.39.refs_1_, bf16[2048,256]{1,0:T(8,128)(2,1)S(1)} %get-tuple-element.40.refs_2_, ...), custom_call_target="tpu_custom_call" | custom-call | bytes 6000000 | tf_op jit(solution)/shard_map/inner_flow/pallas_call | solution.py:95
  81.4 0.2 collective-permute-done.refs_6_
  81.6 4.0 %collective-permute-done.1.refs_7_ = f32[16,256]{1,0:T(8,128)S(1)} collective-permute-done((f32[16,256]{1,0:T(8,128)S(1)}, f32[16,256]{1,0:T(8,128)S(1)}, u32[]{:S(2)}, u32[]{:S(2)}) %collective-permute-start.1) | collective-permute-done | bytes 16416 | tf_op jit(solution)/shard_map/ppermute | solution.py:556
  85.7 0.1 collective-permute-start.3
  85.8 0.7 collective-permute-start.2
  86.5 4.0 %collective-permute-done.3.refs_9_ = f32[16,768]{1,0:T(8,128)S(1)} collective-permute-done((f32[16,768]{1,0:T(8,128)S(1)}, f32[16,768]{1,0:T(8,128)S(1)}, u32[]{:S(2)}, u32[]{:S(2)}) %collective-permute-start.3) | collective-permute-done | bytes 49184 | tf_op jit(solution)/shard_map/ppermute | solution.py:556
  90.5 0.0 collective-permute-done.2.refs_8_
  90.5 0.0 copy-done.1
  90.5 4.6 %lateral_relax.1 = f32[256,512]{1,0:T(8,128)} custom-call(s32[1]{0:T(128)S(6)} %select_n.39.refs_0_, f32[6]{0:T(128)S(1)} %convert_element_type.3.refs_3_.refs_4_.refs_6_.refs_1_, f32[256,512]{1,0:T(8,128)S(1)} %get-tuple-element.32.refs_2_, f32[256,512]{1,0:T(8,128)S(1)} %copy-done.1, f32[256,512]{1,0:T(8,128)S(1)} %get-tuple-element.34.refs_4_, ...), custom_call_target="tpu_custom_call" | custom-call | bytes 18000000 | tf_op jit(solution)/shard_map/lateral_relax/pallas_call | solution.py:95
  (5 shorter events, 0.0 us)
Async XLA Ops:
  5.3 41.5 %all-to-all-start = ((f32[128,1,4224]{2,1,0:T(1,128)}), f32[128,1,4224]{2,1,0:T(1,128)S(1)}, u32[]{:S(2)}, u32[]{:S(2)}) async-start(f32[128,1,4224]{2,1,0:T(1,128)} %bitcast.20), calls=%async_computation | async-start | bytes 4325376 | tf_op jit(solution)/shard_map/all_to_all | solution.py:693
  19.0 0.8 copy-start
  52.0 23.7 %all-to-all-start.1 = ((f32[128,16,128]{2,1,0:T(8,128)}), f32[128,16,128]{2,1,0:T(8,128)S(1)}, u32[]{:S(2)}, u32[]{:S(2)}) async-start(f32[128,16,128]{2,1,0:T(8,128)} %bitcast.21), calls=%async_computation.1 | async-start | bytes 2097152 | tf_op jit(solution)/shard_map/all_to_all | solution.py:703
  71.3 19.1 %copy-start.1 = (f32[256,512]{1,0:T(8,128)S(1)}, f32[256,512]{1,0:T(8,128)}, u32[]{:S(2)}) copy-start(f32[256,512]{1,0:T(8,128)} %copy-done) | copy-start | bytes 1572868
  77.8 3.8 %collective-permute-start = (f32[16,256]{1,0:T(8,128)S(1)}, f32[16,256]{1,0:T(8,128)S(1)}, u32[]{:S(2)}, u32[]{:S(2)}) collective-permute-start(f32[16,256]{1,0:T(8,128)S(1)} %get-tuple-element.44), channel_id=1, source_target_pairs={{0,1},{1,0},{2,3},{3,2},{4,5},{5,4},{6,7},{7,6},{8,9},{9,8},{10,11... | collective-permute-start | bytes 49160 | tf_op jit(solution)/shard_map/ppermute | solution.py:556
  78.6 7.1 %collective-permute-start.1 = (f32[16,256]{1,0:T(8,128)S(1)}, f32[16,256]{1,0:T(8,128)S(1)}, u32[]{:S(2)}, u32[]{:S(2)}) collective-permute-start(f32[16,256]{1,0:T(8,128)S(1)} %get-tuple-element.45), channel_id=1, source_target_pairs={{0,15},{1,2},{2,1},{3,4},{4,3},{5,6},{6,5},{7,8},{8,7},{9,10},{10,... | collective-permute-start | bytes 49160 | tf_op jit(solution)/shard_map/ppermute | solution.py:556
  85.7 4.8 %collective-permute-start.3 = (f32[16,768]{1,0:T(8,128)S(1)}, f32[16,768]{1,0:T(8,128)S(1)}, u32[]{:S(2)}, u32[]{:S(2)}) collective-permute-start(f32[16,768]{1,0:T(8,128)S(1)} %pad_maximum_fusion.1), channel_id=1, source_target_pairs={{0,112},{16,32},{32,16},{48,64},{64,48},{80,96},{96,80},{112,0},{1... | collective-permute-start | bytes 147464 | tf_op jit(solution)/shard_map/ppermute | solution.py:556
  85.8 4.7 %collective-permute-start.2 = (f32[16,768]{1,0:T(8,128)S(1)}, f32[16,768]{1,0:T(8,128)S(1)}, u32[]{:S(2)}, u32[]{:S(2)}) collective-permute-start(f32[16,768]{1,0:T(8,128)S(1)} %pad_maximum_fusion), channel_id=1, source_target_pairs={{0,16},{16,0},{32,48},{48,32},{64,80},{80,64},{96,112},{112,96},{1... | collective-permute-start | bytes 147464 | tf_op jit(solution)/shard_map/ppermute | solution.py:556

commit v5 on v4

--- a/solution.py
+++ b/solution.py
@@ -12,7 +12,7 @@
 EDGE = 8
 WIDE = 4
 PAD = 8
-GROUPS = 4
+GROUPS = 8
 
 layer_depth = 0.1
 step_ratio = 0.1
@@ -617,44 +617,50 @@
         for b in range(count):
             ref[b, first_row:last_row, :] = tile[:, b * LANES : (b + 1) * LANES].astype(F32)
 
-    edge = iota((height, LANES), 1)
-
-    def around(ref):
-        mid = [ref[b, top : top + height, :] for b in range(count + 1)]
+    step = 16
+    edge = iota((step, LANES), 1)
+
+    def around(ref, row):
+        mid = [ref[b, top + row : top + row + step, :] for b in range(count + 1)]
         later = [pltpu.roll(x, 1, 1) for x in mid]
         sooner = [pltpu.roll(x, LANES - 1, 1) for x in mid]
         for b in range(count + 1):
             yield (
                 mid[b],
-                ref[b, pl.ds(top - one, height), :],
-                ref[b, pl.ds(top + one, height), :],
+                ref[b, pl.ds(top + row - one, step), :],
+                ref[b, pl.ds(top + row + one, step), :],
                 jnp.where(edge == 0, later[b - 1], later[b]),
                 jnp.where(edge == LANES - 1, sooner[(b + 1) % (count + 1)], sooner[b]),
             )
 
-    up_ref, down_ref, left_ref, right_ref = weight_refs
-    line = slice(top, top + height)
-    for b, (mid, *others) in enumerate(around(trans_ref)):
-        sums = [mid + x for x in others]
-        total = 0.5 * (sums[0] + sums[1] + sums[2] + sums[3])
-        scale = share_ref[b, line, :] / (store_rate + total)
-        half = 0.5 * scale
-        for ref, x in zip(weight_refs, sums):
-            ref[b] = half * x
-        flow_ref[b, line, :] = scale * (store_rate * initial_ref[b, line, :] + flow_ref[b, line, :])
+    for row in range(0, height, step):
+        line = slice(top + row, top + row + step)
+        for b, (mid, *others) in enumerate(around(trans_ref, row)):
+            sums = [mid + x for x in others]
+            total = 0.5 * (sums[0] + sums[1] + sums[2] + sums[3])
+            scale = share_ref[b, line, :] / (store_rate + total)
+            half = 0.5 * scale
+            for ref, x in zip(weight_refs, sums):
+                ref[b, row : row + step, :] = half * x
+            flow_ref[b, line, :] = scale * (store_rate * initial_ref[b, line, :] + flow_ref[b, line, :])
     now, later_ref = initial_ref, next_ref
+    piece = rows // 4
     for sweep in range(SWEEPS):
-        for b, (_, above, below, on_left, on_right) in enumerate(around(now)):
-            if sweep == SWEEPS - 1 and b == count:
-                continue
-            inflow = up_ref[b] * above + down_ref[b] * below
-            inflow = inflow + left_ref[b] * on_left + right_ref[b] * on_right
-            surface = flow_ref[b, line, :] + inflow
-            if sweep == SWEEPS - 1:
-                out_ref[:, b * LANES : (b + 1) * LANES] = surface[EDGE : EDGE + rows, :]
-                give(0, b)
-            else:
-                later_ref[b, line, :] = surface
+        final = sweep == SWEEPS - 1
+        for row in range(EDGE, EDGE + rows, step) if final else range(0, height, step):
+            part = slice(row, row + step)
+            line = slice(top + row, top + row + step)
+            for b, (_, *others) in enumerate(around(now, row)):
+                if final and b == count:
+                    continue
+                up, down, left, right = [ref[b, part, :] * x for ref, x in zip(weight_refs, others)]
+                surface = flow_ref[b, line, :] + ((up + down) + (left + right))
+                if final:
+                    out_ref[row - EDGE : row - EDGE + step, b * LANES : (b + 1) * LANES] = surface
+                else:
+                    later_ref[b, line, :] = surface
+            if final and (row - EDGE + step) % piece == 0:
+                give(0, (row - EDGE + step) // piece - 1)
         now, later_ref = later_ref, now
 
 
@@ -673,8 +679,7 @@
         6,
         held=range(2, 10),
         in_smem=(0, 1),
-        pieces=(cols // LANES,),
-        by_lanes=True,
+        pieces=(4,),
     )[0]
 
 

time: 96 us -> 95.4 us (level)
  no operation moved by 1% of the time
where the time goes in v5:
time: 95.4 us; the launch traced here: 94.6 us
  Pallas kernels  46.1 us (48%)
  waiting for transfers between devices  28.1 us (29%)
  starting transfers between devices  18.6 us (19%)
    pallas_call x6, Pallas kernels, staged(): pl.pallas_call(kernel, out_shape=tuple((pltpu.VMEM(x.shape, x.dtype) if i...  19.9 us
    all_to_all x1, waiting for transfers between devices, on_device(): lax.all_to_all(sent.reshape(peers, 1, wide), axes, split_axis=0, concat_a...  15.6 us
    pallas_call x1, Pallas kernels, saturate(): pl.pallas_call(kernel, grid=(owned // size,), out_shape=pltpu.HBM((owned...  14.7 us
    pallas_call x1, Pallas kernels, response(): pl.pallas_call(kernel, grid=(owned // size,), out_shape=(pltpu.HBM((owned...  11.5 us
    all_to_all x1, starting transfers between devices, on_device(): lax.all_to_all(sent.reshape(peers, 1, wide), axes, split_axis=0, concat_a...  11.1 us
    ppermute x4, waiting for transfers between devices, swap(): lax.ppermute(x, axis, pairs)  8.22 us
    all_to_all x1, starting transfers between devices, on_device(): lax.all_to_all(answer.reshape(peers, cap, LANES), axes, split_axis=0, con...  4.65 us
    all_to_all x1, waiting for transfers between devices, on_device(): lax.all_to_all(answer.reshape(peers, cap, LANES), axes, split_axis=0, con...  4.32 us
  transfers between devices with their start and end apart: 6, of which 5 were waited for; matrix products, arithmetic and copies ran while one was open for 0% of the time, Pallas kernels for 32%

profile of v5, /device:TPU:0, one launch (start us, length us, event | category | flops | bytes accessed | tf_op | source)
XLA Modules:
  0.0 94.6 jit_solution(17164189998470451450)
XLA Ops:
  0.6 4.6 %pack_forcing.1 = (f32[4224,128]{1,0:T(8,128)}, s32[1,1024]{1,0:T(1,128)S(1)}) custom-call(s32[4,256]{1,0:T(4,128)} %bitcast.22, f32[256,512]{1,0:T(8,128)} %refs_1_.4, f32[256,512]{1,0:T(8,128)} %refs_0_.1, s32[256,512]{1,0:T(8,128)} %refs_2_.3), custom_call_target="tpu_custom_call" | custom-call | bytes 15000000 | tf_op jit(solution)/shard_map/pack_forcing/pallas_call | solution.py:95
  5.2 11.1 %all-to-all-start = ((f32[128,1,4224]{2,1,0:T(1,128)}), f32[128,1,4224]{2,1,0:T(1,128)S(1)}, u32[]{:S(2)}, u32[]{:S(2)}) async-start(f32[128,1,4224]{2,1,0:T(1,128)} %bitcast.20), calls=%async_computation | async-start | bytes 4325376 | tf_op jit(solution)/shard_map/all_to_all | solution.py:698
  16.4 0.1 stack.27
  16.5 2.4 %derive_tile.1 = (f32[256,512]{1,0:T(8,128)S(1)}, f32[256,512]{1,0:T(8,128)S(1)}, f32[256,512]{1,0:T(8,128)S(1)}, f32[12,256]{1,0:T(8,128)S(1)}, f32[12,256]{1,0...) custom-call(f32[256,512]{1,0:T(8,128)} %refs_0_.1, f32[256,512]{1,0:T(8,128)} %refs_1_.6, ...), custom_call_target="tpu_custom_call" | custom-call | bytes 6000000 | tf_op jit(solution)/shard_map/derive_tile/pallas_call | solution.py:95
  18.9 0.0 copy-start
  18.9 0.8 copy-done
  19.7 11.5 %column_response.1 = (f32[1024,128]{1,0:T(8,128)}, f32[1024,128]{1,0:T(8,128)}, f32[1024,128]{1,0:T(8,128)}) custom-call(f32[16384,128]{1,0:T(8,128)} %bitcast.17, f32[1024,128]{1,0:T(8,128)} %refs_1_.7), custom_call_target="tpu_custom_call" | custom-call | bytes 39000000 | tf_op jit(solution)/shard_map/column_response/pallas_call | solution.py:276
  31.2 15.6 %all-to-all-done = f32[128,1,4224]{2,1,0:T(1,128)S(1)} async-done(((f32[128,1,4224]{2,1,0:T(1,128)}), f32[128,1,4224]{2,1,0:T(1,128)S(1)}, u32[]{:S(2)}, u32[]{:S(2)}) %all-to-all-start) | async-done | bytes 2162720 | tf_op jit(solution)/shard_map/all_to_all | solution.py:698
  46.8 5.0 %owner_side.1 = (f32[1024,128]{1,0:T(8,128)}, f32[1024,128]{1,0:T(8,128)}, f32[2048,128]{1,0:T(8,128)}) custom-call(f32[4224,128]{1,0:T(8,128)S(1)} %bitcast.14, f32[1024,128]{1,0:T(8,128)} %get-tuple-element.26.refs_1_, f32[1024,128]{1,0:T(8,128)} %get-tuple-element.27.refs_2_, f32[1024,128]{1,0:T(8,128)} %get-tuple-element.28.refs_3_, ...), custom_call_target="tpu_custom_call" | custom-call | bytes 24000000 | tf_op jit(solution)/shard_map/owner_side/pallas_call | solution.py:95
  51.8 4.6 %all-to-all-start.1 = ((f32[128,16,128]{2,1,0:T(8,128)}), f32[128,16,128]{2,1,0:T(8,128)S(1)}, u32[]{:S(2)}, u32[]{:S(2)}) async-start(f32[128,16,128]{2,1,0:T(8,128)} %bitcast.21), calls=%async_computation.1 | async-start | bytes 2097152 | tf_op jit(solution)/shard_map/all_to_all | solution.py:708
  56.4 14.7 %column_saturation.1.refs_5_ = f32[16384,128]{1,0:T(8,128)} custom-call(f32[16384,128]{1,0:T(8,128)} %bitcast.18, f32[1024,128]{1,0:T(8,128)} %refs_1_.7, f32[1024,128]{1,0:T(8,128)} %get-tuple-element.30.refs_2_, f32[1024,128]{1,0:T(8,128)} %get-tuple-element.31.refs_3_), custom_call_target="tpu_custom_call" | custom-call | bytes 42000000 | tf_op jit(solution)/shard_map/column_saturation/pallas_call | solution.py:319
  71.2 0.0 copy-start.1
  71.2 4.3 %all-to-all-done.1 = f32[128,16,128]{2,1,0:T(8,128)S(1)} async-done(((f32[128,16,128]{2,1,0:T(8,128)}), f32[128,16,128]{2,1,0:T(8,128)S(1)}, u32[]{:S(2)}, u32[]{:S(2)}) %all-to-all-start.1) | async-done | bytes 1048608 | tf_op jit(solution)/shard_map/all_to_all | solution.py:708
  75.5 2.1 %outer_flow.1 = (f32[256,128]{1,0:T(8,128)S(1)}, f32[256,128]{1,0:T(8,128)S(1)}, bf16[2048,256]{1,0:T(8,128)(2,1)S(1)}, f32[16,256]{1,0:T(8,128)S(1)}, f32[16,256]{1,0:T(8,128)S(1)}) custom-call(f32[2048,128]{1,0:T(8,128)S(1)} %bitcast.15, s32[1,1024]{1,0:T(1,128)S(1)} %get-tuple-element.36.refs_1_.refs_3_, f32[12,256]{1,0:T(8,128)S(1)} %get-tuple-element.29.refs_4_.refs_2_, ...), custom_call_target="tpu_custom_call" | custom-call | bytes 6000000 | tf_op jit(solution)/shard_map/outer_flow/pallas_call | solution.py:95
  77.6 0.8 collective-permute-start
  78.4 1.2 %collective-permute-start.1 = (f32[16,256]{1,0:T(8,128)S(1)}, f32[16,256]{1,0:T(8,128)S(1)}, u32[]{:S(2)}, u32[]{:S(2)}) collective-permute-start(f32[16,256]{1,0:T(8,128)S(1)} %get-tuple-element.45), channel_id=1, source_target_pairs={{0,15},{1,2},{2,1},{3,4},{4,3},{5,6},{6,5},{7,8},{8,7},{9,10},{10,... | collective-permute-start | bytes 49160 | tf_op jit(solution)/shard_map/ppermute | solution.py:556
  79.6 1.6 %inner_flow.1 = (f32[256,512]{1,0:T(8,128)S(1)}, f32[16,512]{1,0:T(8,128)S(1)}, f32[16,512]{1,0:T(8,128)S(1)}) custom-call(f32[256,128]{1,0:T(8,128)S(1)} %get-tuple-element.38.refs_0_, f32[256,128]{1,0:T(8,128)S(1)} %get-tuple-element.39.refs_1_, bf16[2048,256]{1,0:T(8,128)(2,1)S(1)} %get-tuple-element.40.refs_2_, ...), custom_call_target="tpu_custom_call" | custom-call | bytes 6000000 | tf_op jit(solution)/shard_map/inner_flow/pallas_call | solution.py:95
  81.2 0.2 collective-permute-done.refs_6_
  81.4 4.0 %collective-permute-done.1.refs_7_ = f32[16,256]{1,0:T(8,128)S(1)} collective-permute-done((f32[16,256]{1,0:T(8,128)S(1)}, f32[16,256]{1,0:T(8,128)S(1)}, u32[]{:S(2)}, u32[]{:S(2)}) %collective-permute-start.1) | collective-permute-done | bytes 16416 | tf_op jit(solution)/shard_map/ppermute | solution.py:556
  85.5 0.1 collective-permute-start.3
  85.6 0.7 collective-permute-start.2
  86.3 4.0 %collective-permute-done.3.refs_9_ = f32[16,768]{1,0:T(8,128)S(1)} collective-permute-done((f32[16,768]{1,0:T(8,128)S(1)}, f32[16,768]{1,0:T(8,128)S(1)}, u32[]{:S(2)}, u32[]{:S(2)}) %collective-permute-start.3) | collective-permute-done | bytes 49184 | tf_op jit(solution)/shard_map/ppermute | solution.py:556
  90.3 0.0 collective-permute-done.2.refs_8_
  90.3 0.0 copy-done.1
  90.3 4.2 %lateral_relax.1 = f32[256,512]{1,0:T(8,128)} custom-call(s32[1]{0:T(128)S(6)} %select_n.39.refs_0_, f32[6]{0:T(128)S(1)} %convert_element_type.3.refs_3_.refs_4_.refs_6_.refs_1_, f32[256,512]{1,0:T(8,128)S(1)} %get-tuple-element.32.refs_2_, f32[256,512]{1,0:T(8,128)S(1)} %copy-done.1, f32[256,512]{1,0:T(8,128)S(1)} %get-tuple-element.34.refs_4_, ...), custom_call_target="tpu_custom_call" | custom-call | bytes 18000000 | tf_op jit(solution)/shard_map/lateral_relax/pallas_call | solution.py:95
  (5 shorter events, 0.0 us)
Async XLA Ops:
  5.2 41.5 %all-to-all-start = ((f32[128,1,4224]{2,1,0:T(1,128)}), f32[128,1,4224]{2,1,0:T(1,128)S(1)}, u32[]{:S(2)}, u32[]{:S(2)}) async-start(f32[128,1,4224]{2,1,0:T(1,128)} %bitcast.20), calls=%async_computation | async-start | bytes 4325376 | tf_op jit(solution)/shard_map/all_to_all | solution.py:698
  18.9 0.8 copy-start
  51.8 23.7 %all-to-all-start.1 = ((f32[128,16,128]{2,1,0:T(8,128)}), f32[128,16,128]{2,1,0:T(8,128)S(1)}, u32[]{:S(2)}, u32[]{:S(2)}) async-start(f32[128,16,128]{2,1,0:T(8,128)} %bitcast.21), calls=%async_computation.1 | async-start | bytes 2097152 | tf_op jit(solution)/shard_map/all_to_all | solution.py:708
  71.2 19.1 %copy-start.1 = (f32[256,512]{1,0:T(8,128)S(1)}, f32[256,512]{1,0:T(8,128)}, u32[]{:S(2)}) copy-start(f32[256,512]{1,0:T(8,128)} %copy-done) | copy-start | bytes 1572868
  77.6 3.8 %collective-permute-start = (f32[16,256]{1,0:T(8,128)S(1)}, f32[16,256]{1,0:T(8,128)S(1)}, u32[]{:S(2)}, u32[]{:S(2)}) collective-permute-start(f32[16,256]{1,0:T(8,128)S(1)} %get-tuple-element.44), channel_id=1, source_target_pairs={{0,1},{1,0},{2,3},{3,2},{4,5},{5,4},{6,7},{7,6},{8,9},{9,8},{10,11... | collective-permute-start | bytes 49160 | tf_op jit(solution)/shard_map/ppermute | solution.py:556
  78.4 7.1 %collective-permute-start.1 = (f32[16,256]{1,0:T(8,128)S(1)}, f32[16,256]{1,0:T(8,128)S(1)}, u32[]{:S(2)}, u32[]{:S(2)}) collective-permute-start(f32[16,256]{1,0:T(8,128)S(1)} %get-tuple-element.45), channel_id=1, source_target_pairs={{0,15},{1,2},{2,1},{3,4},{4,3},{5,6},{6,5},{7,8},{8,7},{9,10},{10,... | collective-permute-start | bytes 49160 | tf_op jit(solution)/shard_map/ppermute | solution.py:556
  85.5 4.8 %collective-permute-start.3 = (f32[16,768]{1,0:T(8,128)S(1)}, f32[16,768]{1,0:T(8,128)S(1)}, u32[]{:S(2)}, u32[]{:S(2)}) collective-permute-start(f32[16,768]{1,0:T(8,128)S(1)} %pad_maximum_fusion.1), channel_id=1, source_target_pairs={{0,112},{16,32},{32,16},{48,64},{64,48},{80,96},{96,80},{112,0},{1... | collective-permute-start | bytes 147464 | tf_op jit(solution)/shard_map/ppermute | solution.py:556
  85.6 4.7 %collective-permute-start.2 = (f32[16,768]{1,0:T(8,128)S(1)}, f32[16,768]{1,0:T(8,128)S(1)}, u32[]{:S(2)}, u32[]{:S(2)}) collective-permute-start(f32[16,768]{1,0:T(8,128)S(1)} %pad_maximum_fusion), channel_id=1, source_target_pairs={{0,16},{16,0},{32,48},{48,32},{64,80},{80,64},{96,112},{112,96},{1... | collective-permute-start | bytes 147464 | tf_op jit(solution)/shard_map/ppermute | solution.py:556
